TPU v7x, 512 devices: a whole 4x4x16 slice. The times are simulated.
512 devices in a mesh: chan: 32 (over z_lo, y, core), tm: 16 (over x, z_hi).
Axes of the slice: x: 4, y: 4, z: 16 (z_hi: 4, z_lo: 4; z = z_hi * 4 + z_lo), core: 2. Of those that a mesh axis runs over, the one named last changes fastest.
Arguments:
- samples: bfloat16 [32, 2, 1024, 4096], P('chan', None, None, 'tm')
- feed_flags: int32 [32, 1024], P('chan'), may hold values 0 or 1
- cal_channel: int32 [16], replicated, may hold values from 0 to 31, as said below
- gain_state: float32 [32, 2, 2, 1024], P('chan', None, None, 'tm'), may hold values from -6 to 6
Outputs:
- calibrated: bfloat16 [32, 1024, 2, 1024], P('chan', 'tm')
- new_gains: float32 [32, 2, 2, 1024], P('chan', None, None, 'tm')
Inputs may be any that keep to these rules, and one draw needn't show every extreme that they name: `cal_channel`: entry p is 2 p or 2 p + 1; entry 0 is 1.
All inputs are finite; a program needn't handle non-finite values. No bound on the sum of `feed_flags` on one device may be relied on, other than what follows from the above.
Results may differ from a plain program's by a relative error of at most 0.017.
Values may be sent and summed in bfloat16 or wider, within the bound.
No kernel may reach another device: no remote copies, remote signals or barrier semaphores. Data moves between devices by JAX's collectives and lax.ppermute only.
A program may use at most 64 MiB of HBM per device.

v0:
```python
import jax
import jax.numpy as jnp
from jax import lax
from jax.sharding import PartitionSpec as P

ITERS = 8


epsilon = 1e-06
smoothing = 0.75


def partner_2(value, axis, bit):
    return lax.ppermute(value, axis, [(i, i ^ 1 << bit) for i in range(lax.axis_size(axis))])


def gram_rows(pieces, many_rows, all_time):
    real_part = pieces[0]
    imag_part = pieces[1]
    feeds = real_part.shape[0]
    width = real_part.shape[1]
    paired = jnp.stack(
        [jnp.concatenate([real_part, imag_part], 1), jnp.concatenate([imag_part, -real_part], 1)], 1
    )
    paired = paired.reshape(2 * many_rows, 2 * width)
    right_side = jnp.concatenate([real_part, imag_part], 1)
    product = lax.dot_general(
        paired, right_side, (((1,), (1,)), ((), ())), preferred_element_type=jnp.float32
    )
    return product.reshape(many_rows, 2, feeds) / all_time


def start_basis(feeds):
    positions = jnp.arange(feeds).astype(jnp.float32)
    modes = jnp.arange(1, 3).astype(jnp.float32)
    angles = 2.0 * jnp.pi * modes[:, None] * positions[None, :] / feeds
    factor = 1.0 / jnp.sqrt(jnp.ones((), jnp.float32) * feeds)
    return jnp.stack([jnp.cos(angles), jnp.sin(angles)]) * factor


def highest(left_side, right_side):
    return jnp.dot(
        left_side, right_side, precision=lax.Precision.HIGHEST, preferred_element_type=jnp.float32
    )


def subspace_gains(cal_block):
    real_block = cal_block[:, 0, :]
    imag_block = cal_block[:, 1, :]
    feeds = cal_block.shape[2]
    basis = start_basis(feeds)
    for sweep in range(ITERS):
        zeta_real = highest(real_block, basis[0].T) - highest(imag_block, basis[1].T)
        zeta_imag = highest(real_block, basis[1].T) + highest(imag_block, basis[0].T)
        one_real, two_real = (zeta_real[:, 0], zeta_real[:, 1])
        one_imag, two_imag = (zeta_imag[:, 0], zeta_imag[:, 1])
        local_one = jnp.sum(one_real * one_real + one_imag * one_imag)
        local_real = jnp.sum(one_real * two_real + one_imag * two_imag)
        local_imag = jnp.sum(one_real * two_imag - one_imag * two_real)
        norm_one, sum_real, sum_imag = lax.psum((local_one, local_real, local_imag), "tm")
        first_norm = jnp.sqrt(epsilon + norm_one)
        cross_real = sum_real / first_norm
        cross_imag = sum_imag / first_norm
        rest_real = two_real - (one_real * cross_real - one_imag * cross_imag) / first_norm
        rest_imag = two_imag - (one_real * cross_imag + one_imag * cross_real) / first_norm
        rest_sum = lax.psum(jnp.sum(rest_real * rest_real + rest_imag * rest_imag), "tm")
        second_norm = jnp.sqrt(epsilon + rest_sum)
        local_basis = jnp.stack(
            [
                jnp.stack([one_real / first_norm, rest_real / second_norm]),
                jnp.stack([one_imag / first_norm, rest_imag / second_norm]),
            ]
        )
        if sweep + 1 < ITERS:
            basis = lax.all_gather(local_basis, "tm", axis=2, tiled=True)
    weights = jnp.sqrt(jnp.stack([first_norm, second_norm]) * feeds)
    return local_basis * weights[None, :, None]


def on_device(samples, feed_flags, cal_channel, gain_state):
    feeds = samples.shape[2]
    tm_count = lax.axis_size("tm")
    row_count = feeds // tm_count
    row_first = lax.axis_index("tm") * row_count
    local_time = samples.shape[3]
    all_time = local_time * tm_count
    masked = samples[0] * feed_flags[0][None, :, None].astype(jnp.bfloat16)
    visibility = lax.psum_scatter(
        gram_rows(masked, row_count * lax.axis_size("tm"), all_time).astype(jnp.bfloat16),
        "tm",
        scatter_dimension=0,
        tiled=True,
    ).astype(jnp.float32)
    chan_index = lax.axis_index("chan")
    own_channel = cal_channel[chan_index // 2] == chan_index
    partner = partner_2(visibility.astype(jnp.bfloat16), "chan", 0).astype(visibility.dtype)
    solved = subspace_gains(jnp.where(own_channel, visibility, partner))
    gains_now = smoothing * gain_state[0] + (1.0 - smoothing) * solved
    power = jnp.sum(gains_now * gains_now, axis=(0, 1))
    all_power = lax.all_gather(power, "tm", axis=0, tiled=True)
    mean_power = jnp.mean(all_power)
    scale_all = jnp.sqrt((mean_power + epsilon) / (all_power + mean_power + epsilon))
    scale_rows = lax.dynamic_slice_in_dim(scale_all, row_first, row_count, 0)
    calibrated = (visibility * scale_rows[:, None, None] * scale_all[None, None, :]).astype(
        jnp.bfloat16
    )
    return (calibrated[None], gains_now[None])


def solution(mesh):
    return jax.shard_map(
        on_device,
        mesh=mesh,
        in_specs=(P("chan", None, None, "tm"), P("chan", None), P(), P("chan", None, None, "tm")),
        out_specs=(P("chan", "tm", None, None), P("chan", None, None, "tm")),
        check_vma=False,
    )
```

profile of v0, /device:TPU:88, one launch (start us, length us, event | category | flops | bytes accessed | tf_op | source)
XLA Modules:
  0.0 1542.6 jit_solution(4308000299347750320)
XLA Ops:
  7.9 1.4 bitcast_multiply_fusion
  9.6 4.3 multiply_convert_fusion
  15.9 155.7 %reduce-scatter.2.cloned.1.call-done = bf16[64,2,1024]{2,0,1:T(8,128)(2,1)} async-done(((bf16[1024,2,1024]{2,0,1:T(8,128)(2,1)}), bf16[64,2,1024]{2,0,1:T(8,128)(2,1)}) %reduce-scatter.2.cloned.1.call-update) | async-done | bytes 262160 | tf_op jit(solution)/shard_map/reduce_scatter | solution.py:88
  171.6 1.9 collective-permute-start
  173.7 1.5 collective-permute-done
  175.2 1.0 convert_select_fusion
  178.2 52.7 %all-reduce.8 = (f32[]{:T(128)}, f32[]{:T(128)}, f32[]{:T(128)}) all-reduce(f32[]{:T(128)} %get-tuple-element.29, f32[]{:T(128)} %get-tuple-element.28, f32[]{:T(128)} %get-tuple-element.27), channel_id=1, replica_groups=mesh['chan'=32,'tm'=16] {'tm'}, use_global_device_ids=true, to_apply=%region_2.3 | all-reduce | flops 3 | bytes 24 | tf_op jit(solution)/shard_map/psum | solution.py:60
  233.5 47.0 %psum.227 = f32[]{:T(128)} all-reduce(f32[]{:T(128)} %fusion.128), channel_id=1, replica_groups=mesh['chan'=32,'tm'=16] {'tm'}, use_global_device_ids=true, to_apply=%region_8.9 | all-reduce | flops 1 | bytes 8 | tf_op jit(solution)/shard_map/psum | solution.py:66
  281.3 73.3 %all_gather.24 = f32[2,2,1024]{1,0,2:T(2,128)S(1)} all-gather(f32[2,2,64]{1,0,2:T(2,128)S(1)} %copy.7), channel_id=1, replica_groups=mesh['chan'=32,'tm'=16] {'tm'}, dimensions={2}, use_global_device_ids=true | all-gather | bytes 17408 | tf_op jit(solution)/shard_map/all_gather | solution.py:75
  354.6 0.8 fusion.141
  355.4 1.0 fusion.20
  356.4 1.0 fusion.21
  357.3 0.9 convolution_add_fusion.7
  358.2 1.0 convolution_subtract_fusion.7
  360.0 46.9 %all-reduce.7 = (f32[]{:T(128)}, f32[]{:T(128)}, f32[]{:T(128)}) all-reduce(f32[]{:T(128)} %get-tuple-element.26, f32[]{:T(128)} %get-tuple-element.25, f32[]{:T(128)} %get-tuple-element.24), channel_id=1, replica_groups=mesh['chan'=32,'tm'=16] {'tm'}, use_global_device_ids=true, to_apply=%region_10.11 | all-reduce | flops 3 | bytes 24 | tf_op jit(solution)/shard_map/psum | solution.py:60
  409.4 53.5 %psum.231 = f32[]{:T(128)} all-reduce(f32[]{:T(128)} %fusion.127), channel_id=1, replica_groups=mesh['chan'=32,'tm'=16] {'tm'}, use_global_device_ids=true, to_apply=%region_16.17 | all-reduce | flops 1 | bytes 8 | tf_op jit(solution)/shard_map/psum | solution.py:66
  463.7 57.6 %all_gather.25 = f32[2,2,1024]{1,0,2:T(2,128)S(1)} all-gather(f32[2,2,64]{1,0,2:T(2,128)S(1)} %copy.8), channel_id=1, replica_groups=mesh['chan'=32,'tm'=16] {'tm'}, dimensions={2}, use_global_device_ids=true | all-gather | bytes 17408 | tf_op jit(solution)/shard_map/all_gather | solution.py:75
  521.4 0.8 fusion.140
  522.2 1.0 fusion.18
  523.2 1.0 fusion.19
  524.1 0.9 convolution_add_fusion.6
  525.0 1.0 convolution_subtract_fusion.6
  526.8 53.1 %all-reduce.6 = (f32[]{:T(128)}, f32[]{:T(128)}, f32[]{:T(128)}) all-reduce(f32[]{:T(128)} %get-tuple-element.23, f32[]{:T(128)} %get-tuple-element.22, f32[]{:T(128)} %get-tuple-element.21), channel_id=1, replica_groups=mesh['chan'=32,'tm'=16] {'tm'}, use_global_device_ids=true, to_apply=%region_18.19 | all-reduce | flops 3 | bytes 24 | tf_op jit(solution)/shard_map/psum | solution.py:60
  582.5 48.2 %psum.235 = f32[]{:T(128)} all-reduce(f32[]{:T(128)} %fusion.126), channel_id=1, replica_groups=mesh['chan'=32,'tm'=16] {'tm'}, use_global_device_ids=true, to_apply=%region_24.25 | all-reduce | flops 1 | bytes 8 | tf_op jit(solution)/shard_map/psum | solution.py:66
  631.5 61.0 %all_gather.26 = f32[2,2,1024]{1,0,2:T(2,128)S(1)} all-gather(f32[2,2,64]{1,0,2:T(2,128)S(1)} %copy.9), channel_id=1, replica_groups=mesh['chan'=32,'tm'=16] {'tm'}, dimensions={2}, use_global_device_ids=true | all-gather | bytes 17408 | tf_op jit(solution)/shard_map/all_gather | solution.py:75
  692.5 0.8 fusion.139
  693.3 1.0 fusion.16
  694.3 1.0 fusion.17
  695.3 0.9 convolution_add_fusion.5
  696.2 1.0 convolution_subtract_fusion.5
  697.9 47.6 %all-reduce.5 = (f32[]{:T(128)}, f32[]{:T(128)}, f32[]{:T(128)}) all-reduce(f32[]{:T(128)} %get-tuple-element.20, f32[]{:T(128)} %get-tuple-element.19, f32[]{:T(128)} %get-tuple-element.18), channel_id=1, replica_groups=mesh['chan'=32,'tm'=16] {'tm'}, use_global_device_ids=true, to_apply=%region_26.27 | all-reduce | flops 3 | bytes 24 | tf_op jit(solution)/shard_map/psum | solution.py:60
  748.0 52.9 %psum.239 = f32[]{:T(128)} all-reduce(f32[]{:T(128)} %fusion.125), channel_id=1, replica_groups=mesh['chan'=32,'tm'=16] {'tm'}, use_global_device_ids=true, to_apply=%region_32.33 | all-reduce | flops 1 | bytes 8 | tf_op jit(solution)/shard_map/psum | solution.py:66
  801.8 54.6 %all_gather.27 = f32[2,2,1024]{1,0,2:T(2,128)S(1)} all-gather(f32[2,2,64]{1,0,2:T(2,128)S(1)} %copy.10), channel_id=1, replica_groups=mesh['chan'=32,'tm'=16] {'tm'}, dimensions={2}, use_global_device_ids=true | all-gather | bytes 17408 | tf_op jit(solution)/shard_map/all_gather | solution.py:75
  856.4 0.8 fusion.138
  857.2 1.0 fusion.14
  858.1 1.0 fusion.15
  859.1 0.9 convolution_add_fusion.4
  860.0 1.0 convolution_subtract_fusion.4
  861.7 54.4 %all-reduce.4 = (f32[]{:T(128)}, f32[]{:T(128)}, f32[]{:T(128)}) all-reduce(f32[]{:T(128)} %get-tuple-element.17, f32[]{:T(128)} %get-tuple-element.16, f32[]{:T(128)} %get-tuple-element.15), channel_id=1, replica_groups=mesh['chan'=32,'tm'=16] {'tm'}, use_global_device_ids=true, to_apply=%region_34.35 | all-reduce | flops 3 | bytes 24 | tf_op jit(solution)/shard_map/psum | solution.py:60
  918.6 46.9 %psum.243 = f32[]{:T(128)} all-reduce(f32[]{:T(128)} %fusion.124), channel_id=1, replica_groups=mesh['chan'=32,'tm'=16] {'tm'}, use_global_device_ids=true, to_apply=%region_40.41 | all-reduce | flops 1 | bytes 8 | tf_op jit(solution)/shard_map/psum | solution.py:66
  966.4 57.9 %all_gather.28 = f32[2,2,1024]{1,0,2:T(2,128)S(1)} all-gather(f32[2,2,64]{1,0,2:T(2,128)S(1)} %copy.11), channel_id=1, replica_groups=mesh['chan'=32,'tm'=16] {'tm'}, dimensions={2}, use_global_device_ids=true | all-gather | bytes 17408 | tf_op jit(solution)/shard_map/all_gather | solution.py:75
  1025.1 1.0 fusion.12
  1026.1 1.0 fusion.13
  1027.0 0.9 convolution_add_fusion.3
  1027.9 1.0 convolution_subtract_fusion.3
  1029.7 53.8 %all-reduce.3 = (f32[]{:T(128)}, f32[]{:T(128)}, f32[]{:T(128)}) all-reduce(f32[]{:T(128)} %get-tuple-element.14, f32[]{:T(128)} %get-tuple-element.13, f32[]{:T(128)} %get-tuple-element.12), channel_id=1, replica_groups=mesh['chan'=32,'tm'=16] {'tm'}, use_global_device_ids=true, to_apply=%region_42.43 | all-reduce | flops 3 | bytes 24 | tf_op jit(solution)/shard_map/psum | solution.py:60
  1086.0 1.3 dynamic-slice
  1087.3 46.9 %psum.247 = f32[]{:T(128)} all-reduce(f32[]{:T(128)} %fusion.123), channel_id=1, replica_groups=mesh['chan'=32,'tm'=16] {'tm'}, use_global_device_ids=true, to_apply=%region_48.49 | all-reduce | flops 1 | bytes 8 | tf_op jit(solution)/shard_map/psum | solution.py:66
  1135.1 65.3 %all_gather.29 = f32[2,2,1024]{1,0,2:T(2,128)S(1)} all-gather(f32[2,2,64]{1,0,2:T(2,128)S(1)} %copy.12), channel_id=1, replica_groups=mesh['chan'=32,'tm'=16] {'tm'}, dimensions={2}, use_global_device_ids=true | all-gather | bytes 17408 | tf_op jit(solution)/shard_map/all_gather | solution.py:75
  1201.2 1.0 fusion.10
  1202.2 1.0 fusion.11
  1203.2 0.9 convolution_add_fusion.2
  1204.1 1.0 convolution_subtract_fusion.2
  1205.7 49.4 %all-reduce.2 = (f32[]{:T(128)}, f32[]{:T(128)}, f32[]{:T(128)}) all-reduce(f32[]{:T(128)} %get-tuple-element.11, f32[]{:T(128)} %get-tuple-element.10, f32[]{:T(128)} %get-tuple-element.9), channel_id=1, replica_groups=mesh['chan'=32,'tm'=16] {'tm'}, use_global_device_ids=true, to_apply=%region_50.51 | all-reduce | flops 3 | bytes 24 | tf_op jit(solution)/shard_map/psum | solution.py:60
  1258.4 52.4 %psum.251 = f32[]{:T(128)} all-reduce(f32[]{:T(128)} %fusion.122), channel_id=1, replica_groups=mesh['chan'=32,'tm'=16] {'tm'}, use_global_device_ids=true, to_apply=%region_56.57 | all-reduce | flops 1 | bytes 8 | tf_op jit(solution)/shard_map/psum | solution.py:66
  1311.6 59.6 %all_gather.30 = f32[2,2,1024]{1,0,2:T(2,128)S(1)} all-gather(f32[2,2,64]{1,0,2:T(2,128)S(1)} %copy.13), channel_id=1, replica_groups=mesh['chan'=32,'tm'=16] {'tm'}, dimensions={2}, use_global_device_ids=true | all-gather | bytes 17408 | tf_op jit(solution)/shard_map/all_gather | solution.py:75
  1372.0 1.0 fusion.8
  1373.0 1.0 fusion.9
  1374.0 0.9 convolution_add_fusion.1
  1374.9 1.0 convolution_subtract_fusion.1
  1376.5 53.3 %all-reduce.1 = (f32[]{:T(128)}, f32[]{:T(128)}, f32[]{:T(128)}) all-reduce(f32[]{:T(128)} %get-tuple-element.8, f32[]{:T(128)} %get-tuple-element.7, f32[]{:T(128)} %get-tuple-element.6), channel_id=1, replica_groups=mesh['chan'=32,'tm'=16] {'tm'}, use_global_device_ids=true, to_apply=%region_58.59 | all-reduce | flops 3 | bytes 24 | tf_op jit(solution)/shard_map/psum | solution.py:60
  1432.4 46.9 %psum.255 = f32[]{:T(128)} all-reduce(f32[]{:T(128)} %fusion.121), channel_id=1, replica_groups=mesh['chan'=32,'tm'=16] {'tm'}, use_global_device_ids=true, to_apply=%region_64.65 | all-reduce | flops 1 | bytes 8 | tf_op jit(solution)/shard_map/psum | solution.py:66
  1480.5 52.2 %all-reduce = f32[1024]{0:T(1024)S(1)} all-reduce(f32[1024]{0:T(1024)S(1)} %dynamic-update-slice), channel_id=1, replica_groups=mesh['chan'=32,'tm'=16] {'tm'}, use_global_device_ids=true, to_apply=%add | all-reduce | flops 1024 | bytes 8192
  1534.1 1.0 copy.14
  (86 shorter events, 19.5 us)
Async XLA Ops:
  7.2 164.4 %reduce-scatter.2.cloned.1.call-start = ((), (), s32[]{:S(2)}) async-start(), calls=%async_computation.1 | async-start | bytes 4456448 | tf_op jit(solution)/shard_map/reduce_scatter | solution.py:88
  14.0 0.7 copy-start.2
  171.6 3.6 collective-permute-start
  1372.0 108.1 %copy-start.1 = (f32[1,2,2,64]{3,2,1,0:T(2,128)S(1)}, f32[1,2,2,64]{3,2,1,0:T(2,128)}, u32[]{:S(2)}) copy-start(f32[1,2,2,64]{3,2,1,0:T(2,128)} %param.7) | copy-start | bytes 3076
  1372.0 162.0 %copy-start = (bf16[64,2,1024]{2,0,1:T(8,128)(2,1)S(1)}, bf16[64,2,1024]{2,0,1:T(8,128)(2,1)}, u32[]{:S(2)}) copy-start(bf16[64,2,1024]{2,0,1:T(8,128)(2,1)} %reduce-scatter.2.cloned.1.call-done) | copy-start | bytes 786436
Sparse Core Ops, SparseCore 0:
  14.1 157.3 reduce-scatter.1
where the time goes:
time: 1540 us
  blocking collectives  1290 us (84%)
  waiting for transfers between devices  157 us (10%)
  between operations  37.5 us (2%)
  matrix products  32.7 us (2%)
  other arithmetic  15.8 us (1%)
    all_gather x7, blocking collectives, subspace_gains(): basis = lax.all_gather(local_basis, 'tm', axis=2, tiled=True)  429 us
    psum x8, blocking collectives, subspace_gains(): lax.psum((local_one, local_real, local_imag), 'tm')  411 us
    psum x8, blocking collectives, subspace_gains(): lax.psum(jnp.sum(rest_real * rest_real + rest_imag * rest_imag), 'tm')  395 us
    reduce_scatter x1, waiting for transfers between devices, on_device(): lax.psum_scatter(gram_rows(masked, row_count * lax.axis_size('tm'), all_t...  156 us
    unnamed x1, blocking collectives  52.2 us
  transfers between devices with their start and end apart: 2, of which 2 were waited for; matrix products, arithmetic and copies ran while one was open for 0% of the time, Pallas kernels for 0%

commit v1 on v0

v1 whole, which is shorter than its diff:
```python
import functools, math
import numpy as np
import jax
import jax.numpy as jnp
from jax import lax
from jax.experimental import pallas as pl
from jax.experimental.pallas import tpu as pltpu
from jax.sharding import PartitionSpec as P

ITERS = 8
epsilon = 1e-06
smoothing = 0.75

def gram_kernel(scale, samples_ref, flags_ref, out_ref, left, right):
    feeds, width = samples_ref.shape[1:]
    block = out_ref.shape[0]
    step = pl.program_id(0)

    @pl.when(step == 0)
    def _():
        good = jnp.broadcast_to(flags_ref[...].astype(jnp.float32), (128, feeds)).T
        good = jnp.concatenate([good] * (width // 128), 1).astype(jnp.bfloat16)
        re = samples_ref[0] * good
        im = samples_ref[1] * good
        right[:, :width] = re
        right[:, width:] = im
        left[:, :width] = im
        left[:, width:] = -re

    rows = pl.ds(pl.multiple_of(step * block, block), block)
    nt = (((1,), (1,)), ((), ()))
    total = lax.dot_general(right[rows, :], right[...], nt, preferred_element_type=jnp.float32)
    total += lax.dot_general(left[rows, :], right[...], nt, preferred_element_type=jnp.float32)
    out_ref[...] = (total * scale).astype(jnp.bfloat16)

def gram(samples, flags, all_time):
    _, feeds, width = samples.shape
    blocks = 4
    return pl.pallas_call(
        functools.partial(gram_kernel, 1.0 / all_time),
        grid=(blocks,),
        out_shape=jax.ShapeDtypeStruct((feeds, feeds), jnp.bfloat16),
        in_specs=[pl.BlockSpec((2, feeds, width), lambda i: (0, 0, 0)), pl.BlockSpec((1, feeds), lambda i: (0, 0))],
        out_specs=pl.BlockSpec((feeds // blocks, feeds), lambda i: (i, 0)),
        scratch_shapes=[pltpu.VMEM((feeds, 2 * width), jnp.bfloat16)] * 2,
        compiler_params=pltpu.CompilerParams(vmem_limit_bytes=40 << 20),
        name="gram",
    )(samples, flags)

def basis_rows(feeds):
    f = np.arange(feeds, dtype=np.float64)
    ang = 2 * np.pi * np.arange(1, 3)[:, None] * f / feeds
    return (np.concatenate([np.cos(ang), np.sin(ang)]) / math.sqrt(feeds)).astype(np.float32)

def split3(v):
    hi = v.astype(jnp.bfloat16)
    rest = v - hi.astype(jnp.float32)
    mid = rest.astype(jnp.bfloat16)
    lo = (rest - mid.astype(jnp.float32)).astype(jnp.bfloat16)
    return hi, mid, lo

def total(v):
    return jnp.sum(v, axis=1, keepdims=True)

def solve_kernel(parity_ref, own_ref, other_ref, basis_ref, state_ref, gains_ref, scale_ref, mat, mat_t):
    feeds = mat.shape[0]
    parity = parity_ref[0]
    half = 32
    for s in range(feeds // (2 * half)):
        mat[pl.ds(pl.multiple_of(2 * half * s + half * parity, half), half), :] = own_ref[half * s:half * (s + 1), :]
        mat[pl.ds(pl.multiple_of(2 * half * s + half * (1 - parity), half), half), :] = other_ref[half * s:half * (s + 1), :]
    for i in range(feeds // 256):
        mat_t[:, 256 * i:256 * (i + 1)] = mat[256 * i:256 * (i + 1), :].T

    def sweep(_, carry):
        qr, qi, _, _ = carry
        s4 = jnp.concatenate([qr + qi, qr - qi], 0)
        hi, mid, lo = split3(s4)
        left = jnp.concatenate([hi, mid, lo, jnp.zeros_like(hi)], 0)
        with_t = jnp.dot(left, mat_t[...], preferred_element_type=jnp.float32)
        with_m = jnp.dot(left, mat[...], preferred_element_type=jnp.float32)
        with_t = (with_t[0:4] + with_t[4:8]) + with_t[8:12]
        with_m = (with_m[0:4] + with_m[4:8]) + with_m[8:12]
        zr = 0.5 * (with_t[2:4] + with_m[0:2])
        zi = 0.5 * (with_t[0:2] - with_m[2:4])
        one_r, two_r = zr[0:1], zr[1:2]
        one_i, two_i = zi[0:1], zi[1:2]
        n1 = total(one_r * one_r + one_i * one_i)
        cr = total(one_r * two_r + one_i * two_i)
        ci = total(one_r * two_i - one_i * two_r)
        first = jnp.sqrt(epsilon + n1)
        cr = cr / first
        ci = ci / first
        rest_r = two_r - (one_r * cr - one_i * ci) / first
        rest_i = two_i - (one_r * ci + one_i * cr) / first
        second = jnp.sqrt(epsilon + total(rest_r * rest_r + rest_i * rest_i))
        qr = jnp.concatenate([one_r / first, rest_r / second], 0)
        qi = jnp.concatenate([one_i / first, rest_i / second], 0)
        return qr, qi, first, second

    one = jnp.ones((1, 1), jnp.float32)
    qr, qi, first, second = lax.fori_loop(0, ITERS, sweep, (basis_ref[0:2], basis_ref[2:4], one, one))
    weights = jnp.concatenate([jnp.sqrt(first * feeds), jnp.sqrt(second * feeds)], 0)
    solved = jnp.concatenate([qr * weights, qi * weights], 0)
    gains = smoothing * state_ref[...] + (1.0 - smoothing) * solved
    gains_ref[...] = gains
    power = jnp.sum(gains * gains, axis=0, keepdims=True)
    mean_power = total(power) / feeds
    scale_ref[...] = jnp.sqrt((mean_power + epsilon) / (power + mean_power + epsilon))

def solve(parity, own, other, state):
    feeds = own.shape[1]
    vm = pl.BlockSpec(memory_space=pltpu.VMEM)
    return pl.pallas_call(
        solve_kernel,
        out_shape=(jax.ShapeDtypeStruct((4, feeds), jnp.float32), jax.ShapeDtypeStruct((1, feeds), jnp.float32)),
        in_specs=[pl.BlockSpec(memory_space=pltpu.SMEM), vm, vm, vm, vm],
        out_specs=(vm, vm),
        scratch_shapes=[pltpu.VMEM((feeds, feeds), jnp.bfloat16)] * 2,
        compiler_params=pltpu.CompilerParams(vmem_limit_bytes=40 << 20),
        name="solve",
    )(parity, own, other, jnp.asarray(basis_rows(feeds)), state)


def groups(mesh_shape_x, mesh_shape_z):
    along_x = [[x * mesh_shape_z + z for x in range(mesh_shape_x)] for z in range(mesh_shape_z)]
    along_z = [[x * mesh_shape_z + z for z in range(mesh_shape_z)] for x in range(mesh_shape_x)]
    return along_x, along_z


def exchange(value, which):
    return lax.all_to_all(value, "tm", 0, 0, axis_index_groups=which)


def swap_cores(value):
    count = lax.axis_size("chan")
    return lax.ppermute(value, "chan", [(i, i ^ 1) for i in range(count)])


def on_device(samples, feed_flags, cal_channel, gain_state):
    feeds = samples.shape[2]
    tm_count = lax.axis_size("tm")
    nx = nz = 4
    along_x, along_z = groups(nx, nz)
    rows = feeds // tm_count
    half = rows // 2
    tm = lax.axis_index("tm")
    chan = lax.axis_index("chan")
    parity = chan % 2
    f32, bf16 = jnp.float32, jnp.bfloat16

    state = lax.all_gather(gain_state[0], "tm", axis=2, tiled=True).reshape(4, feeds)
    packed = gram(samples[0], feed_flags, samples.shape[3] * tm_count)

    part = exchange(packed.reshape(nx, nz * rows, feeds), along_x)
    part = jnp.sum(part.astype(f32), axis=0).astype(bf16)
    part = exchange(part.reshape(nz, rows, feeds), along_z)
    mine = jnp.sum(part.astype(f32), axis=0)
    sent = mine.astype(bf16)

    is_cal = cal_channel[chan // 2] == chan
    keep = lax.dynamic_slice_in_dim(sent, parity * half, half, 0)
    give = lax.dynamic_slice_in_dim(sent, (1 - parity) * half, half, 0)
    cal_rows = jnp.where(is_cal, keep, swap_cores(give))

    mirror = sent.reshape(rows, nx, nz, rows).transpose(2, 0, 1, 3)
    mirror = mirror.reshape(nz, 4, rows // 4, nx * rows).transpose(0, 2, 1, 3).reshape(nz, rows // 4, feeds)
    payload = jnp.concatenate([jnp.broadcast_to(cal_rows[None], (nz, half, feeds)), mirror], 1)
    got = exchange(payload, along_z)
    cal_rows = got[:, :half].reshape(nz * half, feeds)
    mirror = got[:, half:].reshape(nz, rows // 4, 4, nx * rows).transpose(0, 2, 1, 3).reshape(nz * rows, nx * rows)
    mirror = mirror.T.reshape(nx, 4, rows // 4, nz * rows).transpose(0, 2, 1, 3).reshape(nx, rows // 4, feeds)
    payload = jnp.concatenate([jnp.broadcast_to(cal_rows[None], (nx, nz * half, feeds)), mirror], 1)
    got = exchange(payload, along_x)
    own = got[:, : nz * half].reshape(feeds // 2, feeds)
    other = swap_cores(own)
    mirror = got[:, nz * half :].reshape(nx, rows // 4, 4, nz * rows).transpose(2, 1, 0, 3).reshape(rows, feeds)

    gains, scale = solve(parity.reshape(1).astype(jnp.int32), own, other, state)
    gains_now = lax.dynamic_slice_in_dim(gains, tm * rows, rows, 1).reshape(1, 2, 2, rows)
    scale_rows = lax.dynamic_slice_in_dim(scale[0], tm * rows, rows, 0)
    mirror = mirror.astype(f32)
    both = 0.5 * jnp.stack([mine + mirror, mine - mirror], 1)
    calibrated = (both * scale_rows[:, None, None] * scale[0][None, None, :]).astype(bf16)
    return (calibrated[None], gains_now)


def solution(mesh):
    return jax.shard_map(
        on_device,
        mesh=mesh,
        in_specs=(P("chan", None, None, "tm"), P("chan", None), P(), P("chan", None, None, "tm")),
        out_specs=(P("chan", "tm", None, None), P("chan", None, None, "tm")),
        check_vma=False,
    )
```

time: 1540 us -> 235 us (0.15)
  the two profiles are of different devices: /device:TPU:88 before, /device:TPU:96 now
where the time goes in v1:
time: 235 us; the launch traced here: 234 us
  blocking collectives  167 us (71%)
  waiting for transfers between devices  24.9 us (11%)
  starting transfers between devices  16.4 us (7%)
  Pallas kernels  11.3 us (5%)
  local copies, waits for them, and re-layouts  10.3 us (4%)
  other arithmetic  2.48 us (1%)
    all_gather x1, blocking collectives, on_device(): lax.all_gather(gain_state[0], 'tm', axis=2, tiled=True).reshape(4, feeds)  86.1 us
    all_to_all x3, blocking collectives, exchange(): return lax.all_to_all(value, 'tm', 0, 0, axis_index_groups=which)  81.2 us
    all_to_all x1, waiting for transfers between devices, exchange(): return lax.all_to_all(value, 'tm', 0, 0, axis_index_groups=which)  24.9 us
    all_to_all x1, starting transfers between devices, exchange(): return lax.all_to_all(value, 'tm', 0, 0, axis_index_groups=which)  12.5 us
    pallas_call x1, Pallas kernels, solve(): pl.pallas_call(solve_kernel, out_shape=(jax.ShapeDtypeStruct((4, feeds),...  8.11 us
  transfers between devices with their start and end apart: 3, of which 1 were waited for; matrix products, arithmetic and copies ran while one was open for 3% of the time, Pallas kernels for 0%

profile of v1, /device:TPU:96, one launch (start us, length us, event | category | flops | bytes accessed | tf_op | source)
XLA Modules:
  0.0 234.2 jit_solution(4641811225617132683)
XLA Ops:
  0.6 0.0 copy-start
  0.6 1.2 copy-done
  1.9 0.0 copy-start.2
  1.9 0.7 copy-done.2
  2.5 3.2 %gram.1 = bf16[1024,1024]{1,0:T(8,128)(2,1)S(1)} custom-call(bf16[2,1024,256]{2,1,0:T(8,128)(2,1)S(1)} %bitcast.43, s32[1,1024]{1,0:T(1,128)S(1)} %copy-done.2), custom_call_target="tpu_custom_call" | custom-call | tf_op jit(solution)/shard_map/gram/pallas_call | solution.py:39
  5.8 30.4 %all_to_all.20 = bf16[4,256,1024]{2,1,0:T(8,128)(2,1)S(1)} all-to-all(bf16[4,256,1024]{2,1,0:T(8,128)(2,1)S(1)} %bitcast.40), channel_id=1, replica_groups={{0,4,8,12},{1,5,9,13},{2,6,10,14},{3,7,11,15},{16,20,24,28},{17,21,25,2..., dimensions={0} | all-to-all | bytes 4194304 | tf_op jit(solution)/shard_map/all_to_all | solution.py:132
  36.2 1.3 reduce_sum.23
  37.5 0.0 copy-start.4
  37.5 12.5 %all-to-all-start.1 = ((bf16[4,64,1024]{2,1,0:T(8,128)(2,1)}), bf16[4,64,1024]{2,1,0:T(8,128)(2,1)S(1)}, u32[]{:S(2)}, u32[]{:S(2)}) async-start(bf16[4,64,1024]{2,1,0:T(8,128)(2,1)} %bitcast.2), calls=%async_computation.1 | async-start | bytes 1048576 | tf_op jit(solution)/shard_map/all_to_all | solution.py:132
  50.0 24.9 %all-to-all-done.1 = bf16[4,64,1024]{2,1,0:T(8,128)(2,1)S(1)} async-done(((bf16[4,64,1024]{2,1,0:T(8,128)(2,1)}), bf16[4,64,1024]{2,1,0:T(8,128)(2,1)S(1)}, u32[]{:S(2)}, u32[]{:S(2)}) %all-to-all-start.1) | async-done | bytes 524320 | tf_op jit(solution)/shard_map/all_to_all | solution.py:132
  74.9 0.1 convert_reduce_fusion
  75.0 1.9 collective-permute-start
  77.0 0.0 copy-done.4
  77.0 0.6 dynamic_slice.15
  78.2 0.2 convert_element_type.59
  78.4 0.1 copy.39
  78.5 0.2 reshape.134
  78.8 0.0 collective-permute-done
  78.9 31.7 %all_to_all.21 = bf16[4,48,1024]{2,1,0:T(8,128)(2,1)S(1)} all-to-all(bf16[4,48,1024]{2,1,0:T(8,128)(2,1)S(1)} %pad_maximum_fusion.1), channel_id=1, replica_groups={{0,1,2,3},{4,5,6,7},{8,9,10,11},{12,13,14,15},{16,17,18,19},{20,21,22,2..., dimensions={0} | all-to-all | bytes 786432 | tf_op jit(solution)/shard_map/all_to_all | solution.py:132
  110.6 0.1 reshape.136
  110.7 0.1 copy.28
  110.9 0.1 broadcast_in_dim.8
  111.0 0.1 pad_maximum_fusion
  111.1 19.0 %all_to_all.22 = bf16[4,144,1024]{2,1,0:T(8,128)(2,1)S(1)} all-to-all(bf16[4,144,1024]{2,1,0:T(8,128)(2,1)S(1)} %pad_maximum_fusion), channel_id=1, replica_groups={{0,4,8,12},{1,5,9,13},{2,6,10,14},{3,7,11,15},{16,20,24,28},{17,21,25,2..., dimensions={0} | all-to-all | bytes 2359296 | tf_op jit(solution)/shard_map/all_to_all | solution.py:132
  130.1 0.0 copy-start.3
  130.1 0.1 slice.19
  130.2 1.9 collective-permute-start.1
  132.1 0.0 copy-done.3
  132.1 0.7 copy.31
  132.9 86.1 %all-gather = f32[1,2,2,1024]{2,1,0,3:T(2,128)} all-gather(f32[1,2,2,64]{2,1,0,3:T(2,128)} %copy.31), channel_id=2, replica_groups=mesh['chan'=32,'tm'=16] {'tm'}, dimensions={3}, use_global_device_ids=true | all-gather | bytes 17408 | tf_op jit(solution)/shard_map/all_gather | solution.py:152
  218.9 2.0 copy.32
  221.0 0.7 reshape.142.state_ref
  221.7 0.7 slice_convert_fusion
  222.4 1.1 reshape.145
  223.5 0.0 copy-start.1
  223.5 0.2 copy.38
  223.7 0.1 reshape.144
  223.9 0.0 collective-permute-done.1.other_ref
  223.9 0.3 copy-done.1
  224.2 8.1 %solve.1 = (f32[4,1024]{1,0:T(4,128)S(1)}, f32[1,1024]{1,0:T(1,128)S(1)}) custom-call(s32[1]{0:T(128)} %bitcast.16.parity_ref, bf16[512,1024]{1,0:T(8,128)(2,1)S(1)} %bitcast.42, bf16[512,1024]{1,0:T(8,128)(2,1)S(1)} %collective-permute-done.1.other_ref, f32[4,1024]{1,0:T(4,128)S(1)} %copy-done.1, f32[4,1024]{1,0:T(4,128)S(1)} %reshape.142.state_ref), custom_call_target="tpu_custom_call" | custom-call | tf_op jit(solution)/shard_map/solve/pallas_call | solution.py:114
  232.3 0.1 fusion.5
  232.4 0.1 fusion.1
  232.5 1.0 copy.33
  233.5 0.6 constant_dynamic-slice_fusion
  (11 shorter events, 0.2 us)
Async XLA Ops:
  0.6 1.2 copy-start
  1.9 0.7 copy-start.2
  37.5 39.5 %copy-start.4 = (s32[16]{0:T(128)S(1)}, s32[16]{0:T(128)}, u32[]{:S(2)}) copy-start(s32[16]{0:T(128)} %param.7) | copy-start | bytes 196
  37.5 37.4 %all-to-all-start.1 = ((bf16[4,64,1024]{2,1,0:T(8,128)(2,1)}), bf16[4,64,1024]{2,1,0:T(8,128)(2,1)S(1)}, u32[]{:S(2)}, u32[]{:S(2)}) async-start(bf16[4,64,1024]{2,1,0:T(8,128)(2,1)} %bitcast.2), calls=%async_computation.1 | async-start | bytes 1048576 | tf_op jit(solution)/shard_map/all_to_all | solution.py:132
  75.0 3.7 %collective-permute-start = (bf16[32,1024]{1,0:T(8,128)(2,1)S(1)}, bf16[32,1024]{1,0:T(8,128)(2,1)S(1)}, u32[]{:S(2)}, u32[]{:S(2)}) collective-permute-start(bf16[32,1024]{1,0:T(8,128)(2,1)S(1)} %constant_dynamic-slice_fusion.2), channel_id=1, source_target_pairs={{0,16},{16,0},{32,48},{48,32},{64,80},{80,64},{96,112},{112,96},{1... | collective-permute-start | bytes 196616 | tf_op jit(solution)/shard_map/ppermute | solution.py:137
  130.1 2.0 copy-start.3
  130.2 93.7 %collective-permute-start.1 = (bf16[512,1024]{1,0:T(8,128)(2,1)S(1)}, bf16[512,1024]{1,0:T(8,128)(2,1)S(1)}, u32[]{:S(2)}, u32[]{:S(2)}) collective-permute-start(bf16[512,1024]{1,0:T(8,128)(2,1)S(1)} %bitcast.41), channel_id=1, source_target_pairs={{0,16},{16,0},{32,48},{48,32},{64,80},{80,64},{96,112},{112,96},{1... | collective-permute-start | bytes 3145736 | tf_op jit(solution)/shard_map/ppermute | solution.py:137
  223.5 0.7 copy-start.1

commit v2 on v1

--- a/solution.py
+++ b/solution.py
@@ -62,15 +62,12 @@
 def total(v):
     return jnp.sum(v, axis=1, keepdims=True)
 
-def solve_kernel(parity_ref, own_ref, other_ref, basis_ref, state_ref, gains_ref, scale_ref, mat, mat_t):
-    feeds = mat.shape[0]
-    parity = parity_ref[0]
-    half = 32
-    for s in range(feeds // (2 * half)):
-        mat[pl.ds(pl.multiple_of(2 * half * s + half * parity, half), half), :] = own_ref[half * s:half * (s + 1), :]
-        mat[pl.ds(pl.multiple_of(2 * half * s + half * (1 - parity), half), half), :] = other_ref[half * s:half * (s + 1), :]
+def solve_kernel(place_ref, own_ref, basis_ref, solved_ref, mirror_ref, mat_t):
+    feeds = own_ref.shape[0]
+    rows = mirror_ref.shape[0]
     for i in range(feeds // 256):
-        mat_t[:, 256 * i:256 * (i + 1)] = mat[256 * i:256 * (i + 1), :].T
+        mat_t[:, 256 * i:256 * (i + 1)] = own_ref[256 * i:256 * (i + 1), :].T
+    mirror_ref[...] = mat_t[pl.ds(pl.multiple_of(place_ref[0] * rows, rows), rows), :]
 
     def sweep(_, carry):
         qr, qi, _, _ = carry
@@ -78,7 +75,7 @@
         hi, mid, lo = split3(s4)
         left = jnp.concatenate([hi, mid, lo, jnp.zeros_like(hi)], 0)
         with_t = jnp.dot(left, mat_t[...], preferred_element_type=jnp.float32)
-        with_m = jnp.dot(left, mat[...], preferred_element_type=jnp.float32)
+        with_m = jnp.dot(left, own_ref[...], preferred_element_type=jnp.float32)
         with_t = (with_t[0:4] + with_t[4:8]) + with_t[8:12]
         with_m = (with_m[0:4] + with_m[4:8]) + with_m[8:12]
         zr = 0.5 * (with_t[2:4] + with_m[0:2])
@@ -101,25 +98,59 @@
     one = jnp.ones((1, 1), jnp.float32)
     qr, qi, first, second = lax.fori_loop(0, ITERS, sweep, (basis_ref[0:2], basis_ref[2:4], one, one))
     weights = jnp.concatenate([jnp.sqrt(first * feeds), jnp.sqrt(second * feeds)], 0)
-    solved = jnp.concatenate([qr * weights, qi * weights], 0)
-    gains = smoothing * state_ref[...] + (1.0 - smoothing) * solved
-    gains_ref[...] = gains
-    power = jnp.sum(gains * gains, axis=0, keepdims=True)
-    mean_power = total(power) / feeds
-    scale_ref[...] = jnp.sqrt((mean_power + epsilon) / (power + mean_power + epsilon))
-
-def solve(parity, own, other, state):
+    solved_ref[...] = jnp.concatenate([qr * weights, qi * weights], 0)
+
+
+def solve(place, own, rows):
     feeds = own.shape[1]
     vm = pl.BlockSpec(memory_space=pltpu.VMEM)
     return pl.pallas_call(
         solve_kernel,
-        out_shape=(jax.ShapeDtypeStruct((4, feeds), jnp.float32), jax.ShapeDtypeStruct((1, feeds), jnp.float32)),
-        in_specs=[pl.BlockSpec(memory_space=pltpu.SMEM), vm, vm, vm, vm],
+        out_shape=(jax.ShapeDtypeStruct((4, feeds), jnp.float32), jax.ShapeDtypeStruct((rows, feeds), jnp.bfloat16)),
+        in_specs=[pl.BlockSpec(memory_space=pltpu.SMEM), vm, vm],
         out_specs=(vm, vm),
-        scratch_shapes=[pltpu.VMEM((feeds, feeds), jnp.bfloat16)] * 2,
+        scratch_shapes=[pltpu.VMEM((feeds, feeds), jnp.bfloat16)],
         compiler_params=pltpu.CompilerParams(vmem_limit_bytes=40 << 20),
         name="solve",
-    )(parity, own, other, jnp.asarray(basis_rows(feeds)), state)
+    )(place, own, jnp.asarray(basis_rows(feeds)))
+
+
+def rescale_kernel(place_ref, cal_ref, kept_ref, swapped_ref, state_ref, mine_ref, mirror_ref,
+                   gains_ref, out_ref, turned):
+    feeds = mine_ref.shape[1]
+    rows = mine_ref.shape[0]
+    place = place_ref[0]
+    is_cal = cal_ref[0] > 0
+    solved = jnp.where(is_cal, kept_ref[...], swapped_ref[...])
+    state = jnp.where(is_cal, swapped_ref[...], state_ref[...])
+    gains = smoothing * state + (1.0 - smoothing) * solved
+    gains_ref[...] = gains
+    power = jnp.sum(gains * gains, axis=0, keepdims=True)
+    mean_power = total(power) / feeds
+    scale = jnp.sqrt((mean_power + epsilon) / (power + mean_power + epsilon))
+    turned[...] = jnp.broadcast_to(scale, (128, feeds)).T
+    down = turned[pl.ds(pl.multiple_of(place * rows, rows), rows), :]
+    down = jnp.concatenate([down] * (feeds // 128), 1)
+    factor = 0.5 * (down * scale)
+    mine = mine_ref[...]
+    mirror = mirror_ref[...].astype(jnp.float32)
+    out_ref[0] = ((mine + mirror) * factor).astype(jnp.bfloat16)
+    out_ref[1] = ((mine - mirror) * factor).astype(jnp.bfloat16)
+
+
+def rescale(place, cal, kept, swapped, state, mine, mirror):
+    rows, feeds = mine.shape
+    vm = pl.BlockSpec(memory_space=pltpu.VMEM)
+    sm = pl.BlockSpec(memory_space=pltpu.SMEM)
+    return pl.pallas_call(
+        rescale_kernel,
+        out_shape=(jax.ShapeDtypeStruct((4, feeds), jnp.float32), jax.ShapeDtypeStruct((2, rows, feeds), jnp.bfloat16)),
+        in_specs=[sm, sm] + [vm] * 5,
+        out_specs=(vm, vm),
+        scratch_shapes=[pltpu.VMEM((feeds, 128), jnp.float32)],
+        compiler_params=pltpu.CompilerParams(vmem_limit_bytes=40 << 20),
+        name="rescale",
+    )(place, cal, kept, swapped, state, mine, mirror)
 
 
 def groups(mesh_shape_x, mesh_shape_z):
@@ -143,46 +174,54 @@
     nx = nz = 4
     along_x, along_z = groups(nx, nz)
     rows = feeds // tm_count
-    half = rows // 2
+    thin = rows // nz
     tm = lax.axis_index("tm")
     chan = lax.axis_index("chan")
-    parity = chan % 2
     f32, bf16 = jnp.float32, jnp.bfloat16
-
-    state = lax.all_gather(gain_state[0], "tm", axis=2, tiled=True).reshape(4, feeds)
+    place = tm.reshape(1).astype(jnp.int32)
+    is_cal = cal_channel[chan // 2] == chan
+    samples, feed_flags, is_cal, place = lax.optimization_barrier((samples, feed_flags, is_cal, place))
+    cal = is_cal.reshape(1).astype(jnp.int32)
+
     packed = gram(samples[0], feed_flags, samples.shape[3] * tm_count)
-
+    packed, own_state = lax.optimization_barrier((packed, gain_state[0].reshape(4, rows)))
     part = exchange(packed.reshape(nx, nz * rows, feeds), along_x)
+    other_state = swap_cores(own_state)
+    part, other_state = lax.optimization_barrier((part, other_state))
     part = jnp.sum(part.astype(f32), axis=0).astype(bf16)
     part = exchange(part.reshape(nz, rows, feeds), along_z)
+    part, states = lax.optimization_barrier((part, jnp.concatenate([own_state, other_state], 0)))
     mine = jnp.sum(part.astype(f32), axis=0)
     sent = mine.astype(bf16)
 
-    is_cal = cal_channel[chan // 2] == chan
-    keep = lax.dynamic_slice_in_dim(sent, parity * half, half, 0)
-    give = lax.dynamic_slice_in_dim(sent, (1 - parity) * half, half, 0)
-    cal_rows = jnp.where(is_cal, keep, swap_cores(give))
-
-    mirror = sent.reshape(rows, nx, nz, rows).transpose(2, 0, 1, 3)
-    mirror = mirror.reshape(nz, 4, rows // 4, nx * rows).transpose(0, 2, 1, 3).reshape(nz, rows // 4, feeds)
-    payload = jnp.concatenate([jnp.broadcast_to(cal_rows[None], (nz, half, feeds)), mirror], 1)
-    got = exchange(payload, along_z)
-    cal_rows = got[:, :half].reshape(nz * half, feeds)
-    mirror = got[:, half:].reshape(nz, rows // 4, 4, nx * rows).transpose(0, 2, 1, 3).reshape(nz * rows, nx * rows)
-    mirror = mirror.T.reshape(nx, 4, rows // 4, nz * rows).transpose(0, 2, 1, 3).reshape(nx, rows // 4, feeds)
-    payload = jnp.concatenate([jnp.broadcast_to(cal_rows[None], (nx, nz * half, feeds)), mirror], 1)
-    got = exchange(payload, along_x)
-    own = got[:, : nz * half].reshape(feeds // 2, feeds)
-    other = swap_cores(own)
-    mirror = got[:, nz * half :].reshape(nx, rows // 4, 4, nz * rows).transpose(2, 1, 0, 3).reshape(rows, feeds)
-
-    gains, scale = solve(parity.reshape(1).astype(jnp.int32), own, other, state)
+    def with_cal(_):
+        got = exchange(jnp.broadcast_to(sent[None], (nz, rows, feeds)), along_z)
+        got = exchange(jnp.broadcast_to(got.reshape(1, nz * rows, feeds), (nx, nz * rows, feeds)), along_x)
+        solved, mirror = solve(place, got.reshape(feeds, feeds), rows)
+        return solved, jnp.zeros((4, feeds), f32), mirror
+
+    def without(_):
+        high = states.astype(bf16)
+        low = (states - high.astype(f32)).astype(bf16)
+        halves = jnp.concatenate([high, low], 0)
+        halves = jnp.broadcast_to(jnp.pad(halves, ((0, 0), (0, feeds - rows)))[None], (nz, 16, feeds))
+        mirror = sent.reshape(rows, nx, nz, rows).transpose(2, 0, 1, 3)
+        mirror = mirror.reshape(nz, 4, thin, nx * rows).transpose(0, 2, 1, 3).reshape(nz, thin, feeds)
+        got = exchange(jnp.concatenate([mirror, halves], 1), along_z)
+        halves = got[:, thin:, :rows].transpose(1, 0, 2).reshape(16, nz * rows)
+        halves = jnp.broadcast_to(jnp.pad(halves, ((0, 0), (0, feeds - nz * rows)))[None], (nx, 16, feeds))
+        mirror = got[:, :thin].reshape(nz, thin, 4, nx * rows).transpose(0, 2, 1, 3).reshape(nz * rows, nx * rows)
+        mirror = mirror.T.reshape(nx, 4, thin, nz * rows).transpose(0, 2, 1, 3).reshape(nx, thin, feeds)
+        got = exchange(jnp.concatenate([mirror, halves], 1), along_x)
+        halves = got[:, thin:, : nz * rows].transpose(1, 0, 2).reshape(16, feeds).astype(f32)
+        both = halves[:8] + halves[8:]
+        mirror = got[:, :thin].reshape(nx, thin, 4, nz * rows).transpose(2, 1, 0, 3).reshape(rows, feeds)
+        return both[4:], both[:4], mirror
+
+    kept, held, mirror = lax.cond(is_cal, with_cal, without, None)
+    gains, calibrated = rescale(place, cal, kept, swap_cores(kept), held, mine, mirror)
     gains_now = lax.dynamic_slice_in_dim(gains, tm * rows, rows, 1).reshape(1, 2, 2, rows)
-    scale_rows = lax.dynamic_slice_in_dim(scale[0], tm * rows, rows, 0)
-    mirror = mirror.astype(f32)
-    both = 0.5 * jnp.stack([mine + mirror, mine - mirror], 1)
-    calibrated = (both * scale_rows[:, None, None] * scale[0][None, None, :]).astype(bf16)
-    return (calibrated[None], gains_now)
+    return (calibrated.transpose(1, 0, 2)[None], gains_now)
 
 
 def solution(mesh):

time: 235 us -> 146 us (0.62)
  the two profiles are of different devices: /device:TPU:96 before, /device:TPU:25 now
where the time goes in v2:
time: 146 us; the launch traced here: 145 us
  starting transfers between devices  55 us (38%)
  waiting for transfers between devices  49.3 us (34%)
  blocking collectives  27.2 us (19%)
  local copies, waits for them, and re-layouts  5.84 us (4%)
  Pallas kernels  4.45 us (3%)
  other arithmetic  1.46 us (1%)
    all_to_all x2, waiting for transfers between devices, exchange(): return lax.all_to_all(value, 'tm', 0, 0, axis_index_groups=which)  47.7 us
    ppermute x2, starting transfers between devices, swap_cores(): return lax.ppermute(value, 'chan', [(i, i ^ 1) for i in range(count)])  36 us
    all_to_all x2, blocking collectives, exchange(): return lax.all_to_all(value, 'tm', 0, 0, axis_index_groups=which)  27.2 us
    all_to_all x2, starting transfers between devices, exchange(): return lax.all_to_all(value, 'tm', 0, 0, axis_index_groups=which)  18.9 us
    pallas_call x1, Pallas kernels, gram(): pl.pallas_call(functools.partial(gram_kernel, 1.0 / all_time), grid=(bloc...  4.03 us
  transfers between devices with their start and end apart: 4, of which 4 were waited for; matrix products, arithmetic and copies ran while one was open for 0% of the time, Pallas kernels for 0%

profile of v2, /device:TPU:25, one launch (start us, length us, event | category | flops | bytes accessed | tf_op | source)
XLA Modules:
  0.0 144.8 jit_solution(7341309158038052061)
XLA Ops:
  0.6 1.2 dynamic_slice.6
  2.5 0.0 copy-start
  2.6 1.2 copy-done
  3.8 0.0 copy-start.2
  3.8 0.7 copy-done.2
  4.5 4.0 %gram.1 = bf16[1024,1024]{1,0:T(8,128)(2,1)} custom-call(bf16[2,1024,256]{2,1,0:T(8,128)(2,1)S(1)} %bitcast.39, s32[1,1024]{1,0:T(1,128)S(1)} %copy-done.2), custom_call_target="tpu_custom_call" | custom-call | tf_op jit(solution)/shard_map/gram/pallas_call | solution.py:39
  8.5 0.0 copy-start.3
  8.5 4.1 %all-to-all-start.4 = ((bf16[4,256,1024]{2,1,0:T(8,128)(2,1)}), bf16[4,256,1024]{2,1,0:T(8,128)(2,1)S(1)}, u32[]{:S(2)}, u32[]{:S(2)}) async-start(bf16[4,256,1024]{2,1,0:T(8,128)(2,1)} %bitcast.21), calls=%async_computation.4 | async-start | bytes 4194304 | tf_op jit(solution)/shard_map/all_to_all | solution.py:163
  12.6 0.0 copy-done.3
  12.6 2.9 %collective-permute-start = (f32[4,64]{1,0:T(4,128)S(1)}, f32[4,64]{1,0:T(4,128)S(1)}, u32[]{:S(2)}, u32[]{:S(2)}) collective-permute-start(f32[4,64]{1,0:T(4,128)S(1)} %bitcast.55), channel_id=1, source_target_pairs={{0,16},{16,0},{32,48},{48,32},{64,80},{80,64},{96,112},{112,96},{1... | collective-permute-start | bytes 3080 | tf_op jit(solution)/shard_map/ppermute | solution.py:168
  15.5 0.8 collective-permute-done
  16.3 21.8 %all-to-all-done.4 = bf16[4,256,1024]{2,1,0:T(8,128)(2,1)S(1)} async-done(((bf16[4,256,1024]{2,1,0:T(8,128)(2,1)}), bf16[4,256,1024]{2,1,0:T(8,128)(2,1)S(1)}, u32[]{:S(2)}, u32[]{:S(2)}) %all-to-all-start.4) | async-done | bytes 2097184 | tf_op jit(solution)/shard_map/all_to_all | solution.py:163
  38.1 1.3 reduce_sum.21
  39.3 14.8 %all-to-all-start.5 = ((bf16[4,64,1024]{2,1,0:T(8,128)(2,1)}), bf16[4,64,1024]{2,1,0:T(8,128)(2,1)S(1)}, u32[]{:S(2)}, u32[]{:S(2)}) async-start(bf16[4,64,1024]{2,1,0:T(8,128)(2,1)} %bitcast.22), calls=%async_computation.5 | async-start | bytes 1048576 | tf_op jit(solution)/shard_map/all_to_all | solution.py:163
  54.2 25.9 %all-to-all-done.5 = bf16[4,64,1024]{2,1,0:T(8,128)(2,1)S(1)} async-done(((bf16[4,64,1024]{2,1,0:T(8,128)(2,1)}), bf16[4,64,1024]{2,1,0:T(8,128)(2,1)S(1)}, u32[]{:S(2)}, u32[]{:S(2)}) %all-to-all-start.5) | async-done | bytes 524320 | tf_op jit(solution)/shard_map/all_to_all | solution.py:163
  80.1 0.1 convert_reduce_fusion.mine_ref
  80.2 28.5 %conditional.1 = (f32[4,1024]{1,0:T(4,128)S(1)}, f32[4,1024]{1,0:T(4,128)S(1)}, bf16[64,1024]{1,0:T(8,128)(2,1)S(1)}) conditional(s32[]{:T(128)} %convert_element_type.42, (bf16[64,1024]{1,0:T(8,128)(2,1)S(1)}, f32[8,64]{1,0:T(8,128)S(1)}) %tuple.24, (bf16[64,1024]{1,0:T(8,128)(2,1)S(1)}, s32[1]{0:T(128)}, ()) %tuple.25), branch_computations={%region_2.3_spmd, %region_3.4_spmd} | conditional | flops 1189888 | bytes 8601656 | solution.py:221
  80.2 0.2 reshape.49
  80.4 0.1 copy.39
  80.5 0.2 reshape.50
  80.8 19.0 %all_to_all.26 = bf16[4,32,1024]{2,1,0:T(8,128)(2,1)S(1)} all-to-all(bf16[4,32,1024]{2,1,0:T(8,128)(2,1)S(1)} %pad_maximum_fusion), channel_id=1, replica_groups={{0,1,2,3},{4,5,6,7},{8,9,10,11},{12,13,14,15},{16,17,18,19},{20,21,22,2..., dimensions={0} | all-to-all | bytes 524288 | tf_op jit(solution)/shard_map/cond/branch_0_fun/all_to_all | solution.py:163
  99.8 0.1 reshape.52
  99.9 0.1 copy.30
  100.1 0.1 reshape.56
  100.2 8.2 %all_to_all.27 = bf16[4,32,1024]{2,1,0:T(8,128)(2,1)S(1)} all-to-all(bf16[4,32,1024]{2,1,0:T(8,128)(2,1)S(1)} %pad_maximum_fusion.1), channel_id=1, replica_groups={{0,4,8,12},{1,5,9,13},{2,6,10,14},{3,7,11,15},{16,20,24,28},{17,21,25,2..., dimensions={0} | all-to-all | bytes 524288 | tf_op jit(solution)/shard_map/cond/branch_0_fun/all_to_all | solution.py:163
  108.5 0.1 reshape.57
  108.6 0.1 copy.33
  108.7 33.2 %collective-permute-start.1 = (f32[4,1024]{1,0:T(4,128)S(1)}, f32[4,1024]{1,0:T(4,128)S(1)}, u32[]{:S(2)}, u32[]{:S(2)}) collective-permute-start(f32[4,1024]{1,0:T(4,128)S(1)} %get-tuple-element.44.kept_ref), channel_id=1, source_target_pairs={{0,16},{16,0},{32,48},{48,32},{64,80},{80,64},{96,112},{112,96},{1... | collective-permute-start | bytes 49160 | tf_op jit(solution)/shard_map/ppermute | solution.py:168
  141.9 0.8 collective-permute-done.1.swapped_ref
  142.7 0.4 rescale.1
  143.2 1.0 copy.34
  144.1 0.6 constant_dynamic-slice_fusion
  (20 shorter events, 0.2 us)
Async XLA Ops:
  2.5 1.2 copy-start
  3.8 0.7 copy-start.2
  8.5 4.1 %copy-start.3 = (f32[1,2,2,64]{3,2,1,0:T(2,128)S(1)}, f32[1,2,2,64]{3,2,1,0:T(2,128)}, u32[]{:S(2)}) copy-start(f32[1,2,2,64]{3,2,1,0:T(2,128)} %param.10) | copy-start | bytes 3076
  8.5 29.6 %all-to-all-start.4 = ((bf16[4,256,1024]{2,1,0:T(8,128)(2,1)}), bf16[4,256,1024]{2,1,0:T(8,128)(2,1)S(1)}, u32[]{:S(2)}, u32[]{:S(2)}) async-start(bf16[4,256,1024]{2,1,0:T(8,128)(2,1)} %bitcast.21), calls=%async_computation.4 | async-start | bytes 4194304 | tf_op jit(solution)/shard_map/all_to_all | solution.py:163
  12.6 3.7 %collective-permute-start = (f32[4,64]{1,0:T(4,128)S(1)}, f32[4,64]{1,0:T(4,128)S(1)}, u32[]{:S(2)}, u32[]{:S(2)}) collective-permute-start(f32[4,64]{1,0:T(4,128)S(1)} %bitcast.55), channel_id=1, source_target_pairs={{0,16},{16,0},{32,48},{48,32},{64,80},{80,64},{96,112},{112,96},{1... | collective-permute-start | bytes 3080 | tf_op jit(solution)/shard_map/ppermute | solution.py:168
  39.3 40.7 %all-to-all-start.5 = ((bf16[4,64,1024]{2,1,0:T(8,128)(2,1)}), bf16[4,64,1024]{2,1,0:T(8,128)(2,1)S(1)}, u32[]{:S(2)}, u32[]{:S(2)}) async-start(bf16[4,64,1024]{2,1,0:T(8,128)(2,1)} %bitcast.22), calls=%async_computation.5 | async-start | bytes 1048576 | tf_op jit(solution)/shard_map/all_to_all | solution.py:163
  108.7 34.0 %collective-permute-start.1 = (f32[4,1024]{1,0:T(4,128)S(1)}, f32[4,1024]{1,0:T(4,128)S(1)}, u32[]{:S(2)}, u32[]{:S(2)}) collective-permute-start(f32[4,1024]{1,0:T(4,128)S(1)} %get-tuple-element.44.kept_ref), channel_id=1, source_target_pairs={{0,16},{16,0},{32,48},{48,32},{64,80},{80,64},{96,112},{112,96},{1... | collective-permute-start | bytes 49160 | tf_op jit(solution)/shard_map/ppermute | solution.py:168

commit v3 on v2

--- a/solution.py
+++ b/solution.py
@@ -11,41 +11,89 @@
 epsilon = 1e-06
 smoothing = 0.75
 
-def gram_kernel(scale, samples_ref, flags_ref, out_ref, left, right):
+def gram_kernel(scale, cal_hbm, samples_hbm, flags_hbm, out_ref, is_cal_ref, cal_ref, samples_ref, flags_ref, left,
+                right, sems):
     feeds, width = samples_ref.shape[1:]
     block = out_ref.shape[0]
     step = pl.program_id(0)
 
     @pl.when(step == 0)
     def _():
+        copies = [
+            pltpu.make_async_copy(cal_hbm, cal_ref, sems.at[0]),
+            pltpu.make_async_copy(flags_hbm, flags_ref, sems.at[1]),
+            pltpu.make_async_copy(samples_hbm.at[0], samples_ref.at[0], sems.at[2]),
+            pltpu.make_async_copy(samples_hbm.at[1], samples_ref.at[1], sems.at[3]),
+        ]
+        for copy in copies:
+            copy.start()
+        copies[0].wait()
+        chan = lax.axis_index("chan")
+        is_cal_ref[0] = (cal_ref[chan // 2] == chan).astype(jnp.int32)
+        copies[1].wait()
         good = jnp.broadcast_to(flags_ref[...].astype(jnp.float32), (128, feeds)).T
         good = jnp.concatenate([good] * (width // 128), 1).astype(jnp.bfloat16)
+        copies[2].wait()
         re = samples_ref[0] * good
+        right[:, :width] = re
+        left[:, width:] = -re
+        copies[3].wait()
         im = samples_ref[1] * good
-        right[:, :width] = re
         right[:, width:] = im
         left[:, :width] = im
-        left[:, width:] = -re
 
     rows = pl.ds(pl.multiple_of(step * block, block), block)
     nt = (((1,), (1,)), ((), ()))
-    total = lax.dot_general(right[rows, :], right[...], nt, preferred_element_type=jnp.float32)
-    total += lax.dot_general(left[rows, :], right[...], nt, preferred_element_type=jnp.float32)
-    out_ref[...] = (total * scale).astype(jnp.bfloat16)
-
-def gram(samples, flags, all_time):
+    both = lax.dot_general(right[rows, :], right[...], nt, preferred_element_type=jnp.float32)
+    both += lax.dot_general(left[rows, :], right[...], nt, preferred_element_type=jnp.float32)
+    out_ref[...] = (both * scale).astype(jnp.bfloat16)
+
+
+def gram(cal_channel, samples, flags, all_time):
     _, feeds, width = samples.shape
     blocks = 4
+    bf16 = jnp.bfloat16
+    anywhere = pl.BlockSpec(memory_space=pl.ANY)
     return pl.pallas_call(
         functools.partial(gram_kernel, 1.0 / all_time),
         grid=(blocks,),
-        out_shape=jax.ShapeDtypeStruct((feeds, feeds), jnp.bfloat16),
-        in_specs=[pl.BlockSpec((2, feeds, width), lambda i: (0, 0, 0)), pl.BlockSpec((1, feeds), lambda i: (0, 0))],
-        out_specs=pl.BlockSpec((feeds // blocks, feeds), lambda i: (i, 0)),
-        scratch_shapes=[pltpu.VMEM((feeds, 2 * width), jnp.bfloat16)] * 2,
+        out_shape=(jax.ShapeDtypeStruct((feeds, feeds), bf16), jax.ShapeDtypeStruct((1,), jnp.int32)),
+        in_specs=[anywhere] * 3,
+        out_specs=(
+            pl.BlockSpec((feeds // blocks, feeds), lambda i: (i, 0)),
+            pl.BlockSpec(memory_space=pltpu.SMEM),
+        ),
+        scratch_shapes=[
+            pltpu.SMEM(cal_channel.shape, jnp.int32),
+            pltpu.VMEM(samples.shape, bf16),
+            pltpu.VMEM(flags.shape, jnp.int32),
+            pltpu.VMEM((feeds, 2 * width), bf16),
+            pltpu.VMEM((feeds, 2 * width), bf16),
+            pltpu.SemaphoreType.DMA((4,)),
+        ],
+        compiler_params=pltpu.CompilerParams(vmem_limit_bytes=56 << 20),
+        name="gram",
+    )(cal_channel, samples, flags)
+
+
+def fold_kernel(parts_ref, out_ref):
+    parts = parts_ref[...].astype(jnp.float32)
+    out_ref[...] = ((parts[0] + parts[1]) + (parts[2] + parts[3])).astype(jnp.bfloat16)
+
+
+def fold(parts):
+    _, rows, feeds = parts.shape
+    block = 64
+    return pl.pallas_call(
+        fold_kernel,
+        grid=(rows // block,),
+        out_shape=jax.ShapeDtypeStruct((rows, feeds), jnp.bfloat16),
+        in_specs=[pl.BlockSpec((4, block, feeds), lambda i: (0, i, 0))],
+        out_specs=pl.BlockSpec((block, feeds), lambda i: (i, 0)),
         compiler_params=pltpu.CompilerParams(vmem_limit_bytes=40 << 20),
-        name="gram",
-    )(samples, flags)
+        name="fold",
+    )(parts)
+
 
 def basis_rows(feeds):
     f = np.arange(feeds, dtype=np.float64)
@@ -67,7 +115,7 @@
     rows = mirror_ref.shape[0]
     for i in range(feeds // 256):
         mat_t[:, 256 * i:256 * (i + 1)] = own_ref[256 * i:256 * (i + 1), :].T
-    mirror_ref[...] = mat_t[pl.ds(pl.multiple_of(place_ref[0] * rows, rows), rows), :]
+    mirror_ref[...] = mat_t[pl.ds(pl.multiple_of(place_ref[0] * rows, rows), rows), :].astype(jnp.float32)
 
     def sweep(_, carry):
         qr, qi, _, _ = carry
@@ -106,7 +154,7 @@
     vm = pl.BlockSpec(memory_space=pltpu.VMEM)
     return pl.pallas_call(
         solve_kernel,
-        out_shape=(jax.ShapeDtypeStruct((4, feeds), jnp.float32), jax.ShapeDtypeStruct((rows, feeds), jnp.bfloat16)),
+        out_shape=(jax.ShapeDtypeStruct((4, feeds), jnp.float32), jax.ShapeDtypeStruct((rows, feeds), jnp.float32)),
         in_specs=[pl.BlockSpec(memory_space=pltpu.SMEM), vm, vm],
         out_specs=(vm, vm),
         scratch_shapes=[pltpu.VMEM((feeds, feeds), jnp.bfloat16)],
@@ -124,7 +172,8 @@
     solved = jnp.where(is_cal, kept_ref[...], swapped_ref[...])
     state = jnp.where(is_cal, swapped_ref[...], state_ref[...])
     gains = smoothing * state + (1.0 - smoothing) * solved
-    gains_ref[...] = gains
+    shift = (feeds - place * rows) % feeds
+    gains_ref[...] = pltpu.roll(gains, shift, 1)[:, :rows]
     power = jnp.sum(gains * gains, axis=0, keepdims=True)
     mean_power = total(power) / feeds
     scale = jnp.sqrt((mean_power + epsilon) / (power + mean_power + epsilon))
@@ -133,7 +182,7 @@
     down = jnp.concatenate([down] * (feeds // 128), 1)
     factor = 0.5 * (down * scale)
     mine = mine_ref[...]
-    mirror = mirror_ref[...].astype(jnp.float32)
+    mirror = mirror_ref[...]
     out_ref[0] = ((mine + mirror) * factor).astype(jnp.bfloat16)
     out_ref[1] = ((mine - mirror) * factor).astype(jnp.bfloat16)
 
@@ -144,7 +193,7 @@
     sm = pl.BlockSpec(memory_space=pltpu.SMEM)
     return pl.pallas_call(
         rescale_kernel,
-        out_shape=(jax.ShapeDtypeStruct((4, feeds), jnp.float32), jax.ShapeDtypeStruct((2, rows, feeds), jnp.bfloat16)),
+        out_shape=(jax.ShapeDtypeStruct((4, rows), jnp.float32), jax.ShapeDtypeStruct((2, rows, feeds), jnp.bfloat16)),
         in_specs=[sm, sm] + [vm] * 5,
         out_specs=(vm, vm),
         scratch_shapes=[pltpu.VMEM((feeds, 128), jnp.float32)],
@@ -174,54 +223,44 @@
     nx = nz = 4
     along_x, along_z = groups(nx, nz)
     rows = feeds // tm_count
-    thin = rows // nz
     tm = lax.axis_index("tm")
-    chan = lax.axis_index("chan")
     f32, bf16 = jnp.float32, jnp.bfloat16
     place = tm.reshape(1).astype(jnp.int32)
-    is_cal = cal_channel[chan // 2] == chan
-    samples, feed_flags, is_cal, place = lax.optimization_barrier((samples, feed_flags, is_cal, place))
-    cal = is_cal.reshape(1).astype(jnp.int32)
-
-    packed = gram(samples[0], feed_flags, samples.shape[3] * tm_count)
-    packed, own_state = lax.optimization_barrier((packed, gain_state[0].reshape(4, rows)))
-    part = exchange(packed.reshape(nx, nz * rows, feeds), along_x)
+    own_state = gain_state[0].reshape(4, rows)
     other_state = swap_cores(own_state)
-    part, other_state = lax.optimization_barrier((part, other_state))
-    part = jnp.sum(part.astype(f32), axis=0).astype(bf16)
-    part = exchange(part.reshape(nz, rows, feeds), along_z)
-    part, states = lax.optimization_barrier((part, jnp.concatenate([own_state, other_state], 0)))
-    mine = jnp.sum(part.astype(f32), axis=0)
-    sent = mine.astype(bf16)
-
-    def with_cal(_):
-        got = exchange(jnp.broadcast_to(sent[None], (nz, rows, feeds)), along_z)
+    packed, cal = gram(cal_channel, samples[0], feed_flags, samples.shape[3] * tm_count)
+    packed, cal, own_state, other_state = lax.optimization_barrier((packed, cal, own_state, other_state))
+    is_cal = cal[0] > 0
+
+    def with_cal():
+        part = fold(exchange(packed.reshape(nx, nz * rows, feeds), along_x))
+        mine = jnp.sum(exchange(part.reshape(nz, rows, feeds), along_z).astype(f32), axis=0)
+        got = exchange(jnp.broadcast_to(mine.astype(bf16)[None], (nz, rows, feeds)), along_z)
         got = exchange(jnp.broadcast_to(got.reshape(1, nz * rows, feeds), (nx, nz * rows, feeds)), along_x)
         solved, mirror = solve(place, got.reshape(feeds, feeds), rows)
-        return solved, jnp.zeros((4, feeds), f32), mirror
-
-    def without(_):
+        return solved, jnp.zeros((4, feeds), f32), mine, mirror
+
+    def without():
+        states = jnp.concatenate([own_state, other_state], 0)
         high = states.astype(bf16)
         low = (states - high.astype(f32)).astype(bf16)
-        halves = jnp.concatenate([high, low], 0)
-        halves = jnp.broadcast_to(jnp.pad(halves, ((0, 0), (0, feeds - rows)))[None], (nz, 16, feeds))
-        mirror = sent.reshape(rows, nx, nz, rows).transpose(2, 0, 1, 3)
-        mirror = mirror.reshape(nz, 4, thin, nx * rows).transpose(0, 2, 1, 3).reshape(nz, thin, feeds)
-        got = exchange(jnp.concatenate([mirror, halves], 1), along_z)
-        halves = got[:, thin:, :rows].transpose(1, 0, 2).reshape(16, nz * rows)
-        halves = jnp.broadcast_to(jnp.pad(halves, ((0, 0), (0, feeds - nz * rows)))[None], (nx, 16, feeds))
-        mirror = got[:, :thin].reshape(nz, thin, 4, nx * rows).transpose(0, 2, 1, 3).reshape(nz * rows, nx * rows)
-        mirror = mirror.T.reshape(nx, 4, thin, nz * rows).transpose(0, 2, 1, 3).reshape(nx, thin, feeds)
-        got = exchange(jnp.concatenate([mirror, halves], 1), along_x)
-        halves = got[:, thin:, : nz * rows].transpose(1, 0, 2).reshape(16, feeds).astype(f32)
-        both = halves[:8] + halves[8:]
-        mirror = got[:, :thin].reshape(nx, thin, 4, nz * rows).transpose(2, 1, 0, 3).reshape(rows, feeds)
-        return both[4:], both[:4], mirror
-
-    kept, held, mirror = lax.cond(is_cal, with_cal, without, None)
+        halves = jnp.broadcast_to(jnp.concatenate([high, low], 0)[None], (nx, 16, rows))
+        halves = exchange(halves, along_x).transpose(1, 0, 2).reshape(16, nx * rows)
+        halves, late = lax.optimization_barrier((halves, packed))
+        part = fold(exchange(late.reshape(nx, nz * rows, feeds), along_x)).reshape(nz, rows, feeds)
+        halves = jnp.pad(halves, ((0, 0), (0, feeds - nx * rows)))
+        part = jnp.concatenate([part, jnp.broadcast_to(halves[None], (nz, 16, feeds))], 1)
+        got = exchange(part, along_z)
+        mine = jnp.sum(got[:, :rows].astype(f32), axis=0)
+        mirror = exchange(mine.astype(bf16).T.reshape(tm_count, rows, rows), None)
+        mirror = mirror.transpose(1, 0, 2).reshape(rows, feeds).astype(f32)
+        halves = got[:, rows:, : nx * rows].astype(f32).reshape(nz, 2, 8, nx, rows)
+        states = (halves[:, 0] + halves[:, 1]).transpose(1, 2, 0, 3).reshape(8, feeds)
+        return states[4:], states[:4], mine, mirror
+
+    kept, held, mine, mirror = lax.cond(is_cal, with_cal, without)
     gains, calibrated = rescale(place, cal, kept, swap_cores(kept), held, mine, mirror)
-    gains_now = lax.dynamic_slice_in_dim(gains, tm * rows, rows, 1).reshape(1, 2, 2, rows)
-    return (calibrated.transpose(1, 0, 2)[None], gains_now)
+    return (calibrated.transpose(1, 0, 2)[None], gains.reshape(1, 2, 2, rows))
 
 
 def solution(mesh):

time: 146 us -> 135 us (0.925)
  blocking collectives: 27.2 us -> 50.5 us
  waiting for transfers between devices: 49.3 us -> 32.5 us
  starting transfers between devices: 55 us -> 39 us
  local copies, waits for them, and re-layouts: 5.84 us -> 3.35 us
  Pallas kernels: 4.45 us -> 6.15 us
    all_to_all x2, blocking collectives: 27.2 us -> 50.5 us  [exchange(): return lax.all_to_all(value, 'tm', 0, 0, axis_index_groups=which)]
    all_to_all x2, waiting for transfers between devices: 47.7 us -> 31.6 us  [exchange(): return lax.all_to_all(value, 'tm', 0, 0, axis_index_groups=which)]
    all_to_all x2, starting transfers between devices: 18.9 us -> 7.85 us  [exchange(): return lax.all_to_all(value, 'tm', 0, 0, axis_index_groups=which)]
    ppermute x2, starting transfers between devices: 36 us -> 31.2 us  [swap_cores(): return lax.ppermute(value, 'chan', [(i, i ^ 1) for i in range(count)])]
    unnamed x7 -> x1, local copies, waits for them, and re-layouts: 2.88 us -> 0.97 us
    dynamic_slice x2 -> x0, local copies, waits for them, and re-layouts: 1.89 us -> none  [the longest x1 1.24 us: on_device(): is_cal = cal_channel[chan // 2] == chan]
  transfers between devices with their start and end apart: 4 -> 4, of which waited for: 4 -> 3; matrix products, arithmetic and copies ran while one was open for 0% -> 0% of each run, Pallas kernels for 0% -> 3%
where the time goes in v3:
time: 135 us
  blocking collectives  50.5 us (37%)
  starting transfers between devices  39 us (29%)
  waiting for transfers between devices  32.5 us (24%)
  Pallas kernels  6.15 us (5%)
  local copies, waits for them, and re-layouts  3.35 us (2%)
  other arithmetic  1.69 us (1%)
    all_to_all x2, blocking collectives, exchange(): return lax.all_to_all(value, 'tm', 0, 0, axis_index_groups=which)  50.5 us
    all_to_all x2, waiting for transfers between devices, exchange(): return lax.all_to_all(value, 'tm', 0, 0, axis_index_groups=which)  31.6 us
    ppermute x2, starting transfers between devices, swap_cores(): return lax.ppermute(value, 'chan', [(i, i ^ 1) for i in range(count)])  31.2 us
    all_to_all x2, starting transfers between devices, exchange(): return lax.all_to_all(value, 'tm', 0, 0, axis_index_groups=which)  7.85 us
    pallas_call x1, Pallas kernels, gram(): pl.pallas_call(functools.partial(gram_kernel, 1.0 / all_time), grid=(bloc...  4.38 us
  transfers between devices with their start and end apart: 4, of which 3 were waited for; matrix products, arithmetic and copies ran while one was open for 0% of the time, Pallas kernels for 3%

profile of v3, /device:TPU:25, one launch (start us, length us, event | category | flops | bytes accessed | tf_op | source)
XLA Modules:
  0.0 134.6 jit_solution(10626786506700870848)
XLA Ops:
  0.6 2.6 %collective-permute-start = (f32[4,64]{1,0:T(4,128)}, f32[4,64]{1,0:T(4,128)S(1)}, u32[]{:S(2)}, u32[]{:S(2)}) collective-permute-start(f32[4,64]{1,0:T(4,128)} %bitcast.34), channel_id=1, source_target_pairs={{0,16},{16,0},{32,48},{48,32},{64,80},{80,64},{96,112},{112,96},{1... | collective-permute-start | bytes 3080 | tf_op jit(solution)/shard_map/ppermute | solution.py:217
  3.2 4.4 %gram.1 = (bf16[1024,1024]{1,0:T(8,128)(2,1)S(1)}, s32[1]{0:T(128)}) custom-call(s32[16]{0:T(128)} %cal_hbm.1, bf16[2,1024,256]{2,1,0:T(8,128)(2,1)} %bitcast.32, s32[1,1024]{1,0:T(1,128)} %flags_hbm.1), custom_call_target="tpu_custom_call" | custom-call | tf_op jit(solution)/shard_map/gram/pallas_call | solution.py:57
  7.6 0.0 collective-permute-done
  8.3 94.7 %conditional.1 = (f32[4,1024]{1,0:T(4,128)S(1)}, f32[4,1024]{1,0:T(4,128)S(1)}, f32[64,1024]{1,0:T(8,128)S(1)}, f32[64,1024]{1,0:T(8,128)S(1)}) conditional(s32[]{:T(128)} %bitcast.16, (f32[4,64]{1,0:T(4,128)}, f32[4,64]{1,0:T(4,128)S(1)}, bf16[1024,1024]{1,0:T(8,128)(2,1)S(1)}) %tuple.31, (bf16[1024,1024]{1,0:T(8,128)(2,1)S(1)}, s32[1]{0:T(128)}, ...), branch_computations={%region_0.2_spmd, %region_2.4_spmd} | conditional | flops 1933824 | bytes 21999742 | solution.py:261
  8.3 0.0 copy-start.1
  8.3 0.7 fusion.1
  9.0 0.7 subtract_convert_fusion
  9.7 0.1 reshape.62
  9.8 8.3 %all_to_all.32 = bf16[4,2,512]{2,1,0:T(2,128)(2,1)S(1)} all-to-all(bf16[4,2,512]{2,1,0:T(2,128)(2,1)S(1)} %reshape.62), channel_id=1, replica_groups={{0,4,8,12},{1,5,9,13},{2,6,10,14},{3,7,11,15},{16,20,24,28},{17,21,25,2..., dimensions={0} | all-to-all | bytes 16384 | tf_op jit(solution)/shard_map/cond/branch_0_fun/all_to_all | solution.py:212
  18.1 0.1 reshape.63
  18.2 0.1 reshape.44
  18.3 0.0 copy-done.1
  18.3 3.6 %all-to-all-start.5 = ((bf16[4,256,1024]{2,1,0:T(8,128)(2,1)}), bf16[4,256,1024]{2,1,0:T(8,128)(2,1)S(1)}, u32[]{:S(2)}, u32[]{:S(2)}) async-start(bf16[4,256,1024]{2,1,0:T(8,128)(2,1)} %bitcast.28), calls=%async_computation.5 | async-start | bytes 4194304 | tf_op jit(solution)/shard_map/cond/branch_0_fun/all_to_all | solution.py:212
  21.9 17.5 %all-to-all-done.5.parts_ref = bf16[4,256,1024]{2,1,0:T(8,128)(2,1)S(1)} async-done(((bf16[4,256,1024]{2,1,0:T(8,128)(2,1)}), bf16[4,256,1024]{2,1,0:T(8,128)(2,1)S(1)}, u32[]{:S(2)}, u32[]{:S(2)}) %all-to-all-start.5) | async-done | bytes 2097184 | tf_op jit(solution)/shard_map/cond/branch_0_fun/all_to_all | solution.py:212
  39.5 0.5 fold.2
  40.0 42.2 %all_to_all.33 = bf16[4,80,1024]{2,1,0:T(8,128)(2,1)S(1)} all-to-all(bf16[4,80,1024]{2,1,0:T(8,128)(2,1)S(1)} %pad_maximum_fusion), channel_id=1, replica_groups={{0,1,2,3},{4,5,6,7},{8,9,10,11},{12,13,14,15},{16,17,18,19},{20,21,22,2..., dimensions={0} | all-to-all | bytes 1310720 | tf_op jit(solution)/shard_map/cond/branch_0_fun/all_to_all | solution.py:212
  82.2 0.1 reshape.58
  82.3 0.1 convert_reduce_fusion
  82.5 0.2 copy.30
  82.6 0.9 reshape.64
  83.5 4.2 %all-to-all-start.7 = ((bf16[16,2,2048]{2,1,0:T(2,128)(2,1)}), bf16[16,2,2048]{2,1,0:T(2,128)(2,1)S(1)}, u32[]{:S(2)}, u32[]{:S(2)}) async-start(bf16[16,2,2048]{2,1,0:T(2,128)(2,1)} %reshape.64), calls=%async_computation.7 | async-start | bytes 262144 | tf_op jit(solution)/shard_map/cond/branch_0_fun/all_to_all | solution.py:212
  87.8 0.1 fusion
  87.9 0.1 slice.20
  88.0 0.1 slice.22
  88.1 14.1 %all-to-all-done.7 = bf16[16,2,2048]{2,1,0:T(2,128)(2,1)S(1)} async-done(((bf16[16,2,2048]{2,1,0:T(2,128)(2,1)}), bf16[16,2,2048]{2,1,0:T(2,128)(2,1)S(1)}, u32[]{:S(2)}, u32[]{:S(2)}) %all-to-all-start.7) | async-done | bytes 131104 | tf_op jit(solution)/shard_map/cond/branch_0_fun/all_to_all | solution.py:212
  102.2 0.2 reshape.65
  102.4 0.3 copy.28
  102.8 0.2 reshape.59
  102.9 28.6 %collective-permute-start.1 = (f32[4,1024]{1,0:T(4,128)S(1)}, f32[4,1024]{1,0:T(4,128)S(1)}, u32[]{:S(2)}, u32[]{:S(2)}) collective-permute-start(f32[4,1024]{1,0:T(4,128)S(1)} %get-tuple-element.42.kept_ref), channel_id=1, source_target_pairs={{0,16},{16,0},{32,48},{48,32},{64,80},{80,64},{96,112},{112,96},{1... | collective-permute-start | bytes 49160 | tf_op jit(solution)/shard_map/ppermute | solution.py:217
  131.5 0.8 collective-permute-done.1.swapped_ref
  132.3 1.3 rescale.1
  133.6 1.0 copy.29
  (11 shorter events, 0.2 us)
Async XLA Ops:
  0.6 7.0 %collective-permute-start = (f32[4,64]{1,0:T(4,128)}, f32[4,64]{1,0:T(4,128)S(1)}, u32[]{:S(2)}, u32[]{:S(2)}) collective-permute-start(f32[4,64]{1,0:T(4,128)} %bitcast.34), channel_id=1, source_target_pairs={{0,16},{16,0},{32,48},{48,32},{64,80},{80,64},{96,112},{112,96},{1... | collective-permute-start | bytes 3080 | tf_op jit(solution)/shard_map/ppermute | solution.py:217
  8.3 10.0 %copy-start.1 = (bf16[1024,1024]{1,0:T(8,128)(2,1)}, bf16[1024,1024]{1,0:T(8,128)(2,1)S(1)}, u32[]{:S(2)}) copy-start(bf16[1024,1024]{1,0:T(8,128)(2,1)S(1)} %get-tuple-element.15) | copy-start | bytes 6291460 | tf_op jit(solution)/shard_map/cond
  18.3 21.2 %all-to-all-start.5 = ((bf16[4,256,1024]{2,1,0:T(8,128)(2,1)}), bf16[4,256,1024]{2,1,0:T(8,128)(2,1)S(1)}, u32[]{:S(2)}, u32[]{:S(2)}) async-start(bf16[4,256,1024]{2,1,0:T(8,128)(2,1)} %bitcast.28), calls=%async_computation.5 | async-start | bytes 4194304 | tf_op jit(solution)/shard_map/cond/branch_0_fun/all_to_all | solution.py:212
  83.5 18.6 %all-to-all-start.7 = ((bf16[16,2,2048]{2,1,0:T(2,128)(2,1)}), bf16[16,2,2048]{2,1,0:T(2,128)(2,1)S(1)}, u32[]{:S(2)}, u32[]{:S(2)}) async-start(bf16[16,2,2048]{2,1,0:T(2,128)(2,1)} %reshape.64), calls=%async_computation.7 | async-start | bytes 262144 | tf_op jit(solution)/shard_map/cond/branch_0_fun/all_to_all | solution.py:212
  102.9 29.4 %collective-permute-start.1 = (f32[4,1024]{1,0:T(4,128)S(1)}, f32[4,1024]{1,0:T(4,128)S(1)}, u32[]{:S(2)}, u32[]{:S(2)}) collective-permute-start(f32[4,1024]{1,0:T(4,128)S(1)} %get-tuple-element.42.kept_ref), channel_id=1, source_target_pairs={{0,16},{16,0},{32,48},{48,32},{64,80},{80,64},{96,112},{112,96},{1... | collective-permute-start | bytes 49160 | tf_op jit(solution)/shard_map/ppermute | solution.py:217

commit v4 on v3

--- a/solution.py
+++ b/solution.py
@@ -8,6 +8,7 @@
 from jax.sharding import PartitionSpec as P
 
 ITERS = 8
+FIRST = 16
 epsilon = 1e-06
 smoothing = 0.75
 
@@ -32,20 +33,19 @@
         is_cal_ref[0] = (cal_ref[chan // 2] == chan).astype(jnp.int32)
         copies[1].wait()
         good = jnp.broadcast_to(flags_ref[...].astype(jnp.float32), (128, feeds)).T
-        good = jnp.concatenate([good] * (width // 128), 1).astype(jnp.bfloat16)
+        good = jnp.concatenate([good] * (width // 128), 1)
         copies[2].wait()
-        re = samples_ref[0] * good
-        right[:, :width] = re
-        left[:, width:] = -re
+        re = samples_ref[0].astype(jnp.float32) * good
+        left[:, :width] = re.astype(jnp.bfloat16)
         copies[3].wait()
-        im = samples_ref[1] * good
-        right[:, width:] = im
-        left[:, :width] = im
+        im = samples_ref[1].astype(jnp.float32) * good
+        left[:, width:] = im.astype(jnp.bfloat16)
+        right[:, :width] = (re - im).astype(jnp.bfloat16)
+        right[:, width:] = (re + im).astype(jnp.bfloat16)
 
     rows = pl.ds(pl.multiple_of(step * block, block), block)
     nt = (((1,), (1,)), ((), ()))
-    both = lax.dot_general(right[rows, :], right[...], nt, preferred_element_type=jnp.float32)
-    both += lax.dot_general(left[rows, :], right[...], nt, preferred_element_type=jnp.float32)
+    both = lax.dot_general(left[rows, :], right[...], nt, preferred_element_type=jnp.float32)
     out_ref[...] = (both * scale).astype(jnp.bfloat16)
 
 
@@ -76,23 +76,30 @@
     )(cal_channel, samples, flags)
 
 
-def fold_kernel(parts_ref, out_ref):
-    parts = parts_ref[...].astype(jnp.float32)
-    out_ref[...] = ((parts[0] + parts[1]) + (parts[2] + parts[3])).astype(jnp.bfloat16)
-
-
-def fold(parts):
-    _, rows, feeds = parts.shape
-    block = 64
+def fold_kernel(*refs):
+    *part_refs, out_ref = refs
+    at = 0
+    for ref in part_refs:
+        rows = ref.shape[1]
+        for first in range(0, rows, 16):
+            parts = [ref[k, first:first + 16, :].astype(jnp.float32) for k in range(4)]
+            total_rows = (parts[0] + parts[1]) + (parts[2] + parts[3])
+            out_ref[at + first:at + first + 16, :] = total_rows.astype(jnp.bfloat16)
+        at += rows
+
+
+def fold(*pieces):
+    feeds = pieces[0].shape[2]
+    rows = sum(piece.shape[1] for piece in pieces)
+    vm = pl.BlockSpec(memory_space=pltpu.VMEM)
     return pl.pallas_call(
         fold_kernel,
-        grid=(rows // block,),
         out_shape=jax.ShapeDtypeStruct((rows, feeds), jnp.bfloat16),
-        in_specs=[pl.BlockSpec((4, block, feeds), lambda i: (0, i, 0))],
-        out_specs=pl.BlockSpec((block, feeds), lambda i: (i, 0)),
+        in_specs=[vm] * len(pieces),
+        out_specs=vm,
         compiler_params=pltpu.CompilerParams(vmem_limit_bytes=40 << 20),
         name="fold",
-    )(parts)
+    )(*pieces)
 
 
 def basis_rows(feeds):
@@ -133,14 +140,18 @@
         n1 = total(one_r * one_r + one_i * one_i)
         cr = total(one_r * two_r + one_i * two_i)
         ci = total(one_r * two_i - one_i * two_r)
-        first = jnp.sqrt(epsilon + n1)
-        cr = cr / first
-        ci = ci / first
-        rest_r = two_r - (one_r * cr - one_i * ci) / first
-        rest_i = two_i - (one_r * ci + one_i * cr) / first
-        second = jnp.sqrt(epsilon + total(rest_r * rest_r + rest_i * rest_i))
-        qr = jnp.concatenate([one_r / first, rest_r / second], 0)
-        qi = jnp.concatenate([one_i / first, rest_i / second], 0)
+        square = epsilon + n1
+        inverse = lax.rsqrt(square)
+        first = square * inverse
+        cr = cr / square
+        ci = ci / square
+        rest_r = two_r - (one_r * cr - one_i * ci)
+        rest_i = two_i - (one_r * ci + one_i * cr)
+        square_two = epsilon + total(rest_r * rest_r + rest_i * rest_i)
+        inverse_two = lax.rsqrt(square_two)
+        second = square_two * inverse_two
+        qr = jnp.concatenate([one_r * inverse, rest_r * inverse_two], 0)
+        qi = jnp.concatenate([one_i * inverse, rest_i * inverse_two], 0)
         return qr, qi, first, second
 
     one = jnp.ones((1, 1), jnp.float32)
@@ -164,7 +175,7 @@
 
 
 def rescale_kernel(place_ref, cal_ref, kept_ref, swapped_ref, state_ref, mine_ref, mirror_ref,
-                   gains_ref, out_ref, turned):
+                   gains_ref, out_ref):
     feeds = mine_ref.shape[1]
     rows = mine_ref.shape[0]
     place = place_ref[0]
@@ -177,14 +188,13 @@
     power = jnp.sum(gains * gains, axis=0, keepdims=True)
     mean_power = total(power) / feeds
     scale = jnp.sqrt((mean_power + epsilon) / (power + mean_power + epsilon))
-    turned[...] = jnp.broadcast_to(scale, (128, feeds)).T
-    down = turned[pl.ds(pl.multiple_of(place * rows, rows), rows), :]
+    down = jnp.broadcast_to(pltpu.roll(scale, shift, 1)[:, :128], (128, 128)).T[:rows]
     down = jnp.concatenate([down] * (feeds // 128), 1)
     factor = 0.5 * (down * scale)
     mine = mine_ref[...]
     mirror = mirror_ref[...]
-    out_ref[0] = ((mine + mirror) * factor).astype(jnp.bfloat16)
-    out_ref[1] = ((mine - mirror) * factor).astype(jnp.bfloat16)
+    out_ref[:, 0, :] = ((mine + mirror) * factor).astype(jnp.bfloat16)
+    out_ref[:, 1, :] = ((mine - mirror) * factor).astype(jnp.bfloat16)
 
 
 def rescale(place, cal, kept, swapped, state, mine, mirror):
@@ -193,10 +203,9 @@
     sm = pl.BlockSpec(memory_space=pltpu.SMEM)
     return pl.pallas_call(
         rescale_kernel,
-        out_shape=(jax.ShapeDtypeStruct((4, rows), jnp.float32), jax.ShapeDtypeStruct((2, rows, feeds), jnp.bfloat16)),
+        out_shape=(jax.ShapeDtypeStruct((4, rows), jnp.float32), jax.ShapeDtypeStruct((rows, 2, feeds), jnp.bfloat16)),
         in_specs=[sm, sm] + [vm] * 5,
         out_specs=(vm, vm),
-        scratch_shapes=[pltpu.VMEM((feeds, 128), jnp.float32)],
         compiler_params=pltpu.CompilerParams(vmem_limit_bytes=40 << 20),
         name="rescale",
     )(place, cal, kept, swapped, state, mine, mirror)
@@ -241,26 +250,25 @@
         return solved, jnp.zeros((4, feeds), f32), mine, mirror
 
     def without():
+        blocks = packed.reshape(nx, nz * rows, feeds)
+        lead = exchange(blocks[:, :FIRST], along_x)
+        lead, trail = lax.optimization_barrier((lead, blocks[:, FIRST:]))
+        part = fold(lead, exchange(trail, along_x))
+        mine = jnp.sum(exchange(part.reshape(nz, rows, feeds), along_z).astype(f32), axis=0)
         states = jnp.concatenate([own_state, other_state], 0)
         high = states.astype(bf16)
         low = (states - high.astype(f32)).astype(bf16)
-        halves = jnp.broadcast_to(jnp.concatenate([high, low], 0)[None], (nx, 16, rows))
-        halves = exchange(halves, along_x).transpose(1, 0, 2).reshape(16, nx * rows)
-        halves, late = lax.optimization_barrier((halves, packed))
-        part = fold(exchange(late.reshape(nx, nz * rows, feeds), along_x)).reshape(nz, rows, feeds)
-        halves = jnp.pad(halves, ((0, 0), (0, feeds - nx * rows)))
-        part = jnp.concatenate([part, jnp.broadcast_to(halves[None], (nz, 16, feeds))], 1)
-        got = exchange(part, along_z)
-        mine = jnp.sum(got[:, :rows].astype(f32), axis=0)
-        mirror = exchange(mine.astype(bf16).T.reshape(tm_count, rows, rows), None)
-        mirror = mirror.transpose(1, 0, 2).reshape(rows, feeds).astype(f32)
-        halves = got[:, rows:, : nx * rows].astype(f32).reshape(nz, 2, 8, nx, rows)
-        states = (halves[:, 0] + halves[:, 1]).transpose(1, 2, 0, 3).reshape(8, feeds)
+        halves = jnp.broadcast_to(jnp.concatenate([high, low], 0)[None], (tm_count, 16, rows))
+        mirror = mine.astype(bf16).T.reshape(tm_count, rows, rows)
+        got = exchange(jnp.concatenate([mirror, halves], 1), None)
+        got = got.transpose(1, 0, 2).reshape(rows + 16, feeds).astype(f32)
+        mirror, halves = got[:rows], got[rows:]
+        states = halves[:8] + halves[8:]
         return states[4:], states[:4], mine, mirror
 
     kept, held, mine, mirror = lax.cond(is_cal, with_cal, without)
     gains, calibrated = rescale(place, cal, kept, swap_cores(kept), held, mine, mirror)
-    return (calibrated.transpose(1, 0, 2)[None], gains.reshape(1, 2, 2, rows))
+    return (calibrated[None], gains.reshape(1, 2, 2, rows))
 
 
 def solution(mesh):

time: 135 us -> 137 us (1.015)
  the two profiles are of different devices: /device:TPU:25 before, /device:TPU:49 now
where the time goes in v4:
time: 137 us
  blocking collectives  52.3 us (38%)
  starting transfers between devices  48.3 us (35%)
  waiting for transfers between devices  24.7 us (18%)
  Pallas kernels  6.32 us (5%)
  local copies, waits for them, and re-layouts  3.29 us (2%)
    all_to_all x2, blocking collectives, exchange(): return lax.all_to_all(value, 'tm', 0, 0, axis_index_groups=which)  52.3 us
    ppermute x2, starting transfers between devices, swap_cores(): return lax.ppermute(value, 'chan', [(i, i ^ 1) for i in range(count)])  30.4 us
    all_to_all x2, waiting for transfers between devices, exchange(): return lax.all_to_all(value, 'tm', 0, 0, axis_index_groups=which)  23.9 us
    all_to_all x2, starting transfers between devices, exchange(): return lax.all_to_all(value, 'tm', 0, 0, axis_index_groups=which)  17.9 us
    pallas_call x1, Pallas kernels, gram(): pl.pallas_call(functools.partial(gram_kernel, 1.0 / all_time), grid=(bloc...  3.55 us
  transfers between devices with their start and end apart: 4, of which 3 were waited for; matrix products, arithmetic and copies ran while one was open for 1% of the time, Pallas kernels for 3%

profile of v4, /device:TPU:49, one launch (start us, length us, event | category | flops | bytes accessed | tf_op | source)
XLA Modules:
  0.0 137.0 jit_solution(187453353200126439)
XLA Ops:
  0.6 2.6 %collective-permute-start = (f32[4,64]{1,0:T(4,128)}, f32[4,64]{1,0:T(4,128)S(1)}, u32[]{:S(2)}, u32[]{:S(2)}) collective-permute-start(f32[4,64]{1,0:T(4,128)} %bitcast.32), channel_id=1, source_target_pairs={{0,16},{16,0},{32,48},{48,32},{64,80},{80,64},{96,112},{112,96},{1... | collective-permute-start | bytes 3080 | tf_op jit(solution)/shard_map/ppermute | solution.py:226
  3.2 3.5 %gram.1 = (bf16[1024,1024]{1,0:T(8,128)(2,1)S(1)}, s32[1]{0:T(128)}) custom-call(s32[16]{0:T(128)} %cal_hbm.1, bf16[2,1024,256]{2,1,0:T(8,128)(2,1)} %bitcast.31, s32[1,1024]{1,0:T(1,128)} %flags_hbm.1), custom_call_target="tpu_custom_call" | custom-call | tf_op jit(solution)/shard_map/gram/pallas_call | solution.py:57
  6.8 0.0 collective-permute-done
  7.4 99.2 %conditional.1 = (f32[64,1024]{1,0:T(8,128)S(1)}, f32[4,1024]{1,0:T(4,128)S(1)}, f32[4,1024]{1,0:T(4,128)S(1)}, f32[64,1024]{1,0:T(8,128)S(1)}) conditional(s32[]{:T(128)} %bitcast.14, (bf16[1024,1024]{1,0:T(8,128)(2,1)S(1)}, f32[4,64]{1,0:T(4,128)}, f32[4,64]{1,0:T(4,128)S(1)}) %tuple.36, (bf16[1024,1024]{1,0:T(8,128)(2,1)S(1)}, s32[1]{0:T(128)}, ...), branch_computations={%region_0.0_spmd, %region_2.0_spmd} | conditional | flops 950784 | bytes 17121400 | solution.py:269
  7.4 0.7 slice.35
  8.1 4.0 %all-to-all-start.4 = ((bf16[4,16,1024]{2,1,0:T(8,128)(2,1)}), bf16[4,16,1024]{2,1,0:T(8,128)(2,1)S(1)}, u32[]{:S(2)}, u32[]{:S(2)}) async-start(bf16[4,16,1024]{2,1,0:T(8,128)(2,1)} %slice.35), calls=%async_computation.4 | async-start | bytes 262144 | tf_op jit(solution)/shard_map/cond/branch_0_fun/all_to_all | solution.py:221
  12.1 1.4 %slice.36 = bf16[4,240,1024]{2,1,0:T(8,128)(2,1)} slice(bf16[4,256,1024]{2,1,0:T(8,128)(2,1)S(1)} %bitcast.26), slice={[0:4], [16:256], [0:1024]} | slice | bytes 3932160 | tf_op jit(solution)/shard_map/cond/branch_0_fun/slice | solution.py:255
  13.6 4.2 %all-to-all-done.4.refs_0_ = bf16[4,16,1024]{2,1,0:T(8,128)(2,1)S(1)} async-done(((bf16[4,16,1024]{2,1,0:T(8,128)(2,1)}), bf16[4,16,1024]{2,1,0:T(8,128)(2,1)S(1)}, u32[]{:S(2)}, u32[]{:S(2)}) %all-to-all-start.4) | async-done | bytes 131104 | tf_op jit(solution)/shard_map/cond/branch_0_fun/all_to_all | solution.py:221
  17.7 20.9 %all_to_all.32.refs_1_ = bf16[4,240,1024]{2,1,0:T(8,128)(2,1)S(1)} all-to-all(bf16[4,240,1024]{2,1,0:T(8,128)(2,1)} %slice.36), channel_id=1, replica_groups={{0,4,8,12},{1,5,9,13},{2,6,10,14},{3,7,11,15},{16,20,24,28},{17,21,25,2..., dimensions={0} | all-to-all | bytes 3932160 | tf_op jit(solution)/shard_map/cond/branch_0_fun/all_to_all | solution.py:221
  38.6 0.0 copy-start.3
  38.6 1.0 fold.2
  39.6 13.9 %all-to-all-start.6 = ((bf16[4,64,1024]{2,1,0:T(8,128)(2,1)}), bf16[4,64,1024]{2,1,0:T(8,128)(2,1)S(1)}, u32[]{:S(2)}, u32[]{:S(2)}) async-start(bf16[4,64,1024]{2,1,0:T(8,128)(2,1)} %bitcast.1), calls=%async_computation.6 | async-start | bytes 1048576 | tf_op jit(solution)/shard_map/cond/branch_0_fun/all_to_all | solution.py:221
  53.6 0.0 copy-done.3
  53.6 0.1 copy.25
  53.7 19.7 %all-to-all-done.6 = bf16[4,64,1024]{2,1,0:T(8,128)(2,1)S(1)} async-done(((bf16[4,64,1024]{2,1,0:T(8,128)(2,1)}), bf16[4,64,1024]{2,1,0:T(8,128)(2,1)S(1)}, u32[]{:S(2)}, u32[]{:S(2)}) %all-to-all-start.6) | async-done | bytes 524320 | tf_op jit(solution)/shard_map/cond/branch_0_fun/all_to_all | solution.py:221
  73.4 0.1 convert_reduce_fusion
  73.5 0.2 reshape.40
  73.8 0.1 pad_maximum_fusion
  73.9 0.1 copy.26
  74.0 31.4 %all_to_all.33 = bf16[16,80,64]{1,2,0:T(8,128)(2,1)S(1)} all-to-all(bf16[16,80,64]{1,2,0:T(8,128)(2,1)S(1)} %copy.26), channel_id=1, replica_groups=mesh['chan'=32,'tm'=16] {'tm'}, dimensions={0} | all-to-all | bytes 327680 | tf_op jit(solution)/shard_map/cond/branch_0_fun/all_to_all | solution.py:221
  105.5 0.3 slice_add_fusion
  105.8 0.2 fusion.1
  106.1 0.2 copy.33
  106.2 0.2 copy.35
  106.4 0.2 copy.37
  106.6 27.8 %collective-permute-start.1 = (f32[4,1024]{1,0:T(4,128)S(1)}, f32[4,1024]{1,0:T(4,128)S(1)}, u32[]{:S(2)}, u32[]{:S(2)}) collective-permute-start(f32[4,1024]{1,0:T(4,128)S(1)} %get-tuple-element.65.kept_ref), channel_id=1, source_target_pairs={{0,16},{16,0},{32,48},{48,32},{64,80},{80,64},{96,112},{112,96},{1... | collective-permute-start | bytes 49160 | tf_op jit(solution)/shard_map/ppermute | solution.py:226
  134.5 0.8 collective-permute-done.1.swapped_ref
  135.3 1.7 %rescale.1 = (f32[4,64]{1,0:T(4,128)}, bf16[64,2,1024]{2,1,0:T(2,128)(2,1)}) custom-call(s32[1]{0:T(128)} %bitcast.11.place_ref, s32[1]{0:T(128)} %get-tuple-element.38.cal_ref, f32[4,1024]{1,0:T(4,128)S(1)} %get-tuple-element.65.kept_ref, f32[4,1024]{1,0:T(4,128)S(1)} %collective-permute-done.1.swapped_ref, f32[4,1024]{1,0:T(4,128)S(1)} %get-tuple-element.66.state_ref, ...), custom_call_target="tpu_custom_call" | custom-call | tf_op jit(solution)/shard_map/rescale/pallas_call | solution.py:204
  (6 shorter events, 0.1 us)
Async XLA Ops:
  0.6 6.2 %collective-permute-start = (f32[4,64]{1,0:T(4,128)}, f32[4,64]{1,0:T(4,128)S(1)}, u32[]{:S(2)}, u32[]{:S(2)}) collective-permute-start(f32[4,64]{1,0:T(4,128)} %bitcast.32), channel_id=1, source_target_pairs={{0,16},{16,0},{32,48},{48,32},{64,80},{80,64},{96,112},{112,96},{1... | collective-permute-start | bytes 3080 | tf_op jit(solution)/shard_map/ppermute | solution.py:226
  8.1 9.6 %all-to-all-start.4 = ((bf16[4,16,1024]{2,1,0:T(8,128)(2,1)}), bf16[4,16,1024]{2,1,0:T(8,128)(2,1)S(1)}, u32[]{:S(2)}, u32[]{:S(2)}) async-start(bf16[4,16,1024]{2,1,0:T(8,128)(2,1)} %slice.35), calls=%async_computation.4 | async-start | bytes 262144 | tf_op jit(solution)/shard_map/cond/branch_0_fun/all_to_all | solution.py:221
  38.6 15.0 %copy-start.3 = (f32[4,64]{1,0:T(4,128)S(1)}, f32[4,64]{1,0:T(4,128)}, u32[]{:S(2)}) copy-start(f32[4,64]{1,0:T(4,128)} %get-tuple-element.15) | copy-start | bytes 3076 | tf_op jit(solution)/shard_map/cond
  39.6 33.8 %all-to-all-start.6 = ((bf16[4,64,1024]{2,1,0:T(8,128)(2,1)}), bf16[4,64,1024]{2,1,0:T(8,128)(2,1)S(1)}, u32[]{:S(2)}, u32[]{:S(2)}) async-start(bf16[4,64,1024]{2,1,0:T(8,128)(2,1)} %bitcast.1), calls=%async_computation.6 | async-start | bytes 1048576 | tf_op jit(solution)/shard_map/cond/branch_0_fun/all_to_all | solution.py:221
  106.6 28.6 %collective-permute-start.1 = (f32[4,1024]{1,0:T(4,128)S(1)}, f32[4,1024]{1,0:T(4,128)S(1)}, u32[]{:S(2)}, u32[]{:S(2)}) collective-permute-start(f32[4,1024]{1,0:T(4,128)S(1)} %get-tuple-element.65.kept_ref), channel_id=1, source_target_pairs={{0,16},{16,0},{32,48},{48,32},{64,80},{80,64},{96,112},{112,96},{1... | collective-permute-start | bytes 49160 | tf_op jit(solution)/shard_map/ppermute | solution.py:226

commit v5 on v4

--- a/solution.py
+++ b/solution.py
@@ -55,7 +55,7 @@
     bf16 = jnp.bfloat16
     anywhere = pl.BlockSpec(memory_space=pl.ANY)
     return pl.pallas_call(
-        functools.partial(gram_kernel, 1.0 / all_time),
+        functools.partial(gram_kernel, 0.5 / all_time),
         grid=(blocks,),
         out_shape=(jax.ShapeDtypeStruct((feeds, feeds), bf16), jax.ShapeDtypeStruct((1,), jnp.int32)),
         in_specs=[anywhere] * 3,
@@ -133,8 +133,8 @@
         with_m = jnp.dot(left, own_ref[...], preferred_element_type=jnp.float32)
         with_t = (with_t[0:4] + with_t[4:8]) + with_t[8:12]
         with_m = (with_m[0:4] + with_m[4:8]) + with_m[8:12]
-        zr = 0.5 * (with_t[2:4] + with_m[0:2])
-        zi = 0.5 * (with_t[0:2] - with_m[2:4])
+        zr = with_t[2:4] + with_m[0:2]
+        zi = with_t[0:2] - with_m[2:4]
         one_r, two_r = zr[0:1], zr[1:2]
         one_i, two_i = zi[0:1], zi[1:2]
         n1 = total(one_r * one_r + one_i * one_i)
@@ -190,7 +190,7 @@
     scale = jnp.sqrt((mean_power + epsilon) / (power + mean_power + epsilon))
     down = jnp.broadcast_to(pltpu.roll(scale, shift, 1)[:, :128], (128, 128)).T[:rows]
     down = jnp.concatenate([down] * (feeds // 128), 1)
-    factor = 0.5 * (down * scale)
+    factor = down * scale
     mine = mine_ref[...]
     mirror = mirror_ref[...]
     out_ref[:, 0, :] = ((mine + mirror) * factor).astype(jnp.bfloat16)
@@ -240,6 +240,7 @@
     packed, cal = gram(cal_channel, samples[0], feed_flags, samples.shape[3] * tm_count)
     packed, cal, own_state, other_state = lax.optimization_barrier((packed, cal, own_state, other_state))
     is_cal = cal[0] > 0
+    odd = lax.axis_index("chan") % 2 == 1
 
     def with_cal():
         part = fold(exchange(packed.reshape(nx, nz * rows, feeds), along_x))
@@ -249,9 +250,18 @@
         solved, mirror = solve(place, got.reshape(feeds, feeds), rows)
         return solved, jnp.zeros((4, feeds), f32), mine, mirror
 
+    def around_x(value):
+        here = tm // nz
+        got = [lax.dynamic_index_in_dim(value, here, 0, keepdims=False)]
+        for shift in range(1, nx):
+            pairs = [(i, (i + shift * nz) % tm_count) for i in range(tm_count)]
+            block = lax.dynamic_index_in_dim(value, (here + shift) % nx, 0, keepdims=False)
+            got.append(lax.ppermute(block, "tm", pairs))
+        return jnp.stack(got)
+
     def without():
         blocks = packed.reshape(nx, nz * rows, feeds)
-        lead = exchange(blocks[:, :FIRST], along_x)
+        lead = lax.cond(odd, around_x, lambda value: exchange(value, along_x), blocks[:, :FIRST])
         lead, trail = lax.optimization_barrier((lead, blocks[:, FIRST:]))
         part = fold(lead, exchange(trail, along_x))
         mine = jnp.sum(exchange(part.reshape(nz, rows, feeds), along_z).astype(f32), axis=0)

time: 137 us -> 122 us (0.89)
  the two profiles are of different devices: /device:TPU:49 before, /device:TPU:25 now
where the time goes in v5:
time: 122 us; the launch traced here: 121 us
  starting transfers between devices  45 us (37%)
  blocking collectives  38.3 us (31%)
  waiting for transfers between devices  26.4 us (22%)
  Pallas kernels  6.32 us (5%)
  local copies, waits for them, and re-layouts  2.66 us (2%)
  between operations  1.31 us (1%)
    all_to_all x2, blocking collectives, exchange(): return lax.all_to_all(value, 'tm', 0, 0, axis_index_groups=which)  38.3 us
    all_to_all x1, waiting for transfers between devices, exchange(): return lax.all_to_all(value, 'tm', 0, 0, axis_index_groups=which)  23.3 us
    ppermute x2, starting transfers between devices, swap_cores(): return lax.ppermute(value, 'chan', [(i, i ^ 1) for i in range(count)])  19.4 us
    all_to_all x1, starting transfers between devices, exchange(): return lax.all_to_all(value, 'tm', 0, 0, axis_index_groups=which)  15.1 us
    ppermute x3, starting transfers between devices, around_x(): got.append(lax.ppermute(block, 'tm', pairs))  10.5 us
    pallas_call x1, Pallas kernels, gram(): pl.pallas_call(functools.partial(gram_kernel, 0.5 / all_time), grid=(bloc...  3.55 us
  transfers between devices with their start and end apart: 6, of which 3 were waited for; matrix products, arithmetic and copies ran while one was open for 0% of the time, Pallas kernels for 3%

profile of v5, /device:TPU:25, one launch (start us, length us, event | category | flops | bytes accessed | tf_op | source)
XLA Modules:
  0.0 120.8 jit_solution(6432570022326317756)
XLA Ops:
  0.6 2.6 %collective-permute-start.3 = (f32[4,64]{1,0:T(4,128)}, f32[4,64]{1,0:T(4,128)S(1)}, u32[]{:S(2)}, u32[]{:S(2)}) collective-permute-start(f32[4,64]{1,0:T(4,128)} %bitcast.44), channel_id=1, source_target_pairs={{0,16},{16,0},{32,48},{48,32},{64,80},{80,64},{96,112},{112,96},{1... | collective-permute-start | bytes 3080 | tf_op jit(solution)/shard_map/ppermute | solution.py:226
  3.2 3.5 %gram.1 = (bf16[1024,1024]{1,0:T(8,128)(2,1)S(1)}, s32[1]{0:T(128)}) custom-call(s32[16]{0:T(128)} %cal_hbm.1, bf16[2,1024,256]{2,1,0:T(8,128)(2,1)} %bitcast.40, s32[1,1024]{1,0:T(1,128)} %flags_hbm.1), custom_call_target="tpu_custom_call" | custom-call | tf_op jit(solution)/shard_map/gram/pallas_call | solution.py:57
  6.8 0.0 collective-permute-done.3
  7.4 94.1 %conditional.2 = (f32[64,1024]{1,0:T(8,128)S(1)}, f32[4,1024]{1,0:T(4,128)S(1)}, f32[4,1024]{1,0:T(4,128)S(1)}, f32[64,1024]{1,0:T(8,128)S(1)}) conditional(s32[]{:T(128)} %bitcast.20, (s32[]{:T(128)}, bf16[1024,1024]{1,0:T(8,128)(2,1)S(1)}, s32[]{:T(128)}, f32[4,64]{1,0:T(4,128)}, f32[4,64]{1,0:T(4,128)S(1)}) %tuple.57, ...), branch_computations={%region_0.4_spmd, %region_4.6_spmd} | conditional | flops 1147468 | bytes 17121400 | solution.py:279
  7.5 1.5 %slice.39 = bf16[4,240,1024]{2,1,0:T(8,128)(2,1)} slice(bf16[4,256,1024]{2,1,0:T(8,128)(2,1)S(1)} %bitcast.35), slice={[0:4], [16:256], [0:1024]} | slice | bytes 3932160 | tf_op jit(solution)/shard_map/cond/branch_0_fun/slice | solution.py:265
  8.9 12.9 %conditional = (bf16[4,16,1024]{2,1,0:T(8,128)(2,1)S(1)}) conditional(s32[]{:T(128)} %convert_element_type.32, bf16[4,16,1024]{2,1,0:T(8,128)(2,1)S(1)} %slice.38, (s32[]{:T(128)}, bf16[4,16,1024]{2,1,0:T(8,128)(2,1)S(1)}) %tuple.25), branch_computations={%region_1.1_spmd, %region_2.2_spmd} | conditional | flops 196671 | bytes 918297 | solution.py:264
  8.9 3.1 %collective-permute-start = (bf16[16,1024]{1,0:T(8,128)(2,1)S(1)}, bf16[16,1024]{1,0:T(8,128)(2,1)S(1)}, u32[]{:S(2)}, u32[]{:S(2)}) collective-permute-start(bf16[16,1024]{1,0:T(8,128)(2,1)S(1)} %get-tuple-element.114), channel_id=1, source_target_pairs={{0,4},{1,5},{2,6},{3,7},{4,8},{5,9},{6,10},{7,11},{8,12},{9,13},{1... | collective-permute-start | bytes 98312 | tf_op jit(solution)/shard_map/cond/branch_0_fun/cond/branch_1_fun/ppermute | solution.py:259
  12.1 4.4 %collective-permute-start.1 = (bf16[16,1024]{1,0:T(8,128)(2,1)S(1)}, bf16[16,1024]{1,0:T(8,128)(2,1)S(1)}, u32[]{:S(2)}, u32[]{:S(2)}) collective-permute-start(bf16[16,1024]{1,0:T(8,128)(2,1)S(1)} %get-tuple-element.113), channel_id=1, source_target_pairs={{0,8},{1,9},{2,10},{3,11},{4,12},{5,13},{6,14},{7,15},{8,0},{9,1},... | collective-permute-start | bytes 98312 | tf_op jit(solution)/shard_map/cond/branch_0_fun/cond/branch_1_fun/ppermute | solution.py:259
  16.4 3.1 %collective-permute-start.2 = (bf16[16,1024]{1,0:T(8,128)(2,1)S(1)}, bf16[16,1024]{1,0:T(8,128)(2,1)S(1)}, u32[]{:S(2)}, u32[]{:S(2)}) collective-permute-start(bf16[16,1024]{1,0:T(8,128)(2,1)S(1)} %get-tuple-element.112), channel_id=1, source_target_pairs={{0,12},{1,13},{2,14},{3,15},{4,0},{5,1},{6,2},{7,3},{8,4},{9,5},{1... | collective-permute-start | bytes 98312 | tf_op jit(solution)/shard_map/cond/branch_0_fun/cond/branch_1_fun/ppermute | solution.py:259
  19.5 0.0 collective-permute-done
  19.5 0.0 collective-permute-done.1
  19.5 2.3 %collective-permute-done.2 = bf16[16,1024]{1,0:T(8,128)(2,1)S(1)} collective-permute-done((bf16[16,1024]{1,0:T(8,128)(2,1)S(1)}, bf16[16,1024]{1,0:T(8,128)(2,1)S(1)}, u32[]{:S(2)}, u32[]{:S(2)}) %collective-permute-start.2) | collective-permute-done | bytes 32800 | tf_op jit(solution)/shard_map/cond/branch_0_fun/cond/branch_1_fun/ppermute | solution.py:259
  21.8 18.7 %all_to_all.33.refs_1_ = bf16[4,240,1024]{2,1,0:T(8,128)(2,1)S(1)} all-to-all(bf16[4,240,1024]{2,1,0:T(8,128)(2,1)} %slice.39), channel_id=1, replica_groups={{0,4,8,12},{1,5,9,13},{2,6,10,14},{3,7,11,15},{16,20,24,28},{17,21,25,2..., dimensions={0} | all-to-all | bytes 3932160 | tf_op jit(solution)/shard_map/cond/branch_0_fun/all_to_all | solution.py:221
  40.5 0.0 copy-start.3
  40.5 1.0 fold.2
  41.5 15.1 %all-to-all-start.6 = ((bf16[4,64,1024]{2,1,0:T(8,128)(2,1)}), bf16[4,64,1024]{2,1,0:T(8,128)(2,1)S(1)}, u32[]{:S(2)}, u32[]{:S(2)}) async-start(bf16[4,64,1024]{2,1,0:T(8,128)(2,1)} %bitcast.7), calls=%async_computation.6 | async-start | bytes 1048576 | tf_op jit(solution)/shard_map/cond/branch_0_fun/all_to_all | solution.py:221
  56.6 0.0 copy-done.3
  56.7 0.1 copy.25
  56.8 23.3 %all-to-all-done.6 = bf16[4,64,1024]{2,1,0:T(8,128)(2,1)S(1)} async-done(((bf16[4,64,1024]{2,1,0:T(8,128)(2,1)}), bf16[4,64,1024]{2,1,0:T(8,128)(2,1)S(1)}, u32[]{:S(2)}, u32[]{:S(2)}) %all-to-all-start.6) | async-done | bytes 524320 | tf_op jit(solution)/shard_map/cond/branch_0_fun/all_to_all | solution.py:221
  80.1 0.1 convert_reduce_fusion
  80.2 0.2 reshape.40
  80.4 0.1 pad_maximum_fusion.1
  80.6 0.1 copy.26
  80.7 19.7 %all_to_all.34 = bf16[16,80,64]{1,2,0:T(8,128)(2,1)S(1)} all-to-all(bf16[16,80,64]{1,2,0:T(8,128)(2,1)S(1)} %copy.26), channel_id=1, replica_groups=mesh['chan'=32,'tm'=16] {'tm'}, dimensions={0} | all-to-all | bytes 327680 | tf_op jit(solution)/shard_map/cond/branch_0_fun/all_to_all | solution.py:221
  100.4 0.3 slice_add_fusion
  100.7 0.2 fusion.1
  100.9 0.2 copy.33
  101.1 0.2 copy.35
  101.3 0.2 copy.37
  101.5 16.8 %collective-permute-start.4 = (f32[4,1024]{1,0:T(4,128)S(1)}, f32[4,1024]{1,0:T(4,128)S(1)}, u32[]{:S(2)}, u32[]{:S(2)}) collective-permute-start(f32[4,1024]{1,0:T(4,128)S(1)} %get-tuple-element.108.kept_ref), channel_id=1, source_target_pairs={{0,16},{16,0},{32,48},{48,32},{64,80},{80,64},{96,112},{112,96},{1... | collective-permute-start | bytes 49160 | tf_op jit(solution)/shard_map/ppermute | solution.py:226
  118.3 0.8 collective-permute-done.4.swapped_ref
  119.1 1.7 %rescale.1 = (f32[4,64]{1,0:T(4,128)}, bf16[64,2,1024]{2,1,0:T(2,128)(2,1)}) custom-call(s32[1]{0:T(128)} %bitcast.17.place_ref, s32[1]{0:T(128)} %get-tuple-element.79.cal_ref, f32[4,1024]{1,0:T(4,128)S(1)} %get-tuple-element.108.kept_ref, f32[4,1024]{1,0:T(4,128)S(1)} %collective-permute-done.4.swapped_ref, f32[4,1024]{1,0:T(4,128)S(1)} %get-tuple-element.109.state_ref, ...), custom_call_target="tpu_custom_call" | custom-call | tf_op jit(solution)/shard_map/rescale/pallas_call | solution.py:204
  (9 shorter events, 0.2 us)
Async XLA Ops:
  0.6 6.2 %collective-permute-start.3 = (f32[4,64]{1,0:T(4,128)}, f32[4,64]{1,0:T(4,128)S(1)}, u32[]{:S(2)}, u32[]{:S(2)}) collective-permute-start(f32[4,64]{1,0:T(4,128)} %bitcast.44), channel_id=1, source_target_pairs={{0,16},{16,0},{32,48},{48,32},{64,80},{80,64},{96,112},{112,96},{1... | collective-permute-start | bytes 3080 | tf_op jit(solution)/shard_map/ppermute | solution.py:226
  8.9 10.6 %collective-permute-start = (bf16[16,1024]{1,0:T(8,128)(2,1)S(1)}, bf16[16,1024]{1,0:T(8,128)(2,1)S(1)}, u32[]{:S(2)}, u32[]{:S(2)}) collective-permute-start(bf16[16,1024]{1,0:T(8,128)(2,1)S(1)} %get-tuple-element.114), channel_id=1, source_target_pairs={{0,4},{1,5},{2,6},{3,7},{4,8},{5,9},{6,10},{7,11},{8,12},{9,13},{1... | collective-permute-start | bytes 98312 | tf_op jit(solution)/shard_map/cond/branch_0_fun/cond/branch_1_fun/ppermute | solution.py:259
  12.1 7.4 %collective-permute-start.1 = (bf16[16,1024]{1,0:T(8,128)(2,1)S(1)}, bf16[16,1024]{1,0:T(8,128)(2,1)S(1)}, u32[]{:S(2)}, u32[]{:S(2)}) collective-permute-start(bf16[16,1024]{1,0:T(8,128)(2,1)S(1)} %get-tuple-element.113), channel_id=1, source_target_pairs={{0,8},{1,9},{2,10},{3,11},{4,12},{5,13},{6,14},{7,15},{8,0},{9,1},... | collective-permute-start | bytes 98312 | tf_op jit(solution)/shard_map/cond/branch_0_fun/cond/branch_1_fun/ppermute | solution.py:259
  16.4 5.4 %collective-permute-start.2 = (bf16[16,1024]{1,0:T(8,128)(2,1)S(1)}, bf16[16,1024]{1,0:T(8,128)(2,1)S(1)}, u32[]{:S(2)}, u32[]{:S(2)}) collective-permute-start(bf16[16,1024]{1,0:T(8,128)(2,1)S(1)} %get-tuple-element.112), channel_id=1, source_target_pairs={{0,12},{1,13},{2,14},{3,15},{4,0},{5,1},{6,2},{7,3},{8,4},{9,5},{1... | collective-permute-start | bytes 98312 | tf_op jit(solution)/shard_map/cond/branch_0_fun/cond/branch_1_fun/ppermute | solution.py:259
  40.5 16.1 %copy-start.3 = (f32[4,64]{1,0:T(4,128)S(1)}, f32[4,64]{1,0:T(4,128)}, u32[]{:S(2)}) copy-start(f32[4,64]{1,0:T(4,128)} %get-tuple-element.56) | copy-start | bytes 3076 | tf_op jit(solution)/shard_map/cond
  41.5 38.6 %all-to-all-start.6 = ((bf16[4,64,1024]{2,1,0:T(8,128)(2,1)}), bf16[4,64,1024]{2,1,0:T(8,128)(2,1)S(1)}, u32[]{:S(2)}, u32[]{:S(2)}) async-start(bf16[4,64,1024]{2,1,0:T(8,128)(2,1)} %bitcast.7), calls=%async_computation.6 | async-start | bytes 1048576 | tf_op jit(solution)/shard_map/cond/branch_0_fun/all_to_all | solution.py:221
  101.5 17.6 %collective-permute-start.4 = (f32[4,1024]{1,0:T(4,128)S(1)}, f32[4,1024]{1,0:T(4,128)S(1)}, u32[]{:S(2)}, u32[]{:S(2)}) collective-permute-start(f32[4,1024]{1,0:T(4,128)S(1)} %get-tuple-element.108.kept_ref), channel_id=1, source_target_pairs={{0,16},{16,0},{32,48},{48,32},{64,80},{80,64},{96,112},{112,96},{1... | collective-permute-start | bytes 49160 | tf_op jit(solution)/shard_map/ppermute | solution.py:226

commit v6 on v5

--- a/solution.py
+++ b/solution.py
@@ -9,6 +9,7 @@
 
 ITERS = 8
 FIRST = 16
+SHIFTS = (2, 1, 3)
 epsilon = 1e-06
 smoothing = 0.75
 
@@ -76,30 +77,33 @@
     )(cal_channel, samples, flags)
 
 
-def fold_kernel(*refs):
-    *part_refs, out_ref = refs
+def fold_kernel(count, *refs):
+    part_refs, out_refs = refs[:count], refs[count:]
     at = 0
     for ref in part_refs:
         rows = ref.shape[1]
         for first in range(0, rows, 16):
             parts = [ref[k, first:first + 16, :].astype(jnp.float32) for k in range(4)]
             total_rows = (parts[0] + parts[1]) + (parts[2] + parts[3])
-            out_ref[at + first:at + first + 16, :] = total_rows.astype(jnp.bfloat16)
+            for out_ref in out_refs:
+                out_ref[at + first:at + first + 16, :] = total_rows.astype(jnp.bfloat16)
         at += rows
 
 
-def fold(*pieces):
+def fold(*pieces, copies=1):
     feeds = pieces[0].shape[2]
     rows = sum(piece.shape[1] for piece in pieces)
     vm = pl.BlockSpec(memory_space=pltpu.VMEM)
-    return pl.pallas_call(
-        fold_kernel,
-        out_shape=jax.ShapeDtypeStruct((rows, feeds), jnp.bfloat16),
+    out = jax.ShapeDtypeStruct((rows, feeds), jnp.bfloat16)
+    out = pl.pallas_call(
+        functools.partial(fold_kernel, len(pieces)),
+        out_shape=[out] * copies,
         in_specs=[vm] * len(pieces),
-        out_specs=vm,
+        out_specs=[vm] * copies,
         compiler_params=pltpu.CompilerParams(vmem_limit_bytes=40 << 20),
         name="fold",
     )(*pieces)
+    return out[0] if copies == 1 else out
 
 
 def basis_rows(feeds):
@@ -117,12 +121,18 @@
 def total(v):
     return jnp.sum(v, axis=1, keepdims=True)
 
-def solve_kernel(place_ref, own_ref, basis_ref, solved_ref, mirror_ref, mat_t):
+def solve_kernel(place_ref, *refs):
+    *slab_refs, basis_ref, solved_ref, mirror_ref, own_ref, mat_t = refs
     feeds = own_ref.shape[0]
     rows = mirror_ref.shape[0]
-    for i in range(feeds // 256):
-        mat_t[:, 256 * i:256 * (i + 1)] = own_ref[256 * i:256 * (i + 1), :].T
-    mirror_ref[...] = mat_t[pl.ds(pl.multiple_of(place_ref[0] * rows, rows), rows), :].astype(jnp.float32)
+    size = slab_refs[0].shape[0]
+    here = place_ref[0] * rows // size
+    for shift, ref in zip((0,) + SHIFTS, slab_refs):
+        first = (here + len(slab_refs) - shift) % len(slab_refs)
+        own_ref[pl.ds(pl.multiple_of(first * size, size), size), :] = ref[...]
+    for i in range(feeds // size):
+        mat_t[:, size * i:size * (i + 1)] = own_ref[size * i:size * (i + 1), :].T
+    mirror_ref[...] = mat_t[pl.ds(pl.multiple_of(place_ref[0] * rows, rows), rows), :]
 
     def sweep(_, carry):
         qr, qi, _, _ = carry
@@ -160,26 +170,31 @@
     solved_ref[...] = jnp.concatenate([qr * weights, qi * weights], 0)
 
 
-def solve(place, own, rows):
-    feeds = own.shape[1]
+def solve(place, slabs, rows):
+    feeds = slabs[0].shape[1]
     vm = pl.BlockSpec(memory_space=pltpu.VMEM)
     return pl.pallas_call(
         solve_kernel,
-        out_shape=(jax.ShapeDtypeStruct((4, feeds), jnp.float32), jax.ShapeDtypeStruct((rows, feeds), jnp.float32)),
-        in_specs=[pl.BlockSpec(memory_space=pltpu.SMEM), vm, vm],
+        out_shape=(jax.ShapeDtypeStruct((4, feeds), jnp.float32), jax.ShapeDtypeStruct((rows, feeds), jnp.bfloat16)),
+        in_specs=[pl.BlockSpec(memory_space=pltpu.SMEM)] + [vm] * (len(slabs) + 1),
         out_specs=(vm, vm),
-        scratch_shapes=[pltpu.VMEM((feeds, feeds), jnp.bfloat16)],
+        scratch_shapes=[pltpu.VMEM((feeds, feeds), jnp.bfloat16)] * 2,
         compiler_params=pltpu.CompilerParams(vmem_limit_bytes=40 << 20),
         name="solve",
-    )(place, own, jnp.asarray(basis_rows(feeds)))
-
-
-def rescale_kernel(place_ref, cal_ref, kept_ref, swapped_ref, state_ref, mine_ref, mirror_ref,
-                   gains_ref, out_ref):
-    feeds = mine_ref.shape[1]
-    rows = mine_ref.shape[0]
+    )(place, *slabs, jnp.asarray(basis_rows(feeds)))
+
+
+def rescale_kernel(place_ref, cal_ref, kept_ref, swapped_ref, state_ref, mine_hbm, mirror_hbm,
+                   gains_ref, out_ref, mine_ref, mirror_ref, sems):
+    rows, feeds = mine_ref.shape
     place = place_ref[0]
     is_cal = cal_ref[0] > 0
+    copies = [
+        pltpu.make_async_copy(mine_hbm, mine_ref, sems.at[0]),
+        pltpu.make_async_copy(mirror_hbm, mirror_ref, sems.at[1]),
+    ]
+    for copy in copies:
+        copy.start()
     solved = jnp.where(is_cal, kept_ref[...], swapped_ref[...])
     state = jnp.where(is_cal, swapped_ref[...], state_ref[...])
     gains = smoothing * state + (1.0 - smoothing) * solved
@@ -191,8 +206,10 @@
     down = jnp.broadcast_to(pltpu.roll(scale, shift, 1)[:, :128], (128, 128)).T[:rows]
     down = jnp.concatenate([down] * (feeds // 128), 1)
     factor = down * scale
-    mine = mine_ref[...]
-    mirror = mirror_ref[...]
+    for copy in copies:
+        copy.wait()
+    mine = mine_ref[...].astype(jnp.float32)
+    mirror = mirror_ref[...].astype(jnp.float32)
     out_ref[:, 0, :] = ((mine + mirror) * factor).astype(jnp.bfloat16)
     out_ref[:, 1, :] = ((mine - mirror) * factor).astype(jnp.bfloat16)
 
@@ -204,8 +221,9 @@
     return pl.pallas_call(
         rescale_kernel,
         out_shape=(jax.ShapeDtypeStruct((4, rows), jnp.float32), jax.ShapeDtypeStruct((rows, 2, feeds), jnp.bfloat16)),
-        in_specs=[sm, sm] + [vm] * 5,
+        in_specs=[sm, sm] + [vm] * 3 + [pl.BlockSpec(memory_space=pl.ANY)] * 2,
         out_specs=(vm, vm),
+        scratch_shapes=[pltpu.VMEM((rows, feeds), jnp.bfloat16)] * 2 + [pltpu.SemaphoreType.DMA((2,))],
         compiler_params=pltpu.CompilerParams(vmem_limit_bytes=40 << 20),
         name="rescale",
     )(place, cal, kept, swapped, state, mine, mirror)
@@ -242,21 +260,23 @@
     is_cal = cal[0] > 0
     odd = lax.axis_index("chan") % 2 == 1
 
+    def shifted_x(block, shift):
+        return lax.ppermute(block, "tm", [(i, (i + shift * nz) % tm_count) for i in range(tm_count)])
+
     def with_cal():
         part = fold(exchange(packed.reshape(nx, nz * rows, feeds), along_x))
-        mine = jnp.sum(exchange(part.reshape(nz, rows, feeds), along_z).astype(f32), axis=0)
-        got = exchange(jnp.broadcast_to(mine.astype(bf16)[None], (nz, rows, feeds)), along_z)
-        got = exchange(jnp.broadcast_to(got.reshape(1, nz * rows, feeds), (nx, nz * rows, feeds)), along_x)
-        solved, mirror = solve(place, got.reshape(feeds, feeds), rows)
+        sent, mine = fold(exchange(part.reshape(nz, rows, feeds), along_z), copies=2)
+        got = exchange(jnp.broadcast_to(sent[None], (nz, rows, feeds)), along_z)
+        slab = got.reshape(nz * rows, feeds)
+        slabs = [shifted_x(slab, shift) for shift in SHIFTS]
+        solved, mirror = solve(place, [slab] + slabs, rows)
         return solved, jnp.zeros((4, feeds), f32), mine, mirror
 
     def around_x(value):
         here = tm // nz
         got = [lax.dynamic_index_in_dim(value, here, 0, keepdims=False)]
         for shift in range(1, nx):
-            pairs = [(i, (i + shift * nz) % tm_count) for i in range(tm_count)]
-            block = lax.dynamic_index_in_dim(value, (here + shift) % nx, 0, keepdims=False)
-            got.append(lax.ppermute(block, "tm", pairs))
+            got.append(shifted_x(lax.dynamic_index_in_dim(value, (here + shift) % nx, 0, keepdims=False), shift))
         return jnp.stack(got)
 
     def without():
@@ -264,15 +284,15 @@
         lead = lax.cond(odd, around_x, lambda value: exchange(value, along_x), blocks[:, :FIRST])
         lead, trail = lax.optimization_barrier((lead, blocks[:, FIRST:]))
         part = fold(lead, exchange(trail, along_x))
-        mine = jnp.sum(exchange(part.reshape(nz, rows, feeds), along_z).astype(f32), axis=0)
+        mine = fold(exchange(part.reshape(nz, rows, feeds), along_z))
         states = jnp.concatenate([own_state, other_state], 0)
         high = states.astype(bf16)
         low = (states - high.astype(f32)).astype(bf16)
         halves = jnp.broadcast_to(jnp.concatenate([high, low], 0)[None], (tm_count, 16, rows))
-        mirror = mine.astype(bf16).T.reshape(tm_count, rows, rows)
+        mirror = mine.T.reshape(tm_count, rows, rows)
         got = exchange(jnp.concatenate([mirror, halves], 1), None)
-        got = got.transpose(1, 0, 2).reshape(rows + 16, feeds).astype(f32)
-        mirror, halves = got[:rows], got[rows:]
+        got = got.transpose(1, 0, 2).reshape(rows + 16, feeds)
+        mirror, halves = got[:rows], got[rows:].astype(f32)
         states = halves[:8] + halves[8:]
         return states[4:], states[:4], mine, mirror
 

time: 122 us -> 121 us (level)
  blocking collectives: 38.3 us -> 45.3 us
  starting transfers between devices: 45 us -> 40.5 us
  waiting for transfers between devices: 26.4 us -> 22.5 us
    all_to_all x2, blocking collectives: 38.3 us -> 45.3 us  [exchange(): return lax.all_to_all(value, 'tm', 0, 0, axis_index_groups=which)]
    all_to_all x1, waiting for transfers between devices: 23.3 us -> 17.1 us  [exchange(): return lax.all_to_all(value, 'tm', 0, 0, axis_index_groups=which)]
    ppermute x2, starting transfers between devices: 19.4 us -> 16.1 us  [swap_cores(): return lax.ppermute(value, 'chan', [(i, i ^ 1) for i in range(count)])]
    ppermute x3, waiting for transfers between devices: 2.28 us -> 4.59 us  [shifted_x(): lax.ppermute(block, 'tm', [(i, (i + shift * nz) % tm_count) for i in rang...]
  transfers between devices with their start and end apart: 6 -> 6, of which waited for: 3 -> 4; matrix products, arithmetic and copies ran while one was open for 0% -> 0% of each run, Pallas kernels for 3% -> 3%
where the time goes in v6:
time: 121 us; the launch traced here: 120 us
  blocking collectives  45.3 us (37%)
  starting transfers between devices  40.5 us (33%)
  waiting for transfers between devices  22.5 us (19%)
  Pallas kernels  6.77 us (6%)
  local copies, waits for them, and re-layouts  2.61 us (2%)
  between operations  1.24 us (1%)
    all_to_all x2, blocking collectives, exchange(): return lax.all_to_all(value, 'tm', 0, 0, axis_index_groups=which)  45.3 us
    all_to_all x1, waiting for transfers between devices, exchange(): return lax.all_to_all(value, 'tm', 0, 0, axis_index_groups=which)  17.1 us
    ppermute x2, starting transfers between devices, swap_cores(): return lax.ppermute(value, 'chan', [(i, i ^ 1) for i in range(count)])  16.1 us
    all_to_all x1, starting transfers between devices, exchange(): return lax.all_to_all(value, 'tm', 0, 0, axis_index_groups=which)  15.1 us
    ppermute x3, starting transfers between devices, shifted_x(): lax.ppermute(block, 'tm', [(i, (i + shift * nz) % tm_count) for i in rang...  9.33 us
    ppermute x3, waiting for transfers between devices, shifted_x(): lax.ppermute(block, 'tm', [(i, (i + shift * nz) % tm_count) for i in rang...  4.59 us
    pallas_call x1, Pallas kernels, gram(): pl.pallas_call(functools.partial(gram_kernel, 0.5 / all_time), grid=(bloc...  3.55 us
  transfers between devices with their start and end apart: 6, of which 4 were waited for; matrix products, arithmetic and copies ran while one was open for 0% of the time, Pallas kernels for 3%

profile of v6, /device:TPU:25, one launch (start us, length us, event | category | flops | bytes accessed | tf_op | source)
XLA Modules:
  0.0 119.6 jit_solution(10777619557376644571)
XLA Ops:
  0.6 2.6 %collective-permute-start.6 = (f32[4,64]{1,0:T(4,128)}, f32[4,64]{1,0:T(4,128)S(1)}, u32[]{:S(2)}, u32[]{:S(2)}) collective-permute-start(f32[4,64]{1,0:T(4,128)} %bitcast.45), channel_id=1, source_target_pairs={{0,16},{16,0},{32,48},{48,32},{64,80},{80,64},{96,112},{112,96},{1... | collective-permute-start | bytes 3080 | tf_op jit(solution)/shard_map/ppermute | solution.py:244
  3.2 3.5 %gram.1 = (bf16[1024,1024]{1,0:T(8,128)(2,1)S(1)}, s32[1]{0:T(128)}) custom-call(s32[16]{0:T(128)} %cal_hbm.1, bf16[2,1024,256]{2,1,0:T(8,128)(2,1)} %bitcast.41, s32[1,1024]{1,0:T(1,128)} %flags_hbm.1), custom_call_target="tpu_custom_call" | custom-call | tf_op jit(solution)/shard_map/gram/pallas_call | solution.py:58
  6.8 0.0 collective-permute-done.6
  7.4 95.8 %conditional.2 = (bf16[64,1024]{1,0:T(8,128)(2,1)S(1)}, f32[4,1024]{1,0:T(4,128)S(1)}, f32[4,1024]{1,0:T(4,128)S(1)}, bf16[64,1024]{1,0:T(8,128)(2,1)S(1)}) conditional(s32[]{:T(128)} %bitcast.19, (s32[]{:T(128)}, bf16[1024,1024]{1,0:T(8,128)(2,1)S(1)}, s32[]{:T(128)}, f32[4,64]{1,0:T(4,128)}, f32[4,64]{1,0:T(4,128)S(1)}) %tuple.55, ...), branch_computations={%region_0.3_spmd, %region_3.4_spmd} | conditional | flops 557644 | bytes 13320376 | solution.py:299
  7.4 1.5 %slice.40 = bf16[4,240,1024]{2,1,0:T(8,128)(2,1)} slice(bf16[4,256,1024]{2,1,0:T(8,128)(2,1)S(1)} %bitcast.34), slice={[0:4], [16:256], [0:1024]} | slice | bytes 3932160 | tf_op jit(solution)/shard_map/cond/branch_0_fun/slice | solution.py:285
  8.8 14.0 %conditional = (bf16[4,16,1024]{2,1,0:T(8,128)(2,1)S(1)}) conditional(s32[]{:T(128)} %convert_element_type.15, bf16[4,16,1024]{2,1,0:T(8,128)(2,1)S(1)} %slice.39, (s32[]{:T(128)}, bf16[4,16,1024]{2,1,0:T(8,128)(2,1)S(1)}) %tuple.25), branch_computations={%region_1.1_spmd, %region_2.2_spmd} | conditional | flops 196671 | bytes 918297 | solution.py:284
  8.9 4.4 %collective-permute-start.5 = (bf16[16,1024]{1,0:T(8,128)(2,1)S(1)}, bf16[16,1024]{1,0:T(8,128)(2,1)S(1)}, u32[]{:S(2)}, u32[]{:S(2)}) collective-permute-start(bf16[16,1024]{1,0:T(8,128)(2,1)S(1)} %get-tuple-element.106), channel_id=1, source_target_pairs={{0,12},{1,13},{2,14},{3,15},{4,0},{5,1},{6,2},{7,3},{8,4},{9,5},{1... | collective-permute-start | bytes 98312 | tf_op jit(solution)/shard_map/cond/branch_0_fun/cond/branch_1_fun/ppermute | solution.py:264
  13.3 2.4 %collective-permute-start.4 = (bf16[16,1024]{1,0:T(8,128)(2,1)S(1)}, bf16[16,1024]{1,0:T(8,128)(2,1)S(1)}, u32[]{:S(2)}, u32[]{:S(2)}) collective-permute-start(bf16[16,1024]{1,0:T(8,128)(2,1)S(1)} %get-tuple-element.107), channel_id=1, source_target_pairs={{0,8},{1,9},{2,10},{3,11},{4,12},{5,13},{6,14},{7,15},{8,0},{9,1},... | collective-permute-start | bytes 98312 | tf_op jit(solution)/shard_map/cond/branch_0_fun/cond/branch_1_fun/ppermute | solution.py:264
  15.7 2.5 %collective-permute-start.3 = (bf16[16,1024]{1,0:T(8,128)(2,1)S(1)}, bf16[16,1024]{1,0:T(8,128)(2,1)S(1)}, u32[]{:S(2)}, u32[]{:S(2)}) collective-permute-start(bf16[16,1024]{1,0:T(8,128)(2,1)S(1)} %get-tuple-element.108), channel_id=1, source_target_pairs={{0,4},{1,5},{2,6},{3,7},{4,8},{5,9},{6,10},{7,11},{8,12},{9,13},{1... | collective-permute-start | bytes 98312 | tf_op jit(solution)/shard_map/cond/branch_0_fun/cond/branch_1_fun/ppermute | solution.py:264
  18.2 0.0 collective-permute-done.5
  18.2 1.9 %collective-permute-done.4 = bf16[16,1024]{1,0:T(8,128)(2,1)S(1)} collective-permute-done((bf16[16,1024]{1,0:T(8,128)(2,1)S(1)}, bf16[16,1024]{1,0:T(8,128)(2,1)S(1)}, u32[]{:S(2)}, u32[]{:S(2)}) %collective-permute-start.4) | collective-permute-done | bytes 32800 | tf_op jit(solution)/shard_map/cond/branch_0_fun/cond/branch_1_fun/ppermute | solution.py:264
  20.1 2.7 %collective-permute-done.3 = bf16[16,1024]{1,0:T(8,128)(2,1)S(1)} collective-permute-done((bf16[16,1024]{1,0:T(8,128)(2,1)S(1)}, bf16[16,1024]{1,0:T(8,128)(2,1)S(1)}, u32[]{:S(2)}, u32[]{:S(2)}) %collective-permute-start.3) | collective-permute-done | bytes 32800 | tf_op jit(solution)/shard_map/cond/branch_0_fun/cond/branch_1_fun/ppermute | solution.py:264
  22.8 18.2 %all_to_all.29.refs_1_ = bf16[4,240,1024]{2,1,0:T(8,128)(2,1)S(1)} all-to-all(bf16[4,240,1024]{2,1,0:T(8,128)(2,1)} %slice.40), channel_id=1, replica_groups={{0,4,8,12},{1,5,9,13},{2,6,10,14},{3,7,11,15},{16,20,24,28},{17,21,25,2..., dimensions={0} | all-to-all | bytes 3932160 | tf_op jit(solution)/shard_map/cond/branch_0_fun/all_to_all | solution.py:239
  41.1 0.0 copy-start.1
  41.1 1.1 fold.4
  42.1 15.1 %all-to-all-start.5 = ((bf16[4,64,1024]{2,1,0:T(8,128)(2,1)}), bf16[4,64,1024]{2,1,0:T(8,128)(2,1)S(1)}, u32[]{:S(2)}, u32[]{:S(2)}) async-start(bf16[4,64,1024]{2,1,0:T(8,128)(2,1)} %bitcast.7), calls=%async_computation.5 | async-start | bytes 1048576 | tf_op jit(solution)/shard_map/cond/branch_0_fun/all_to_all | solution.py:239
  57.2 0.0 copy-done.1
  57.3 0.1 copy.17
  57.4 17.1 %all-to-all-done.5.refs_0_ = bf16[4,64,1024]{2,1,0:T(8,128)(2,1)S(1)} async-done(((bf16[4,64,1024]{2,1,0:T(8,128)(2,1)}), bf16[4,64,1024]{2,1,0:T(8,128)(2,1)S(1)}, u32[]{:S(2)}, u32[]{:S(2)}) %all-to-all-start.5) | async-done | bytes 524320 | tf_op jit(solution)/shard_map/cond/branch_0_fun/all_to_all | solution.py:239
  74.5 0.1 fold.5
  74.5 0.2 reshape.37
  74.7 0.1 copy.18
  74.8 0.2 pad_maximum_fusion.1
  75.0 27.1 %all_to_all.30 = bf16[16,80,64]{1,2,0:T(8,128)(2,1)S(1)} all-to-all(bf16[16,80,64]{1,2,0:T(8,128)(2,1)S(1)} %pad_maximum_fusion.1), channel_id=1, replica_groups=mesh['chan'=32,'tm'=16] {'tm'}, dimensions={0} | all-to-all | bytes 327680 | tf_op jit(solution)/shard_map/cond/branch_0_fun/all_to_all | solution.py:239
  102.1 0.1 slice_convert_fusion
  102.2 0.2 slice_add_fusion
  102.4 0.2 fusion.1
  102.6 0.2 copy.25
  102.8 0.2 copy.27
  103.0 0.1 copy.29
  103.2 13.5 %collective-permute-start.7 = (f32[4,1024]{1,0:T(4,128)S(1)}, f32[4,1024]{1,0:T(4,128)S(1)}, u32[]{:S(2)}, u32[]{:S(2)}) collective-permute-start(f32[4,1024]{1,0:T(4,128)S(1)} %get-tuple-element.102.kept_ref), channel_id=1, source_target_pairs={{0,16},{16,0},{32,48},{48,32},{64,80},{80,64},{96,112},{112,96},{1... | collective-permute-start | bytes 49160 | tf_op jit(solution)/shard_map/ppermute | solution.py:244
  116.7 0.8 collective-permute-done.7.swapped_ref
  117.5 2.1 %rescale.1 = (f32[4,64]{1,0:T(4,128)}, bf16[64,2,1024]{2,1,0:T(2,128)(2,1)}) custom-call(s32[1]{0:T(128)} %bitcast.16.place_ref, s32[1]{0:T(128)} %get-tuple-element.81.cal_ref, f32[4,1024]{1,0:T(4,128)S(1)} %get-tuple-element.102.kept_ref, f32[4,1024]{1,0:T(4,128)S(1)} %collective-permute-done.7.swapped_ref, f32[4,1024]{1,0:T(4,128)S(1)} %get-tuple-element.103.state_ref, ...), custom_call_target="tpu_custom_call" | custom-call | tf_op jit(solution)/shard_map/rescale/pallas_call | solution.py:221
  (7 shorter events, 0.1 us)
Async XLA Ops:
  0.6 6.2 %collective-permute-start.6 = (f32[4,64]{1,0:T(4,128)}, f32[4,64]{1,0:T(4,128)S(1)}, u32[]{:S(2)}, u32[]{:S(2)}) collective-permute-start(f32[4,64]{1,0:T(4,128)} %bitcast.45), channel_id=1, source_target_pairs={{0,16},{16,0},{32,48},{48,32},{64,80},{80,64},{96,112},{112,96},{1... | collective-permute-start | bytes 3080 | tf_op jit(solution)/shard_map/ppermute | solution.py:244
  8.9 9.4 %collective-permute-start.5 = (bf16[16,1024]{1,0:T(8,128)(2,1)S(1)}, bf16[16,1024]{1,0:T(8,128)(2,1)S(1)}, u32[]{:S(2)}, u32[]{:S(2)}) collective-permute-start(bf16[16,1024]{1,0:T(8,128)(2,1)S(1)} %get-tuple-element.106), channel_id=1, source_target_pairs={{0,12},{1,13},{2,14},{3,15},{4,0},{5,1},{6,2},{7,3},{8,4},{9,5},{1... | collective-permute-start | bytes 98312 | tf_op jit(solution)/shard_map/cond/branch_0_fun/cond/branch_1_fun/ppermute | solution.py:264
  13.3 6.9 %collective-permute-start.4 = (bf16[16,1024]{1,0:T(8,128)(2,1)S(1)}, bf16[16,1024]{1,0:T(8,128)(2,1)S(1)}, u32[]{:S(2)}, u32[]{:S(2)}) collective-permute-start(bf16[16,1024]{1,0:T(8,128)(2,1)S(1)} %get-tuple-element.107), channel_id=1, source_target_pairs={{0,8},{1,9},{2,10},{3,11},{4,12},{5,13},{6,14},{7,15},{8,0},{9,1},... | collective-permute-start | bytes 98312 | tf_op jit(solution)/shard_map/cond/branch_0_fun/cond/branch_1_fun/ppermute | solution.py:264
  15.7 7.1 %collective-permute-start.3 = (bf16[16,1024]{1,0:T(8,128)(2,1)S(1)}, bf16[16,1024]{1,0:T(8,128)(2,1)S(1)}, u32[]{:S(2)}, u32[]{:S(2)}) collective-permute-start(bf16[16,1024]{1,0:T(8,128)(2,1)S(1)} %get-tuple-element.108), channel_id=1, source_target_pairs={{0,4},{1,5},{2,6},{3,7},{4,8},{5,9},{6,10},{7,11},{8,12},{9,13},{1... | collective-permute-start | bytes 98312 | tf_op jit(solution)/shard_map/cond/branch_0_fun/cond/branch_1_fun/ppermute | solution.py:264
  41.1 16.2 %copy-start.1 = (f32[4,64]{1,0:T(4,128)S(1)}, f32[4,64]{1,0:T(4,128)}, u32[]{:S(2)}) copy-start(f32[4,64]{1,0:T(4,128)} %get-tuple-element.56) | copy-start | bytes 3076 | tf_op jit(solution)/shard_map/cond
  42.1 32.3 %all-to-all-start.5 = ((bf16[4,64,1024]{2,1,0:T(8,128)(2,1)}), bf16[4,64,1024]{2,1,0:T(8,128)(2,1)S(1)}, u32[]{:S(2)}, u32[]{:S(2)}) async-start(bf16[4,64,1024]{2,1,0:T(8,128)(2,1)} %bitcast.7), calls=%async_computation.5 | async-start | bytes 1048576 | tf_op jit(solution)/shard_map/cond/branch_0_fun/all_to_all | solution.py:239
  103.2 14.4 %collective-permute-start.7 = (f32[4,1024]{1,0:T(4,128)S(1)}, f32[4,1024]{1,0:T(4,128)S(1)}, u32[]{:S(2)}, u32[]{:S(2)}) collective-permute-start(f32[4,1024]{1,0:T(4,128)S(1)} %get-tuple-element.102.kept_ref), channel_id=1, source_target_pairs={{0,16},{16,0},{32,48},{48,32},{64,80},{80,64},{96,112},{112,96},{1... | collective-permute-start | bytes 49160 | tf_op jit(solution)/shard_map/ppermute | solution.py:244

commit v7 on v5

--- a/solution.py
+++ b/solution.py
@@ -15,54 +15,49 @@
 def gram_kernel(scale, cal_hbm, samples_hbm, flags_hbm, out_ref, is_cal_ref, cal_ref, samples_ref, flags_ref, left,
                 right, sems):
     feeds, width = samples_ref.shape[1:]
-    block = out_ref.shape[0]
-    step = pl.program_id(0)
-
-    @pl.when(step == 0)
-    def _():
-        copies = [
-            pltpu.make_async_copy(cal_hbm, cal_ref, sems.at[0]),
-            pltpu.make_async_copy(flags_hbm, flags_ref, sems.at[1]),
-            pltpu.make_async_copy(samples_hbm.at[0], samples_ref.at[0], sems.at[2]),
-            pltpu.make_async_copy(samples_hbm.at[1], samples_ref.at[1], sems.at[3]),
-        ]
-        for copy in copies:
-            copy.start()
-        copies[0].wait()
-        chan = lax.axis_index("chan")
-        is_cal_ref[0] = (cal_ref[chan // 2] == chan).astype(jnp.int32)
-        copies[1].wait()
-        good = jnp.broadcast_to(flags_ref[...].astype(jnp.float32), (128, feeds)).T
-        good = jnp.concatenate([good] * (width // 128), 1)
-        copies[2].wait()
-        re = samples_ref[0].astype(jnp.float32) * good
-        left[:, :width] = re.astype(jnp.bfloat16)
-        copies[3].wait()
-        im = samples_ref[1].astype(jnp.float32) * good
-        left[:, width:] = im.astype(jnp.bfloat16)
-        right[:, :width] = (re - im).astype(jnp.bfloat16)
-        right[:, width:] = (re + im).astype(jnp.bfloat16)
-
-    rows = pl.ds(pl.multiple_of(step * block, block), block)
-    nt = (((1,), (1,)), ((), ()))
-    both = lax.dot_general(left[rows, :], right[...], nt, preferred_element_type=jnp.float32)
-    out_ref[...] = (both * scale).astype(jnp.bfloat16)
+    block = feeds // 4
+    copies = [
+        pltpu.make_async_copy(cal_hbm, cal_ref, sems.at[0]),
+        pltpu.make_async_copy(flags_hbm, flags_ref, sems.at[1]),
+        pltpu.make_async_copy(samples_hbm.at[0], samples_ref.at[0], sems.at[2]),
+        pltpu.make_async_copy(samples_hbm.at[1], samples_ref.at[1], sems.at[3]),
+    ]
+    for copy in copies:
+        copy.start()
+    copies[0].wait()
+    chan = lax.axis_index("chan")
+    is_cal_ref[0] = (cal_ref[chan // 2] == chan).astype(jnp.int32)
+    copies[1].wait()
+    good = jnp.broadcast_to(flags_ref[...].astype(jnp.float32), (128, feeds)).T
+    good = jnp.concatenate([good] * (width // 128), 1)
+    copies[2].wait()
+    re = samples_ref[0].astype(jnp.float32) * good
+    left[:, :width] = re.astype(jnp.bfloat16)
+    copies[3].wait()
+    im = samples_ref[1].astype(jnp.float32) * good
+    left[:, width:] = im.astype(jnp.bfloat16)
+    right[:, :width] = (re - im).astype(jnp.bfloat16)
+    right[:, width:] = (re + im).astype(jnp.bfloat16)
+
+    def rows_of(step, _):
+        rows = pl.ds(pl.multiple_of(step * block, block), block)
+        nt = (((1,), (1,)), ((), ()))
+        both = lax.dot_general(left[rows, :], right[...], nt, preferred_element_type=jnp.float32)
+        out_ref[rows, :] = (both * scale).astype(jnp.bfloat16)
+        return 0
+
+    lax.fori_loop(0, 4, rows_of, 0)
 
 
 def gram(cal_channel, samples, flags, all_time):
     _, feeds, width = samples.shape
-    blocks = 4
     bf16 = jnp.bfloat16
-    anywhere = pl.BlockSpec(memory_space=pl.ANY)
+    outside = pl.BlockSpec(memory_space=pltpu.HBM)
     return pl.pallas_call(
         functools.partial(gram_kernel, 0.5 / all_time),
-        grid=(blocks,),
         out_shape=(jax.ShapeDtypeStruct((feeds, feeds), bf16), jax.ShapeDtypeStruct((1,), jnp.int32)),
-        in_specs=[anywhere] * 3,
-        out_specs=(
-            pl.BlockSpec((feeds // blocks, feeds), lambda i: (i, 0)),
-            pl.BlockSpec(memory_space=pltpu.SMEM),
-        ),
+        in_specs=[outside] * 3,
+        out_specs=(pl.BlockSpec(memory_space=pltpu.VMEM), pl.BlockSpec(memory_space=pltpu.SMEM)),
         scratch_shapes=[
             pltpu.SMEM(cal_channel.shape, jnp.int32),
             pltpu.VMEM(samples.shape, bf16),

time: 122 us -> 122 us (level)
  blocking collectives: 38.3 us -> 50 us
  waiting for transfers between devices: 26.4 us -> 20.6 us
  starting transfers between devices: 45 us -> 40.3 us
    all_to_all x2, blocking collectives: 38.3 us -> 50 us  [exchange(): return lax.all_to_all(value, 'tm', 0, 0, axis_index_groups=which)]
    all_to_all x1, waiting for transfers between devices: 23.3 us -> 17.5 us  [exchange(): return lax.all_to_all(value, 'tm', 0, 0, axis_index_groups=which)]
    ppermute x2, starting transfers between devices: 19.4 us -> 14.6 us  [swap_cores(): return lax.ppermute(value, 'chan', [(i, i ^ 1) for i in range(count)])]
where the time goes in v7:
time: 122 us
  blocking collectives  50 us (41%)
  starting transfers between devices  40.3 us (33%)
  waiting for transfers between devices  20.6 us (17%)
  Pallas kernels  6.25 us (5%)
  local copies, waits for them, and re-layouts  2.66 us (2%)
  between operations  1.31 us (1%)
    all_to_all x2, blocking collectives, exchange(): return lax.all_to_all(value, 'tm', 0, 0, axis_index_groups=which)  50 us
    all_to_all x1, waiting for transfers between devices, exchange(): return lax.all_to_all(value, 'tm', 0, 0, axis_index_groups=which)  17.5 us
    all_to_all x1, starting transfers between devices, exchange(): return lax.all_to_all(value, 'tm', 0, 0, axis_index_groups=which)  15.1 us
    ppermute x2, starting transfers between devices, swap_cores(): return lax.ppermute(value, 'chan', [(i, i ^ 1) for i in range(count)])  14.6 us
    ppermute x3, starting transfers between devices, around_x(): got.append(lax.ppermute(block, 'tm', pairs))  10.5 us
    pallas_call x1, Pallas kernels, gram(): pl.pallas_call(functools.partial(gram_kernel, 0.5 / all_time), out_shape=...  3.47 us
  transfers between devices with their start and end apart: 6, of which 3 were waited for; matrix products, arithmetic and copies ran while one was open for 0% of the time, Pallas kernels for 3%

profile of v7, /device:TPU:25, one launch (start us, length us, event | category | flops | bytes accessed | tf_op | source)
XLA Modules:
  0.0 121.8 jit_solution(7792945193223161339)
XLA Ops:
  0.6 2.6 %collective-permute-start.3 = (f32[4,64]{1,0:T(4,128)}, f32[4,64]{1,0:T(4,128)S(1)}, u32[]{:S(2)}, u32[]{:S(2)}) collective-permute-start(f32[4,64]{1,0:T(4,128)} %bitcast.44), channel_id=1, source_target_pairs={{0,16},{16,0},{32,48},{48,32},{64,80},{80,64},{96,112},{112,96},{1... | collective-permute-start | bytes 3080 | tf_op jit(solution)/shard_map/ppermute | solution.py:221
  3.2 3.5 %gram.1 = (bf16[1024,1024]{1,0:T(8,128)(2,1)S(1)}, s32[1]{0:T(128)}) custom-call(s32[16]{0:T(128)} %cal_hbm.1, bf16[2,1024,256]{2,1,0:T(8,128)(2,1)} %bitcast.40, s32[1,1024]{1,0:T(1,128)} %flags_hbm.1), custom_call_target="tpu_custom_call" | custom-call | tf_op jit(solution)/shard_map/gram/pallas_call | solution.py:56
  6.7 0.0 collective-permute-done.3
  7.4 99.9 %conditional.2 = (f32[64,1024]{1,0:T(8,128)S(1)}, f32[4,1024]{1,0:T(4,128)S(1)}, f32[4,1024]{1,0:T(4,128)S(1)}, f32[64,1024]{1,0:T(8,128)S(1)}) conditional(s32[]{:T(128)} %bitcast.20, (s32[]{:T(128)}, bf16[1024,1024]{1,0:T(8,128)(2,1)S(1)}, s32[]{:T(128)}, f32[4,64]{1,0:T(4,128)}, f32[4,64]{1,0:T(4,128)S(1)}) %tuple.57, ...), branch_computations={%region_0.4_spmd, %region_4.6_spmd} | conditional | flops 1147468 | bytes 17121400 | solution.py:274
  7.4 1.5 %slice.39 = bf16[4,240,1024]{2,1,0:T(8,128)(2,1)} slice(bf16[4,256,1024]{2,1,0:T(8,128)(2,1)S(1)} %bitcast.35), slice={[0:4], [16:256], [0:1024]} | slice | bytes 3932160 | tf_op jit(solution)/shard_map/cond/branch_0_fun/slice | solution.py:260
  8.9 12.9 %conditional = (bf16[4,16,1024]{2,1,0:T(8,128)(2,1)S(1)}) conditional(s32[]{:T(128)} %convert_element_type.32, bf16[4,16,1024]{2,1,0:T(8,128)(2,1)S(1)} %slice.38, (s32[]{:T(128)}, bf16[4,16,1024]{2,1,0:T(8,128)(2,1)S(1)}) %tuple.25), branch_computations={%region_1.1_spmd, %region_2.2_spmd} | conditional | flops 196671 | bytes 918297 | solution.py:259
  8.9 3.1 %collective-permute-start = (bf16[16,1024]{1,0:T(8,128)(2,1)S(1)}, bf16[16,1024]{1,0:T(8,128)(2,1)S(1)}, u32[]{:S(2)}, u32[]{:S(2)}) collective-permute-start(bf16[16,1024]{1,0:T(8,128)(2,1)S(1)} %get-tuple-element.114), channel_id=1, source_target_pairs={{0,4},{1,5},{2,6},{3,7},{4,8},{5,9},{6,10},{7,11},{8,12},{9,13},{1... | collective-permute-start | bytes 98312 | tf_op jit(solution)/shard_map/cond/branch_0_fun/cond/branch_1_fun/ppermute | solution.py:254
  12.0 4.4 %collective-permute-start.1 = (bf16[16,1024]{1,0:T(8,128)(2,1)S(1)}, bf16[16,1024]{1,0:T(8,128)(2,1)S(1)}, u32[]{:S(2)}, u32[]{:S(2)}) collective-permute-start(bf16[16,1024]{1,0:T(8,128)(2,1)S(1)} %get-tuple-element.113), channel_id=1, source_target_pairs={{0,8},{1,9},{2,10},{3,11},{4,12},{5,13},{6,14},{7,15},{8,0},{9,1},... | collective-permute-start | bytes 98312 | tf_op jit(solution)/shard_map/cond/branch_0_fun/cond/branch_1_fun/ppermute | solution.py:254
  16.4 3.1 %collective-permute-start.2 = (bf16[16,1024]{1,0:T(8,128)(2,1)S(1)}, bf16[16,1024]{1,0:T(8,128)(2,1)S(1)}, u32[]{:S(2)}, u32[]{:S(2)}) collective-permute-start(bf16[16,1024]{1,0:T(8,128)(2,1)S(1)} %get-tuple-element.112), channel_id=1, source_target_pairs={{0,12},{1,13},{2,14},{3,15},{4,0},{5,1},{6,2},{7,3},{8,4},{9,5},{1... | collective-permute-start | bytes 98312 | tf_op jit(solution)/shard_map/cond/branch_0_fun/cond/branch_1_fun/ppermute | solution.py:254
  19.4 0.0 collective-permute-done
  19.4 0.0 collective-permute-done.1
  19.5 2.3 %collective-permute-done.2 = bf16[16,1024]{1,0:T(8,128)(2,1)S(1)} collective-permute-done((bf16[16,1024]{1,0:T(8,128)(2,1)S(1)}, bf16[16,1024]{1,0:T(8,128)(2,1)S(1)}, u32[]{:S(2)}, u32[]{:S(2)}) %collective-permute-start.2) | collective-permute-done | bytes 32800 | tf_op jit(solution)/shard_map/cond/branch_0_fun/cond/branch_1_fun/ppermute | solution.py:254
  21.8 18.7 %all_to_all.33.refs_1_ = bf16[4,240,1024]{2,1,0:T(8,128)(2,1)S(1)} all-to-all(bf16[4,240,1024]{2,1,0:T(8,128)(2,1)} %slice.39), channel_id=1, replica_groups={{0,4,8,12},{1,5,9,13},{2,6,10,14},{3,7,11,15},{16,20,24,28},{17,21,25,2..., dimensions={0} | all-to-all | bytes 3932160 | tf_op jit(solution)/shard_map/cond/branch_0_fun/all_to_all | solution.py:216
  40.4 0.0 copy-start.3
  40.4 1.0 fold.2
  41.5 15.1 %all-to-all-start.6 = ((bf16[4,64,1024]{2,1,0:T(8,128)(2,1)}), bf16[4,64,1024]{2,1,0:T(8,128)(2,1)S(1)}, u32[]{:S(2)}, u32[]{:S(2)}) async-start(bf16[4,64,1024]{2,1,0:T(8,128)(2,1)} %bitcast.7), calls=%async_computation.6 | async-start | bytes 1048576 | tf_op jit(solution)/shard_map/cond/branch_0_fun/all_to_all | solution.py:216
  56.6 0.0 copy-done.3
  56.6 0.1 copy.25
  56.7 17.5 %all-to-all-done.6 = bf16[4,64,1024]{2,1,0:T(8,128)(2,1)S(1)} async-done(((bf16[4,64,1024]{2,1,0:T(8,128)(2,1)}), bf16[4,64,1024]{2,1,0:T(8,128)(2,1)S(1)}, u32[]{:S(2)}, u32[]{:S(2)}) %all-to-all-start.6) | async-done | bytes 524320 | tf_op jit(solution)/shard_map/cond/branch_0_fun/all_to_all | solution.py:216
  74.2 0.1 convert_reduce_fusion
  74.3 0.2 reshape.40
  74.5 0.1 pad_maximum_fusion.1
  74.7 0.1 copy.26
  74.7 31.3 %all_to_all.34 = bf16[16,80,64]{1,2,0:T(8,128)(2,1)S(1)} all-to-all(bf16[16,80,64]{1,2,0:T(8,128)(2,1)S(1)} %copy.26), channel_id=1, replica_groups=mesh['chan'=32,'tm'=16] {'tm'}, dimensions={0} | all-to-all | bytes 327680 | tf_op jit(solution)/shard_map/cond/branch_0_fun/all_to_all | solution.py:216
  106.1 0.3 slice_add_fusion
  106.4 0.2 fusion.1
  106.6 0.2 copy.33
  106.8 0.2 copy.35
  107.0 0.2 copy.37
  107.2 12.1 %collective-permute-start.4 = (f32[4,1024]{1,0:T(4,128)S(1)}, f32[4,1024]{1,0:T(4,128)S(1)}, u32[]{:S(2)}, u32[]{:S(2)}) collective-permute-start(f32[4,1024]{1,0:T(4,128)S(1)} %get-tuple-element.108.kept_ref), channel_id=1, source_target_pairs={{0,16},{16,0},{32,48},{48,32},{64,80},{80,64},{96,112},{112,96},{1... | collective-permute-start | bytes 49160 | tf_op jit(solution)/shard_map/ppermute | solution.py:221
  119.3 0.8 collective-permute-done.4.swapped_ref
  120.1 1.7 %rescale.1 = (f32[4,64]{1,0:T(4,128)}, bf16[64,2,1024]{2,1,0:T(2,128)(2,1)}) custom-call(s32[1]{0:T(128)} %bitcast.17.place_ref, s32[1]{0:T(128)} %get-tuple-element.79.cal_ref, f32[4,1024]{1,0:T(4,128)S(1)} %get-tuple-element.108.kept_ref, f32[4,1024]{1,0:T(4,128)S(1)} %collective-permute-done.4.swapped_ref, f32[4,1024]{1,0:T(4,128)S(1)} %get-tuple-element.109.state_ref, ...), custom_call_target="tpu_custom_call" | custom-call | tf_op jit(solution)/shard_map/rescale/pallas_call | solution.py:199
  (9 shorter events, 0.2 us)
Async XLA Ops:
  0.6 6.1 %collective-permute-start.3 = (f32[4,64]{1,0:T(4,128)}, f32[4,64]{1,0:T(4,128)S(1)}, u32[]{:S(2)}, u32[]{:S(2)}) collective-permute-start(f32[4,64]{1,0:T(4,128)} %bitcast.44), channel_id=1, source_target_pairs={{0,16},{16,0},{32,48},{48,32},{64,80},{80,64},{96,112},{112,96},{1... | collective-permute-start | bytes 3080 | tf_op jit(solution)/shard_map/ppermute | solution.py:221
  8.9 10.6 %collective-permute-start = (bf16[16,1024]{1,0:T(8,128)(2,1)S(1)}, bf16[16,1024]{1,0:T(8,128)(2,1)S(1)}, u32[]{:S(2)}, u32[]{:S(2)}) collective-permute-start(bf16[16,1024]{1,0:T(8,128)(2,1)S(1)} %get-tuple-element.114), channel_id=1, source_target_pairs={{0,4},{1,5},{2,6},{3,7},{4,8},{5,9},{6,10},{7,11},{8,12},{9,13},{1... | collective-permute-start | bytes 98312 | tf_op jit(solution)/shard_map/cond/branch_0_fun/cond/branch_1_fun/ppermute | solution.py:254
  12.0 7.5 %collective-permute-start.1 = (bf16[16,1024]{1,0:T(8,128)(2,1)S(1)}, bf16[16,1024]{1,0:T(8,128)(2,1)S(1)}, u32[]{:S(2)}, u32[]{:S(2)}) collective-permute-start(bf16[16,1024]{1,0:T(8,128)(2,1)S(1)} %get-tuple-element.113), channel_id=1, source_target_pairs={{0,8},{1,9},{2,10},{3,11},{4,12},{5,13},{6,14},{7,15},{8,0},{9,1},... | collective-permute-start | bytes 98312 | tf_op jit(solution)/shard_map/cond/branch_0_fun/cond/branch_1_fun/ppermute | solution.py:254
  16.4 5.4 %collective-permute-start.2 = (bf16[16,1024]{1,0:T(8,128)(2,1)S(1)}, bf16[16,1024]{1,0:T(8,128)(2,1)S(1)}, u32[]{:S(2)}, u32[]{:S(2)}) collective-permute-start(bf16[16,1024]{1,0:T(8,128)(2,1)S(1)} %get-tuple-element.112), channel_id=1, source_target_pairs={{0,12},{1,13},{2,14},{3,15},{4,0},{5,1},{6,2},{7,3},{8,4},{9,5},{1... | collective-permute-start | bytes 98312 | tf_op jit(solution)/shard_map/cond/branch_0_fun/cond/branch_1_fun/ppermute | solution.py:254
  40.4 16.1 %copy-start.3 = (f32[4,64]{1,0:T(4,128)S(1)}, f32[4,64]{1,0:T(4,128)}, u32[]{:S(2)}) copy-start(f32[4,64]{1,0:T(4,128)} %get-tuple-element.56) | copy-start | bytes 3076 | tf_op jit(solution)/shard_map/cond
  41.5 32.7 %all-to-all-start.6 = ((bf16[4,64,1024]{2,1,0:T(8,128)(2,1)}), bf16[4,64,1024]{2,1,0:T(8,128)(2,1)S(1)}, u32[]{:S(2)}, u32[]{:S(2)}) async-start(bf16[4,64,1024]{2,1,0:T(8,128)(2,1)} %bitcast.7), calls=%async_computation.6 | async-start | bytes 1048576 | tf_op jit(solution)/shard_map/cond/branch_0_fun/all_to_all | solution.py:216
  107.2 12.9 %collective-permute-start.4 = (f32[4,1024]{1,0:T(4,128)S(1)}, f32[4,1024]{1,0:T(4,128)S(1)}, u32[]{:S(2)}, u32[]{:S(2)}) collective-permute-start(f32[4,1024]{1,0:T(4,128)S(1)} %get-tuple-element.108.kept_ref), channel_id=1, source_target_pairs={{0,16},{16,0},{32,48},{48,32},{64,80},{80,64},{96,112},{112,96},{1... | collective-permute-start | bytes 49160 | tf_op jit(solution)/shard_map/ppermute | solution.py:221

commit v8 on v5

--- a/solution.py
+++ b/solution.py
@@ -8,7 +8,7 @@
 from jax.sharding import PartitionSpec as P
 
 ITERS = 8
-FIRST = 16
+FIRST = 32
 epsilon = 1e-06
 smoothing = 0.75
 

time: 122 us -> 124 us (1.016)
  blocking collectives: 38.3 us -> 50.4 us
  starting transfers between devices: 45 us -> 39.2 us
  waiting for transfers between devices: 26.4 us -> 21.3 us
    all_to_all x2, blocking collectives: 38.3 us -> 50.4 us  [exchange(): return lax.all_to_all(value, 'tm', 0, 0, axis_index_groups=which)]
    all_to_all x1, waiting for transfers between devices: 23.3 us -> 17.5 us  [exchange(): return lax.all_to_all(value, 'tm', 0, 0, axis_index_groups=which)]
    ppermute x2, starting transfers between devices: 19.4 us -> 13.5 us  [swap_cores(): return lax.ppermute(value, 'chan', [(i, i ^ 1) for i in range(count)])]
  transfers between devices with their start and end apart: 6 -> 6, of which waited for: 3 -> 4; matrix products, arithmetic and copies ran while one was open for 0% -> 0% of each run, Pallas kernels for 3% -> 3%
where the time goes in v8:
time: 124 us; the launch traced here: 122 us
  blocking collectives  50.4 us (41%)
  starting transfers between devices  39.2 us (32%)
  waiting for transfers between devices  21.3 us (17%)
  Pallas kernels  6.29 us (5%)
  local copies, waits for them, and re-layouts  2.63 us (2%)
  between operations  1.28 us (1%)
    all_to_all x2, blocking collectives, exchange(): return lax.all_to_all(value, 'tm', 0, 0, axis_index_groups=which)  50.4 us
    all_to_all x1, waiting for transfers between devices, exchange(): return lax.all_to_all(value, 'tm', 0, 0, axis_index_groups=which)  17.5 us
    all_to_all x1, starting transfers between devices, exchange(): return lax.all_to_all(value, 'tm', 0, 0, axis_index_groups=which)  15.1 us
    ppermute x2, starting transfers between devices, swap_cores(): return lax.ppermute(value, 'chan', [(i, i ^ 1) for i in range(count)])  13.5 us
    ppermute x3, starting transfers between devices, around_x(): got.append(lax.ppermute(block, 'tm', pairs))  10.5 us
    pallas_call x1, Pallas kernels, gram(): pl.pallas_call(functools.partial(gram_kernel, 0.5 / all_time), grid=(bloc...  3.55 us
    ppermute x3, waiting for transfers between devices, around_x(): got.append(lax.ppermute(block, 'tm', pairs))  2.99 us
  transfers between devices with their start and end apart: 6, of which 4 were waited for; matrix products, arithmetic and copies ran while one was open for 0% of the time, Pallas kernels for 3%

profile of v8, /device:TPU:25, one launch (start us, length us, event | category | flops | bytes accessed | tf_op | source)
XLA Modules:
  0.0 121.9 jit_solution(8968490402760625975)
XLA Ops:
  0.6 2.6 %collective-permute-start.3 = (f32[4,64]{1,0:T(4,128)}, f32[4,64]{1,0:T(4,128)S(1)}, u32[]{:S(2)}, u32[]{:S(2)}) collective-permute-start(f32[4,64]{1,0:T(4,128)} %bitcast.44), channel_id=1, source_target_pairs={{0,16},{16,0},{32,48},{48,32},{64,80},{80,64},{96,112},{112,96},{1... | collective-permute-start | bytes 3080 | tf_op jit(solution)/shard_map/ppermute | solution.py:226
  3.2 3.5 %gram.1 = (bf16[1024,1024]{1,0:T(8,128)(2,1)S(1)}, s32[1]{0:T(128)}) custom-call(s32[16]{0:T(128)} %cal_hbm.1, bf16[2,1024,256]{2,1,0:T(8,128)(2,1)} %bitcast.40, s32[1,1024]{1,0:T(1,128)} %flags_hbm.1), custom_call_target="tpu_custom_call" | custom-call | tf_op jit(solution)/shard_map/gram/pallas_call | solution.py:57
  6.8 0.0 collective-permute-done.3
  7.4 101.0 %conditional.2 = (f32[64,1024]{1,0:T(8,128)S(1)}, f32[4,1024]{1,0:T(4,128)S(1)}, f32[4,1024]{1,0:T(4,128)S(1)}, f32[64,1024]{1,0:T(8,128)S(1)}) conditional(s32[]{:T(128)} %bitcast.20, (s32[]{:T(128)}, bf16[1024,1024]{1,0:T(8,128)(2,1)S(1)}, s32[]{:T(128)}, f32[4,64]{1,0:T(4,128)}, f32[4,64]{1,0:T(4,128)S(1)}) %tuple.57, ...), branch_computations={%region_0.4_spmd, %region_4.6_spmd} | conditional | flops 1344076 | bytes 17121400 | solution.py:279
  7.4 1.4 %slice.39 = bf16[4,224,1024]{2,1,0:T(8,128)(2,1)} slice(bf16[4,256,1024]{2,1,0:T(8,128)(2,1)S(1)} %bitcast.34), slice={[0:4], [32:256], [0:1024]} | slice | bytes 3670016 | tf_op jit(solution)/shard_map/cond/branch_0_fun/slice | solution.py:265
  8.9 13.6 %conditional = (bf16[4,32,1024]{2,1,0:T(8,128)(2,1)S(1)}) conditional(s32[]{:T(128)} %convert_element_type.32, bf16[4,32,1024]{2,1,0:T(8,128)(2,1)S(1)} %slice.38, (s32[]{:T(128)}, bf16[4,32,1024]{2,1,0:T(8,128)(2,1)S(1)}) %tuple.25), branch_computations={%region_1.1_spmd, %region_2.2_spmd} | conditional | flops 393279 | bytes 1835801 | solution.py:264
  8.9 3.1 %collective-permute-start = (bf16[32,1024]{1,0:T(8,128)(2,1)S(1)}, bf16[32,1024]{1,0:T(8,128)(2,1)S(1)}, u32[]{:S(2)}, u32[]{:S(2)}) collective-permute-start(bf16[32,1024]{1,0:T(8,128)(2,1)S(1)} %get-tuple-element.114), channel_id=1, source_target_pairs={{0,4},{1,5},{2,6},{3,7},{4,8},{5,9},{6,10},{7,11},{8,12},{9,13},{1... | collective-permute-start | bytes 196616 | tf_op jit(solution)/shard_map/cond/branch_0_fun/cond/branch_1_fun/ppermute | solution.py:259
  12.0 4.4 %collective-permute-start.1 = (bf16[32,1024]{1,0:T(8,128)(2,1)S(1)}, bf16[32,1024]{1,0:T(8,128)(2,1)S(1)}, u32[]{:S(2)}, u32[]{:S(2)}) collective-permute-start(bf16[32,1024]{1,0:T(8,128)(2,1)S(1)} %get-tuple-element.113), channel_id=1, source_target_pairs={{0,8},{1,9},{2,10},{3,11},{4,12},{5,13},{6,14},{7,15},{8,0},{9,1},... | collective-permute-start | bytes 196616 | tf_op jit(solution)/shard_map/cond/branch_0_fun/cond/branch_1_fun/ppermute | solution.py:259
  16.4 3.1 %collective-permute-start.2 = (bf16[32,1024]{1,0:T(8,128)(2,1)S(1)}, bf16[32,1024]{1,0:T(8,128)(2,1)S(1)}, u32[]{:S(2)}, u32[]{:S(2)}) collective-permute-start(bf16[32,1024]{1,0:T(8,128)(2,1)S(1)} %get-tuple-element.112), channel_id=1, source_target_pairs={{0,12},{1,13},{2,14},{3,15},{4,0},{5,1},{6,2},{7,3},{8,4},{9,5},{1... | collective-permute-start | bytes 196616 | tf_op jit(solution)/shard_map/cond/branch_0_fun/cond/branch_1_fun/ppermute | solution.py:259
  19.4 0.0 collective-permute-done
  19.5 0.1 collective-permute-done.1
  19.6 2.9 %collective-permute-done.2 = bf16[32,1024]{1,0:T(8,128)(2,1)S(1)} collective-permute-done((bf16[32,1024]{1,0:T(8,128)(2,1)S(1)}, bf16[32,1024]{1,0:T(8,128)(2,1)S(1)}, u32[]{:S(2)}, u32[]{:S(2)}) %collective-permute-start.2) | collective-permute-done | bytes 65568 | tf_op jit(solution)/shard_map/cond/branch_0_fun/cond/branch_1_fun/ppermute | solution.py:259
  22.5 18.6 %all_to_all.33.refs_1_ = bf16[4,224,1024]{2,1,0:T(8,128)(2,1)S(1)} all-to-all(bf16[4,224,1024]{2,1,0:T(8,128)(2,1)} %slice.39), channel_id=1, replica_groups={{0,4,8,12},{1,5,9,13},{2,6,10,14},{3,7,11,15},{16,20,24,28},{17,21,25,2..., dimensions={0} | all-to-all | bytes 3670016 | tf_op jit(solution)/shard_map/cond/branch_0_fun/all_to_all | solution.py:221
  41.1 0.0 copy-start.3
  41.1 1.0 fold.2
  42.1 15.1 %all-to-all-start.6 = ((bf16[4,64,1024]{2,1,0:T(8,128)(2,1)}), bf16[4,64,1024]{2,1,0:T(8,128)(2,1)S(1)}, u32[]{:S(2)}, u32[]{:S(2)}) async-start(bf16[4,64,1024]{2,1,0:T(8,128)(2,1)} %bitcast.7), calls=%async_computation.6 | async-start | bytes 1048576 | tf_op jit(solution)/shard_map/cond/branch_0_fun/all_to_all | solution.py:221
  57.2 0.0 copy-done.3
  57.3 0.1 copy.25
  57.4 17.5 %all-to-all-done.6 = bf16[4,64,1024]{2,1,0:T(8,128)(2,1)S(1)} async-done(((bf16[4,64,1024]{2,1,0:T(8,128)(2,1)}), bf16[4,64,1024]{2,1,0:T(8,128)(2,1)S(1)}, u32[]{:S(2)}, u32[]{:S(2)}) %all-to-all-start.6) | async-done | bytes 524320 | tf_op jit(solution)/shard_map/cond/branch_0_fun/all_to_all | solution.py:221
  74.8 0.1 convert_reduce_fusion
  74.9 0.2 reshape.40
  75.2 0.1 pad_maximum_fusion.1
  75.3 0.1 copy.26
  75.4 31.8 %all_to_all.34 = bf16[16,80,64]{1,2,0:T(8,128)(2,1)S(1)} all-to-all(bf16[16,80,64]{1,2,0:T(8,128)(2,1)S(1)} %copy.26), channel_id=1, replica_groups=mesh['chan'=32,'tm'=16] {'tm'}, dimensions={0} | all-to-all | bytes 327680 | tf_op jit(solution)/shard_map/cond/branch_0_fun/all_to_all | solution.py:221
  107.3 0.3 slice_add_fusion
  107.6 0.2 fusion.1
  107.8 0.2 copy.33
  108.0 0.2 copy.35
  108.2 0.2 copy.37
  108.4 10.9 %collective-permute-start.4 = (f32[4,1024]{1,0:T(4,128)S(1)}, f32[4,1024]{1,0:T(4,128)S(1)}, u32[]{:S(2)}, u32[]{:S(2)}) collective-permute-start(f32[4,1024]{1,0:T(4,128)S(1)} %get-tuple-element.108.kept_ref), channel_id=1, source_target_pairs={{0,16},{16,0},{32,48},{48,32},{64,80},{80,64},{96,112},{112,96},{1... | collective-permute-start | bytes 49160 | tf_op jit(solution)/shard_map/ppermute | solution.py:226
  119.4 0.8 collective-permute-done.4.swapped_ref
  120.2 1.7 %rescale.1 = (f32[4,64]{1,0:T(4,128)}, bf16[64,2,1024]{2,1,0:T(2,128)(2,1)}) custom-call(s32[1]{0:T(128)} %bitcast.17.place_ref, s32[1]{0:T(128)} %get-tuple-element.79.cal_ref, f32[4,1024]{1,0:T(4,128)S(1)} %get-tuple-element.108.kept_ref, f32[4,1024]{1,0:T(4,128)S(1)} %collective-permute-done.4.swapped_ref, f32[4,1024]{1,0:T(4,128)S(1)} %get-tuple-element.109.state_ref, ...), custom_call_target="tpu_custom_call" | custom-call | tf_op jit(solution)/shard_map/rescale/pallas_call | solution.py:204
  (9 shorter events, 0.2 us)
Async XLA Ops:
  0.6 6.2 %collective-permute-start.3 = (f32[4,64]{1,0:T(4,128)}, f32[4,64]{1,0:T(4,128)S(1)}, u32[]{:S(2)}, u32[]{:S(2)}) collective-permute-start(f32[4,64]{1,0:T(4,128)} %bitcast.44), channel_id=1, source_target_pairs={{0,16},{16,0},{32,48},{48,32},{64,80},{80,64},{96,112},{112,96},{1... | collective-permute-start | bytes 3080 | tf_op jit(solution)/shard_map/ppermute | solution.py:226
  8.9 10.6 %collective-permute-start = (bf16[32,1024]{1,0:T(8,128)(2,1)S(1)}, bf16[32,1024]{1,0:T(8,128)(2,1)S(1)}, u32[]{:S(2)}, u32[]{:S(2)}) collective-permute-start(bf16[32,1024]{1,0:T(8,128)(2,1)S(1)} %get-tuple-element.114), channel_id=1, source_target_pairs={{0,4},{1,5},{2,6},{3,7},{4,8},{5,9},{6,10},{7,11},{8,12},{9,13},{1... | collective-permute-start | bytes 196616 | tf_op jit(solution)/shard_map/cond/branch_0_fun/cond/branch_1_fun/ppermute | solution.py:259
  12.0 7.6 %collective-permute-start.1 = (bf16[32,1024]{1,0:T(8,128)(2,1)S(1)}, bf16[32,1024]{1,0:T(8,128)(2,1)S(1)}, u32[]{:S(2)}, u32[]{:S(2)}) collective-permute-start(bf16[32,1024]{1,0:T(8,128)(2,1)S(1)} %get-tuple-element.113), channel_id=1, source_target_pairs={{0,8},{1,9},{2,10},{3,11},{4,12},{5,13},{6,14},{7,15},{8,0},{9,1},... | collective-permute-start | bytes 196616 | tf_op jit(solution)/shard_map/cond/branch_0_fun/cond/branch_1_fun/ppermute | solution.py:259
  16.4 6.1 %collective-permute-start.2 = (bf16[32,1024]{1,0:T(8,128)(2,1)S(1)}, bf16[32,1024]{1,0:T(8,128)(2,1)S(1)}, u32[]{:S(2)}, u32[]{:S(2)}) collective-permute-start(bf16[32,1024]{1,0:T(8,128)(2,1)S(1)} %get-tuple-element.112), channel_id=1, source_target_pairs={{0,12},{1,13},{2,14},{3,15},{4,0},{5,1},{6,2},{7,3},{8,4},{9,5},{1... | collective-permute-start | bytes 196616 | tf_op jit(solution)/shard_map/cond/branch_0_fun/cond/branch_1_fun/ppermute | solution.py:259
  41.1 16.1 %copy-start.3 = (f32[4,64]{1,0:T(4,128)S(1)}, f32[4,64]{1,0:T(4,128)}, u32[]{:S(2)}) copy-start(f32[4,64]{1,0:T(4,128)} %get-tuple-element.56) | copy-start | bytes 3076 | tf_op jit(solution)/shard_map/cond
  42.1 32.7 %all-to-all-start.6 = ((bf16[4,64,1024]{2,1,0:T(8,128)(2,1)}), bf16[4,64,1024]{2,1,0:T(8,128)(2,1)S(1)}, u32[]{:S(2)}, u32[]{:S(2)}) async-start(bf16[4,64,1024]{2,1,0:T(8,128)(2,1)} %bitcast.7), calls=%async_computation.6 | async-start | bytes 1048576 | tf_op jit(solution)/shard_map/cond/branch_0_fun/all_to_all | solution.py:221
  108.4 11.8 %collective-permute-start.4 = (f32[4,1024]{1,0:T(4,128)S(1)}, f32[4,1024]{1,0:T(4,128)S(1)}, u32[]{:S(2)}, u32[]{:S(2)}) collective-permute-start(f32[4,1024]{1,0:T(4,128)S(1)} %get-tuple-element.108.kept_ref), channel_id=1, source_target_pairs={{0,16},{16,0},{32,48},{48,32},{64,80},{80,64},{96,112},{112,96},{1... | collective-permute-start | bytes 49160 | tf_op jit(solution)/shard_map/ppermute | solution.py:226

commit v9 on v5

--- a/solution.py
+++ b/solution.py
@@ -122,7 +122,7 @@
     rows = mirror_ref.shape[0]
     for i in range(feeds // 256):
         mat_t[:, 256 * i:256 * (i + 1)] = own_ref[256 * i:256 * (i + 1), :].T
-    mirror_ref[...] = mat_t[pl.ds(pl.multiple_of(place_ref[0] * rows, rows), rows), :].astype(jnp.float32)
+    mirror_ref[...] = mat_t[pl.ds(pl.multiple_of(place_ref[0] * rows, rows), rows), :]
 
     def sweep(_, carry):
         qr, qi, _, _ = carry
@@ -165,7 +165,7 @@
     vm = pl.BlockSpec(memory_space=pltpu.VMEM)
     return pl.pallas_call(
         solve_kernel,
-        out_shape=(jax.ShapeDtypeStruct((4, feeds), jnp.float32), jax.ShapeDtypeStruct((rows, feeds), jnp.float32)),
+        out_shape=(jax.ShapeDtypeStruct((4, feeds), jnp.float32), jax.ShapeDtypeStruct((rows, feeds), jnp.bfloat16)),
         in_specs=[pl.BlockSpec(memory_space=pltpu.SMEM), vm, vm],
         out_specs=(vm, vm),
         scratch_shapes=[pltpu.VMEM((feeds, feeds), jnp.bfloat16)],
@@ -191,8 +191,8 @@
     down = jnp.broadcast_to(pltpu.roll(scale, shift, 1)[:, :128], (128, 128)).T[:rows]
     down = jnp.concatenate([down] * (feeds // 128), 1)
     factor = down * scale
-    mine = mine_ref[...]
-    mirror = mirror_ref[...]
+    mine = mine_ref[...].astype(jnp.float32)
+    mirror = mirror_ref[...].astype(jnp.float32)
     out_ref[:, 0, :] = ((mine + mirror) * factor).astype(jnp.bfloat16)
     out_ref[:, 1, :] = ((mine - mirror) * factor).astype(jnp.bfloat16)
 
@@ -244,8 +244,8 @@
 
     def with_cal():
         part = fold(exchange(packed.reshape(nx, nz * rows, feeds), along_x))
-        mine = jnp.sum(exchange(part.reshape(nz, rows, feeds), along_z).astype(f32), axis=0)
-        got = exchange(jnp.broadcast_to(mine.astype(bf16)[None], (nz, rows, feeds)), along_z)
+        mine = fold(exchange(part.reshape(nz, rows, feeds), along_z))
+        got = exchange(jnp.broadcast_to(mine[None], (nz, rows, feeds)), along_z)
         got = exchange(jnp.broadcast_to(got.reshape(1, nz * rows, feeds), (nx, nz * rows, feeds)), along_x)
         solved, mirror = solve(place, got.reshape(feeds, feeds), rows)
         return solved, jnp.zeros((4, feeds), f32), mine, mirror
@@ -264,15 +264,15 @@
         lead = lax.cond(odd, around_x, lambda value: exchange(value, along_x), blocks[:, :FIRST])
         lead, trail = lax.optimization_barrier((lead, blocks[:, FIRST:]))
         part = fold(lead, exchange(trail, along_x))
-        mine = jnp.sum(exchange(part.reshape(nz, rows, feeds), along_z).astype(f32), axis=0)
+        mine = fold(exchange(part.reshape(nz, rows, feeds), along_z))
         states = jnp.concatenate([own_state, other_state], 0)
         high = states.astype(bf16)
         low = (states - high.astype(f32)).astype(bf16)
         halves = jnp.broadcast_to(jnp.concatenate([high, low], 0)[None], (tm_count, 16, rows))
-        mirror = mine.astype(bf16).T.reshape(tm_count, rows, rows)
+        mirror = mine.T.reshape(tm_count, rows, rows)
         got = exchange(jnp.concatenate([mirror, halves], 1), None)
-        got = got.transpose(1, 0, 2).reshape(rows + 16, feeds).astype(f32)
-        mirror, halves = got[:rows], got[rows:]
+        got = got.transpose(1, 0, 2).reshape(rows + 16, feeds)
+        mirror, halves = got[:rows], got[rows:].astype(f32)
         states = halves[:8] + halves[8:]
         return states[4:], states[:4], mine, mirror
 

time: 122 us -> 122 us (level)
  the two profiles are of different devices: /device:TPU:25 before, /device:TPU:17 now
where the time goes in v9:
time: 122 us; the launch traced here: 123 us
  starting transfers between devices  50.7 us (42%)
  blocking collectives  38.8 us (32%)
  waiting for transfers between devices  22.1 us (18%)
  Pallas kernels  6.39 us (5%)
  local copies, waits for them, and re-layouts  2.6 us (2%)
  between operations  1.31 us (1%)
    all_to_all x2, blocking collectives, exchange(): return lax.all_to_all(value, 'tm', 0, 0, axis_index_groups=which)  38.8 us
    ppermute x2, starting transfers between devices, swap_cores(): return lax.ppermute(value, 'chan', [(i, i ^ 1) for i in range(count)])  25.1 us
    all_to_all x1, waiting for transfers between devices, exchange(): return lax.all_to_all(value, 'tm', 0, 0, axis_index_groups=which)  19 us
    all_to_all x1, starting transfers between devices, exchange(): return lax.all_to_all(value, 'tm', 0, 0, axis_index_groups=which)  15.1 us
    ppermute x3, starting transfers between devices, around_x(): got.append(lax.ppermute(block, 'tm', pairs))  10.5 us
    pallas_call x1, Pallas kernels, gram(): pl.pallas_call(functools.partial(gram_kernel, 0.5 / all_time), grid=(bloc...  3.55 us
  transfers between devices with their start and end apart: 6, of which 3 were waited for; matrix products, arithmetic and copies ran while one was open for 0% of the time, Pallas kernels for 3%

profile of v9, /device:TPU:17, one launch (start us, length us, event | category | flops | bytes accessed | tf_op | source)
XLA Modules:
  0.0 122.7 jit_solution(13926658462129119224)
XLA Ops:
  0.6 2.6 %collective-permute-start.3 = (f32[4,64]{1,0:T(4,128)}, f32[4,64]{1,0:T(4,128)S(1)}, u32[]{:S(2)}, u32[]{:S(2)}) collective-permute-start(f32[4,64]{1,0:T(4,128)} %bitcast.44), channel_id=1, source_target_pairs={{0,16},{16,0},{32,48},{48,32},{64,80},{80,64},{96,112},{112,96},{1... | collective-permute-start | bytes 3080 | tf_op jit(solution)/shard_map/ppermute | solution.py:226
  3.2 3.5 %gram.1 = (bf16[1024,1024]{1,0:T(8,128)(2,1)S(1)}, s32[1]{0:T(128)}) custom-call(s32[16]{0:T(128)} %cal_hbm.1, bf16[2,1024,256]{2,1,0:T(8,128)(2,1)} %bitcast.40, s32[1,1024]{1,0:T(1,128)} %flags_hbm.1), custom_call_target="tpu_custom_call" | custom-call | tf_op jit(solution)/shard_map/gram/pallas_call | solution.py:57
  6.8 0.0 collective-permute-done.3
  7.4 90.1 %conditional.2 = (bf16[64,1024]{1,0:T(8,128)(2,1)S(1)}, f32[4,1024]{1,0:T(4,128)S(1)}, f32[4,1024]{1,0:T(4,128)S(1)}, bf16[64,1024]{1,0:T(8,128)(2,1)S(1)}) conditional(s32[]{:T(128)} %bitcast.20, (s32[]{:T(128)}, bf16[1024,1024]{1,0:T(8,128)(2,1)S(1)}, s32[]{:T(128)}, f32[4,64]{1,0:T(4,128)}, f32[4,64]{1,0:T(4,128)S(1)}) %tuple.55, ...), branch_computations={%region_0.3_spmd, %region_3.4_spmd} | conditional | flops 557644 | bytes 14893176 | solution.py:279
  7.5 1.4 %slice.40 = bf16[4,240,1024]{2,1,0:T(8,128)(2,1)} slice(bf16[4,256,1024]{2,1,0:T(8,128)(2,1)S(1)} %bitcast.32), slice={[0:4], [16:256], [0:1024]} | slice | bytes 3932160 | tf_op jit(solution)/shard_map/cond/branch_0_fun/slice | solution.py:265
  8.9 12.9 %conditional = (bf16[4,16,1024]{2,1,0:T(8,128)(2,1)S(1)}) conditional(s32[]{:T(128)} %convert_element_type.15, bf16[4,16,1024]{2,1,0:T(8,128)(2,1)S(1)} %slice.39, (s32[]{:T(128)}, bf16[4,16,1024]{2,1,0:T(8,128)(2,1)S(1)}) %tuple.25), branch_computations={%region_1.1_spmd, %region_2.2_spmd} | conditional | flops 196671 | bytes 918297 | solution.py:264
  8.9 3.1 %collective-permute-start = (bf16[16,1024]{1,0:T(8,128)(2,1)S(1)}, bf16[16,1024]{1,0:T(8,128)(2,1)S(1)}, u32[]{:S(2)}, u32[]{:S(2)}) collective-permute-start(bf16[16,1024]{1,0:T(8,128)(2,1)S(1)} %get-tuple-element.106), channel_id=1, source_target_pairs={{0,4},{1,5},{2,6},{3,7},{4,8},{5,9},{6,10},{7,11},{8,12},{9,13},{1... | collective-permute-start | bytes 98312 | tf_op jit(solution)/shard_map/cond/branch_0_fun/cond/branch_1_fun/ppermute | solution.py:259
  12.1 4.4 %collective-permute-start.1 = (bf16[16,1024]{1,0:T(8,128)(2,1)S(1)}, bf16[16,1024]{1,0:T(8,128)(2,1)S(1)}, u32[]{:S(2)}, u32[]{:S(2)}) collective-permute-start(bf16[16,1024]{1,0:T(8,128)(2,1)S(1)} %get-tuple-element.105), channel_id=1, source_target_pairs={{0,8},{1,9},{2,10},{3,11},{4,12},{5,13},{6,14},{7,15},{8,0},{9,1},... | collective-permute-start | bytes 98312 | tf_op jit(solution)/shard_map/cond/branch_0_fun/cond/branch_1_fun/ppermute | solution.py:259
  16.4 3.1 %collective-permute-start.2 = (bf16[16,1024]{1,0:T(8,128)(2,1)S(1)}, bf16[16,1024]{1,0:T(8,128)(2,1)S(1)}, u32[]{:S(2)}, u32[]{:S(2)}) collective-permute-start(bf16[16,1024]{1,0:T(8,128)(2,1)S(1)} %get-tuple-element.104), channel_id=1, source_target_pairs={{0,12},{1,13},{2,14},{3,15},{4,0},{5,1},{6,2},{7,3},{8,4},{9,5},{1... | collective-permute-start | bytes 98312 | tf_op jit(solution)/shard_map/cond/branch_0_fun/cond/branch_1_fun/ppermute | solution.py:259
  19.5 0.0 collective-permute-done
  19.5 0.0 collective-permute-done.1
  19.5 2.3 %collective-permute-done.2 = bf16[16,1024]{1,0:T(8,128)(2,1)S(1)} collective-permute-done((bf16[16,1024]{1,0:T(8,128)(2,1)S(1)}, bf16[16,1024]{1,0:T(8,128)(2,1)S(1)}, u32[]{:S(2)}, u32[]{:S(2)}) %collective-permute-start.2) | collective-permute-done | bytes 32800 | tf_op jit(solution)/shard_map/cond/branch_0_fun/cond/branch_1_fun/ppermute | solution.py:259
  21.8 18.7 %all_to_all.33.refs_1_ = bf16[4,240,1024]{2,1,0:T(8,128)(2,1)S(1)} all-to-all(bf16[4,240,1024]{2,1,0:T(8,128)(2,1)} %slice.40), channel_id=1, replica_groups={{0,4,8,12},{1,5,9,13},{2,6,10,14},{3,7,11,15},{16,20,24,28},{17,21,25,2..., dimensions={0} | all-to-all | bytes 3932160 | tf_op jit(solution)/shard_map/cond/branch_0_fun/all_to_all | solution.py:221
  40.5 0.0 copy-start.3
  40.5 1.0 fold.4
  41.5 15.1 %all-to-all-start.6 = ((bf16[4,64,1024]{2,1,0:T(8,128)(2,1)}), bf16[4,64,1024]{2,1,0:T(8,128)(2,1)S(1)}, u32[]{:S(2)}, u32[]{:S(2)}) async-start(bf16[4,64,1024]{2,1,0:T(8,128)(2,1)} %bitcast.7), calls=%async_computation.6 | async-start | bytes 1048576 | tf_op jit(solution)/shard_map/cond/branch_0_fun/all_to_all | solution.py:221
  56.6 0.0 copy-done.3
  56.7 0.1 copy.17
  56.8 19.0 %all-to-all-done.6.refs_0_ = bf16[4,64,1024]{2,1,0:T(8,128)(2,1)S(1)} async-done(((bf16[4,64,1024]{2,1,0:T(8,128)(2,1)}), bf16[4,64,1024]{2,1,0:T(8,128)(2,1)S(1)}, u32[]{:S(2)}, u32[]{:S(2)}) %all-to-all-start.6) | async-done | bytes 524320 | tf_op jit(solution)/shard_map/cond/branch_0_fun/all_to_all | solution.py:221
  75.8 0.1 fold.5
  75.9 0.2 reshape.39
  76.0 0.1 copy.18
  76.2 0.2 pad_maximum_fusion.1
  76.3 20.2 %all_to_all.34 = bf16[16,80,64]{1,2,0:T(8,128)(2,1)S(1)} all-to-all(bf16[16,80,64]{1,2,0:T(8,128)(2,1)S(1)} %pad_maximum_fusion.1), channel_id=1, replica_groups=mesh['chan'=32,'tm'=16] {'tm'}, dimensions={0} | all-to-all | bytes 327680 | tf_op jit(solution)/shard_map/cond/branch_0_fun/all_to_all | solution.py:221
  96.5 0.1 slice_convert_fusion
  96.6 0.2 slice_add_fusion
  96.8 0.2 fusion.1
  97.0 0.2 copy.25
  97.2 0.2 copy.27
  97.4 0.1 copy.29
  97.6 22.5 %collective-permute-start.4 = (f32[4,1024]{1,0:T(4,128)S(1)}, f32[4,1024]{1,0:T(4,128)S(1)}, u32[]{:S(2)}, u32[]{:S(2)}) collective-permute-start(f32[4,1024]{1,0:T(4,128)S(1)} %get-tuple-element.100.kept_ref), channel_id=1, source_target_pairs={{0,16},{16,0},{32,48},{48,32},{64,80},{80,64},{96,112},{112,96},{1... | collective-permute-start | bytes 49160 | tf_op jit(solution)/shard_map/ppermute | solution.py:226
  120.1 0.8 collective-permute-done.4.swapped_ref
  120.9 1.7 %rescale.1 = (f32[4,64]{1,0:T(4,128)}, bf16[64,2,1024]{2,1,0:T(2,128)(2,1)}) custom-call(s32[1]{0:T(128)} %bitcast.17.place_ref, s32[1]{0:T(128)} %get-tuple-element.79.cal_ref, f32[4,1024]{1,0:T(4,128)S(1)} %get-tuple-element.100.kept_ref, f32[4,1024]{1,0:T(4,128)S(1)} %collective-permute-done.4.swapped_ref, f32[4,1024]{1,0:T(4,128)S(1)} %get-tuple-element.101.state_ref, ...), custom_call_target="tpu_custom_call" | custom-call | tf_op jit(solution)/shard_map/rescale/pallas_call | solution.py:204
  (7 shorter events, 0.1 us)
Async XLA Ops:
  0.6 6.2 %collective-permute-start.3 = (f32[4,64]{1,0:T(4,128)}, f32[4,64]{1,0:T(4,128)S(1)}, u32[]{:S(2)}, u32[]{:S(2)}) collective-permute-start(f32[4,64]{1,0:T(4,128)} %bitcast.44), channel_id=1, source_target_pairs={{0,16},{16,0},{32,48},{48,32},{64,80},{80,64},{96,112},{112,96},{1... | collective-permute-start | bytes 3080 | tf_op jit(solution)/shard_map/ppermute | solution.py:226
  8.9 10.6 %collective-permute-start = (bf16[16,1024]{1,0:T(8,128)(2,1)S(1)}, bf16[16,1024]{1,0:T(8,128)(2,1)S(1)}, u32[]{:S(2)}, u32[]{:S(2)}) collective-permute-start(bf16[16,1024]{1,0:T(8,128)(2,1)S(1)} %get-tuple-element.106), channel_id=1, source_target_pairs={{0,4},{1,5},{2,6},{3,7},{4,8},{5,9},{6,10},{7,11},{8,12},{9,13},{1... | collective-permute-start | bytes 98312 | tf_op jit(solution)/shard_map/cond/branch_0_fun/cond/branch_1_fun/ppermute | solution.py:259
  12.1 7.4 %collective-permute-start.1 = (bf16[16,1024]{1,0:T(8,128)(2,1)S(1)}, bf16[16,1024]{1,0:T(8,128)(2,1)S(1)}, u32[]{:S(2)}, u32[]{:S(2)}) collective-permute-start(bf16[16,1024]{1,0:T(8,128)(2,1)S(1)} %get-tuple-element.105), channel_id=1, source_target_pairs={{0,8},{1,9},{2,10},{3,11},{4,12},{5,13},{6,14},{7,15},{8,0},{9,1},... | collective-permute-start | bytes 98312 | tf_op jit(solution)/shard_map/cond/branch_0_fun/cond/branch_1_fun/ppermute | solution.py:259
  16.4 5.4 %collective-permute-start.2 = (bf16[16,1024]{1,0:T(8,128)(2,1)S(1)}, bf16[16,1024]{1,0:T(8,128)(2,1)S(1)}, u32[]{:S(2)}, u32[]{:S(2)}) collective-permute-start(bf16[16,1024]{1,0:T(8,128)(2,1)S(1)} %get-tuple-element.104), channel_id=1, source_target_pairs={{0,12},{1,13},{2,14},{3,15},{4,0},{5,1},{6,2},{7,3},{8,4},{9,5},{1... | collective-permute-start | bytes 98312 | tf_op jit(solution)/shard_map/cond/branch_0_fun/cond/branch_1_fun/ppermute | solution.py:259
  40.5 16.2 %copy-start.3 = (f32[4,64]{1,0:T(4,128)S(1)}, f32[4,64]{1,0:T(4,128)}, u32[]{:S(2)}) copy-start(f32[4,64]{1,0:T(4,128)} %get-tuple-element.56) | copy-start | bytes 3076 | tf_op jit(solution)/shard_map/cond
  41.5 34.3 %all-to-all-start.6 = ((bf16[4,64,1024]{2,1,0:T(8,128)(2,1)}), bf16[4,64,1024]{2,1,0:T(8,128)(2,1)S(1)}, u32[]{:S(2)}, u32[]{:S(2)}) async-start(bf16[4,64,1024]{2,1,0:T(8,128)(2,1)} %bitcast.7), calls=%async_computation.6 | async-start | bytes 1048576 | tf_op jit(solution)/shard_map/cond/branch_0_fun/all_to_all | solution.py:221
  97.6 23.3 %collective-permute-start.4 = (f32[4,1024]{1,0:T(4,128)S(1)}, f32[4,1024]{1,0:T(4,128)S(1)}, u32[]{:S(2)}, u32[]{:S(2)}) collective-permute-start(f32[4,1024]{1,0:T(4,128)S(1)} %get-tuple-element.100.kept_ref), channel_id=1, source_target_pairs={{0,16},{16,0},{32,48},{48,32},{64,80},{80,64},{96,112},{112,96},{1... | collective-permute-start | bytes 49160 | tf_op jit(solution)/shard_map/ppermute | solution.py:226
